TPU v7x, 32 devices: a whole 2x2x4 slice. The times are simulated.
32 devices in a mesh: grp: 4 (over y, x), tile: 8 (over z, core).
Axes of the slice: x: 2, y: 2, z: 4, core: 2. Of those that a mesh axis runs over, the one named last changes fastest.
Arguments:
- base_velocity: float32 [2, 256, 1024], P(None, 'grp', 'tile'), may hold values from -6 to 6
- viscosity: float32 [256, 1024], P('grp', 'tile'), may hold values from 0.5 to 2
- friction: float32 [256, 1024], P('grp', 'tile'), may hold values from 2 to 8
- friction_probe: float32 [256, 1024], P('grp', 'tile'), may hold values from -6 to 6
- pixel_los: float32 [4, 8, 2, 512], P('grp', 'tile'), may hold values from -6 to 6
- pixel_weight: float32 [4, 8, 1, 512], P('grp', 'tile'), may hold values from 2 to 20
- pixel_cell: int32 [4, 8, 1, 512], P('grp', 'tile'), may hold values from 0 to 8191
- pixel_count: int32 [4, 8, 1, 8], P('grp', 'tile'), may hold values from 8 to 64, as said below
- panels: bfloat16 [128, 256, 1024], P('grp', None, 'tile'), may hold values from -0.015625 to 0.015625
Outputs:
- increment: float32 [2, 256, 1024], P(None, 'grp', 'tile')
- hessian_probe: float32 [256, 1024], P('grp', 'tile')
- coefficients: float32 [128], replicated
Inputs may be any that keep to these rules, and one draw needn't show every extreme that they name: In group g, tile s uses the first pixel_count[g, s, 0, o] of its 64 slots toward owner tile o; in every group some owner receives 64 from every tile, and such owners are a few times busier than the mean. `pixel_cell`: cells are numbered row by row within the owner's block of 64 x 128 cells.
All inputs are finite; a program needn't handle non-finite values.
Results may differ from a plain program's by a relative error of at most 0.0036.
Values may be sent and summed in bfloat16 or wider, within the bound.
No kernel may reach another device: no remote copies, remote signals or barrier semaphores. Data moves between devices by JAX's collectives and lax.ppermute only.
A program may use at most 64 MiB of HBM per device.

v0:
```python
import jax
import jax.numpy as jnp
from jax import lax
from jax.sharding import PartitionSpec as P

SWEEPS = 8


relax_weight = 0.8


def with_halo(cells, sides, width):
    for axis, dim in sides:
        count = lax.axis_size(axis)
        ends = count - 1
        head = lax.slice_in_dim(cells, 0, width, axis=dim)
        tail = lax.slice_in_dim(cells, cells.shape[dim] - width, cells.shape[dim], axis=dim)
        cells = jnp.concatenate(
            [
                lax.ppermute(tail, axis, [(i, (i + 1) % count) for i in range(ends)]),
                cells,
                lax.ppermute(head, axis, [((i + 1) % count, i) for i in range(ends)]),
            ],
            axis=dim,
        )
    return cells


def face_terms(visc_ext, fric_inner):
    centre = visc_ext[1:-1, 1:-1]
    east = 0.5 * (centre + visc_ext[2:, 1:-1])
    west = 0.5 * (centre + visc_ext[:-2, 1:-1])
    north = 0.5 * (centre + visc_ext[1:-1, 2:])
    south = 0.5 * (centre + visc_ext[1:-1, :-2])
    node_pp = 0.25 * (centre + visc_ext[2:, 1:-1] + visc_ext[1:-1, 2:] + visc_ext[2:, 2:])
    node_mm = 0.25 * (centre + visc_ext[:-2, 1:-1] + visc_ext[1:-1, :-2] + visc_ext[:-2, :-2])
    node_pm = 0.25 * (centre + visc_ext[2:, 1:-1] + visc_ext[1:-1, :-2] + visc_ext[2:, :-2])
    node_mp = 0.25 * (centre + visc_ext[:-2, 1:-1] + visc_ext[1:-1, 2:] + visc_ext[:-2, 2:])
    diag_x = fric_inner + 2.0 * (east + west) + (north + south)
    diag_y = fric_inner + (east + west) + 2.0 * (north + south)
    return jnp.stack([east, west, north, south, node_pp, node_mm, node_pm, node_mp, diag_x, diag_y])


def operate(field_ext, terms):
    east, west, north, south = (terms[0], terms[1], terms[2], terms[3])
    node_pp, node_mm, node_pm, node_mp = (terms[4], terms[5], terms[6], terms[7])
    first = field_ext[0]
    second = field_ext[1]

    def axial(comp, along_one, along_two):
        return along_one * (east * comp[2:, 1:-1] + west * comp[:-2, 1:-1]) + along_two * (
            north * comp[1:-1, 2:] + south * comp[1:-1, :-2]
        )

    def cross(comp):
        return (
            node_pp * comp[2:, 2:]
            + node_mm * comp[:-2, :-2]
            - node_pm * comp[2:, :-2]
            - node_mp * comp[:-2, 2:]
        )

    out_first = terms[8] * first[1:-1, 1:-1] - axial(first, 2.0, 1.0) - 0.25 * cross(second)
    out_second = terms[9] * second[1:-1, 1:-1] - axial(second, 1.0, 2.0) - 0.25 * cross(first)
    return jnp.stack([out_first, out_second])


def on_device(
    base_velocity,
    viscosity,
    friction,
    friction_probe,
    pixel_los,
    pixel_weight,
    pixel_cell,
    pixel_count,
    panels,
):
    rows, columns = viscosity.shape
    stacked = jnp.stack([viscosity, friction])
    coarse_ext = with_halo(stacked, (("grp", 1), ("tile", 2)), 2)
    terms = face_terms(coarse_ext[0], coarse_ext[1][1:-1, 1:-1])
    row_ids = lax.axis_index("grp") * rows + jnp.arange(-1, rows + 1, dtype=jnp.int32)
    col_ids = lax.axis_index("tile") * columns + jnp.arange(-1, columns + 1, dtype=jnp.int32)
    row_inside = (row_ids >= 0) & (row_ids < rows * lax.axis_size("grp"))
    col_inside = (col_ids >= 0) & (col_ids < columns * lax.axis_size("tile"))
    inside = row_inside[:, None] & col_inside[None, :]
    diagonal = jnp.where(inside[None], terms[8:10], 1.0)

    def relax(source):
        depth = 1
        source_ext = jnp.pad(source, ((0, 0), (1, 1), (1, 1)))
        field = source
        finished = 0
        for block in range(-(-SWEEPS // depth)):
            width = min(depth, SWEEPS - finished)
            if finished == 0:
                field_ext = jnp.zeros((2, rows + 2 * width, columns + 2 * width), jnp.float32)
            else:
                field_ext = with_halo(field, (("grp", 1), ("tile", 2)), width)
            margin = width - 1
            offset = 1 - margin
            span_rows = rows + 2 * margin
            span_cols = columns + 2 * margin
            terms_sub = terms[:, offset : offset + span_rows, offset : offset + span_cols]
            diag_sub = diagonal[:, offset : offset + span_rows, offset : offset + span_cols]
            inside_sub = inside[offset : offset + span_rows, offset : offset + span_cols]
            source_sub = source_ext[:, offset : offset + span_rows, offset : offset + span_cols]
            centre = field_ext[:, 1:-1, 1:-1]
            updated = (
                centre + relax_weight * (source_sub - operate(field_ext, terms_sub)) / diag_sub
            )
            field_ext = jnp.where(inside_sub[None], updated, 0.0)
            field = field_ext
            finished = finished + width
        return field

    source = -(friction_probe[None] * base_velocity)
    increment = relax(source)
    los_got, weight_got = (
        lax.all_to_all(pixel_los, "tile", split_axis=3, concat_axis=1, tiled=True),
        lax.all_to_all(pixel_weight, "tile", split_axis=3, concat_axis=1, tiled=True),
    )
    cell_got, count_got = (
        lax.all_to_all(pixel_cell, "tile", split_axis=3, concat_axis=1, tiled=True),
        lax.all_to_all(pixel_count, "tile", split_axis=3, concat_axis=1, tiled=True),
    )
    slot_cap = cell_got.shape[3]
    live = jnp.arange(slot_cap, dtype=jnp.int32)[None, None, None, :] < count_got
    spot = cell_got.reshape(-1)
    los_x = los_got[:, :, 0].reshape(-1)
    los_y = los_got[:, :, 1].reshape(-1)
    flat = increment.reshape(2, -1)
    predicted = los_x * flat[0][spot] + los_y * flat[1][spot]
    amount = jnp.where(live.reshape(-1), weight_got.reshape(-1) * predicted, 0.0)
    adjoint_source = (
        jnp.zeros((2, rows * columns), jnp.float32)
        .at[:, spot]
        .add(jnp.stack([amount * los_x, amount * los_y]))
        .reshape(2, rows, columns)
    )
    multiplier = relax(adjoint_source)
    hessian_probe = -(base_velocity[0] * multiplier[0] + base_velocity[1] * multiplier[1])
    probe_low = hessian_probe.astype(jnp.bfloat16)
    panel_count = panels.shape[0]
    partial_sum = jnp.dot(
        panels.reshape(panel_count, -1),
        lax.all_gather(probe_low, "grp", axis=0, tiled=True).reshape(-1),
        preferred_element_type=jnp.float32,
    )
    summed = lax.psum(partial_sum, "tile")
    coefficients = lax.all_gather(summed, "grp", axis=0, tiled=True)
    return (increment, hessian_probe, coefficients)


def solution(mesh):
    in_specs = (
        P(None, "grp", "tile"),
        P("grp", "tile"),
        P("grp", "tile"),
        P("grp", "tile"),
        P("grp", "tile", None, None),
        P("grp", "tile", None, None),
        P("grp", "tile", None, None),
        P("grp", "tile", None, None),
        P("grp", None, "tile"),
    )
    out_specs = (P(None, "grp", "tile"), P("grp", "tile"), P())
    return jax.shard_map(
        on_device, mesh=mesh, in_specs=in_specs, out_specs=out_specs, check_vma=False
    )
```

profile of v0, /device:TPU:0, one launch (start us, length us, event | category | flops | bytes accessed | tf_op | source)
XLA Modules:
  0.0 345.5 jit_solution(12829618137836094301)
XLA Ops:
  1.5 4.8 %collective-permute-start = (f32[2,2,128]{2,1,0:T(2,128)S(1)}, f32[2,2,128]{2,1,0:T(2,128)S(1)}, u32[]{:S(2)}, u32[]{:S(2)}) collective-permute-start(f32[2,2,128]{2,1,0:T(2,128)S(1)} %get-tuple-element.119), channel_id=1, source_target_pairs={{0,8},{8,16},{16,24},{1,9},{9,17},{17,25},{2,10},{10,18},{18,26},{... | collective-permute-start | bytes 6152 | tf_op jit(solution)/shard_map/ppermute | solution.py:20
  7.7 4.1 %collective-permute-done.1 = f32[2,2,128]{2,1,0:T(2,128)S(1)} collective-permute-done((f32[2,2,128]{2,1,0:T(2,128)S(1)}, f32[2,2,128]{2,1,0:T(2,128)S(1)}, u32[]{:S(2)}, u32[]{:S(2)}) %collective-permute-start.1) | collective-permute-done | bytes 2080 | tf_op jit(solution)/shard_map/ppermute | solution.py:22
  15.5 3.5 %collective-permute-done.3 = f32[2,68,2]{2,1,0:T(8,128)S(1)} collective-permute-done((f32[2,68,2]{2,1,0:T(8,128)S(1)}, f32[2,68,2]{2,1,0:T(8,128)S(1)}, u32[]{:S(2)}, u32[]{:S(2)}) %collective-permute-start.3) | collective-permute-done | bytes 1120 | tf_op jit(solution)/shard_map/ppermute | solution.py:22
  21.5 4.3 %collective-permute-start.4 = (f32[2,1,128]{2,1,0:T(1,128)S(1)}, f32[2,1,128]{2,1,0:T(1,128)S(1)}, u32[]{:S(2)}, u32[]{:S(2)}) collective-permute-start(f32[2,1,128]{2,1,0:T(1,128)S(1)} %get-tuple-element.117), channel_id=1, source_target_pairs={{0,8},{8,16},{16,24},{1,9},{9,17},{17,25},{2,10},{10,18},{18,26},{... | collective-permute-start | bytes 3080 | tf_op jit(solution)/shard_map/ppermute | solution.py:20
  27.1 4.2 %collective-permute-done.5 = f32[2,1,128]{2,1,0:T(1,128)S(1)} collective-permute-done((f32[2,1,128]{2,1,0:T(1,128)S(1)}, f32[2,1,128]{2,1,0:T(1,128)S(1)}, u32[]{:S(2)}, u32[]{:S(2)}) %collective-permute-start.5) | collective-permute-done | bytes 1056 | tf_op jit(solution)/shard_map/ppermute | solution.py:22
  31.3 3.5 %collective-permute-start.6 = (f32[2,66,1]{2,1,0:T(8,128)S(1)}, f32[2,66,1]{2,1,0:T(8,128)S(1)}, u32[]{:S(2)}, u32[]{:S(2)}) collective-permute-start(f32[2,66,1]{2,1,0:T(8,128)S(1)} %get-tuple-element.79), channel_id=1, source_target_pairs={{0,1},{1,2},{2,3},{3,4},{4,5},{5,6},{6,7},{8,9},{9,10},{10,11},{11... | collective-permute-start | bytes 1592 | tf_op jit(solution)/shard_map/ppermute | solution.py:20
  36.1 2.7 collective-permute-done.7
  39.5 3.4 collective-permute-start.8
  44.2 4.2 %collective-permute-done.9 = f32[2,1,128]{2,1,0:T(1,128)S(1)} collective-permute-done((f32[2,1,128]{2,1,0:T(1,128)S(1)}, f32[2,1,128]{2,1,0:T(1,128)S(1)}, u32[]{:S(2)}, u32[]{:S(2)}) %collective-permute-start.9) | collective-permute-done | bytes 1056 | tf_op jit(solution)/shard_map/ppermute | solution.py:22
  48.5 3.5 %collective-permute-start.10 = (f32[2,66,1]{2,1,0:T(8,128)S(1)}, f32[2,66,1]{2,1,0:T(8,128)S(1)}, u32[]{:S(2)}, u32[]{:S(2)}) collective-permute-start(f32[2,66,1]{2,1,0:T(8,128)S(1)} %get-tuple-element.77), channel_id=1, source_target_pairs={{0,1},{1,2},{2,3},{3,4},{4,5},{5,6},{6,7},{8,9},{9,10},{10,11},{11... | collective-permute-start | bytes 1592 | tf_op jit(solution)/shard_map/ppermute | solution.py:20
  53.3 2.7 collective-permute-done.11
  56.6 2.8 collective-permute-start.12
  60.8 4.2 %collective-permute-done.13 = f32[2,1,128]{2,1,0:T(1,128)S(1)} collective-permute-done((f32[2,1,128]{2,1,0:T(1,128)S(1)}, f32[2,1,128]{2,1,0:T(1,128)S(1)}, u32[]{:S(2)}, u32[]{:S(2)}) %collective-permute-start.13) | collective-permute-done | bytes 1056 | tf_op jit(solution)/shard_map/ppermute | solution.py:22
  65.0 3.5 %collective-permute-start.14 = (f32[2,66,1]{2,1,0:T(8,128)S(1)}, f32[2,66,1]{2,1,0:T(8,128)S(1)}, u32[]{:S(2)}, u32[]{:S(2)}) collective-permute-start(f32[2,66,1]{2,1,0:T(8,128)S(1)} %get-tuple-element.75), channel_id=1, source_target_pairs={{0,1},{1,2},{2,3},{3,4},{4,5},{5,6},{6,7},{8,9},{9,10},{10,11},{11... | collective-permute-start | bytes 1592 | tf_op jit(solution)/shard_map/ppermute | solution.py:20
  69.8 2.7 collective-permute-done.15
  73.2 2.8 collective-permute-start.16
  77.4 4.2 %collective-permute-done.17 = f32[2,1,128]{2,1,0:T(1,128)S(1)} collective-permute-done((f32[2,1,128]{2,1,0:T(1,128)S(1)}, f32[2,1,128]{2,1,0:T(1,128)S(1)}, u32[]{:S(2)}, u32[]{:S(2)}) %collective-permute-start.17) | collective-permute-done | bytes 1056 | tf_op jit(solution)/shard_map/ppermute | solution.py:22
  81.6 3.5 %collective-permute-start.18 = (f32[2,66,1]{2,1,0:T(8,128)S(1)}, f32[2,66,1]{2,1,0:T(8,128)S(1)}, u32[]{:S(2)}, u32[]{:S(2)}) collective-permute-start(f32[2,66,1]{2,1,0:T(8,128)S(1)} %get-tuple-element.73), channel_id=1, source_target_pairs={{0,1},{1,2},{2,3},{3,4},{4,5},{5,6},{6,7},{8,9},{9,10},{10,11},{11... | collective-permute-start | bytes 1592 | tf_op jit(solution)/shard_map/ppermute | solution.py:20
  86.4 2.7 collective-permute-done.19
  89.8 2.8 collective-permute-start.20
  93.9 4.2 %collective-permute-done.21 = f32[2,1,128]{2,1,0:T(1,128)S(1)} collective-permute-done((f32[2,1,128]{2,1,0:T(1,128)S(1)}, f32[2,1,128]{2,1,0:T(1,128)S(1)}, u32[]{:S(2)}, u32[]{:S(2)}) %collective-permute-start.21) | collective-permute-done | bytes 1056 | tf_op jit(solution)/shard_map/ppermute | solution.py:22
  98.8 3.5 %collective-permute-start.22 = (f32[2,66,1]{2,1,0:T(8,128)}, f32[2,66,1]{2,1,0:T(8,128)S(1)}, u32[]{:S(2)}, u32[]{:S(2)}) collective-permute-start(f32[2,66,1]{2,1,0:T(8,128)} %get-tuple-element.71), channel_id=1, source_target_pairs={{0,1},{1,2},{2,3},{3,4},{4,5},{5,6},{6,7},{8,9},{9,10},{10,11},{11... | collective-permute-start | bytes 1592 | tf_op jit(solution)/shard_map/ppermute | solution.py:20
  104.3 6.9 %all-to-all-start.1 = ((s32[1,1,1,8]{2,1,0,3:T(1,128)}), s32[1,1,1,8]{2,1,0,3:T(1,128)S(1)}, u32[]{:S(2)}, u32[]{:S(2)}) async-start(s32[1,1,1,8]{2,1,0,3:T(1,128)} %copy.44), calls=%async_computation.1 | async-start | bytes 8192 | tf_op jit(solution)/shard_map/all_to_all | solution.py:126
  112.7 4.0 %all-to-all-done.1 = s32[1,1,1,8]{2,1,0,3:T(1,128)S(1)} async-done(((s32[1,1,1,8]{2,1,0,3:T(1,128)}), s32[1,1,1,8]{2,1,0,3:T(1,128)S(1)}, u32[]{:S(2)}, u32[]{:S(2)}) %all-to-all-start.1) | async-done | bytes 64 | tf_op jit(solution)/shard_map/all_to_all | solution.py:126
  116.7 4.0 %all-to-all-start = ((s32[1,1,1,512]{2,1,0,3:T(1,128)}), s32[1,1,1,512]{2,1,0,3:T(1,128)}, u32[]{:S(2)}, u32[]{:S(2)}) async-start(s32[1,1,1,512]{2,1,0,3:T(1,128)} %copy.43), calls=%async_computation | async-start | bytes 524288 | tf_op jit(solution)/shard_map/all_to_all | solution.py:125
  120.7 2.8 collective-permute-start.24
  130.7 5.0 %all-to-all-start.2 = ((f32[1,1,1,512]{2,1,0,3:T(1,128)}), f32[1,1,1,512]{2,1,0,3:T(1,128)S(1)}, u32[]{:S(2)}, u32[]{:S(2)}) async-start(f32[1,1,1,512]{2,1,0,3:T(1,128)} %copy.45), calls=%async_computation.2 | async-start | bytes 524288 | tf_op jit(solution)/shard_map/all_to_all | solution.py:122
  135.7 10.1 %reduce = s32[512]{0:T(512)S(1)} reduce(s32[1,1,1,512]{2,1,0,3:T(1,128)} %all-to-all-done, s32[]{:T(128)} %constant.18.clone.1), dimensions={0,1,2}, to_apply=%all_to_all.14.reduce_sub_computation | reduce | bytes 4100 | tf_op jit(solution)/shard_map/all_to_all | solution.py:125
  149.6 3.0 collective-permute-done.27
  153.2 4.5 %collective-permute-start.28 = (f32[2,1,128]{2,1,0:T(1,128)S(1)}, f32[2,1,128]{2,1,0:T(1,128)S(1)}, u32[]{:S(2)}, u32[]{:S(2)}) collective-permute-start(f32[2,1,128]{2,1,0:T(1,128)S(1)} %get-tuple-element.105), channel_id=1, source_target_pairs={{0,8},{8,16},{16,24},{1,9},{9,17},{17,25},{2,10},{10,18},{18,26},{... | collective-permute-start | bytes 3080 | tf_op jit(solution)/shard_map/ppermute | solution.py:20
  159.1 6.0 %all-to-all-start.3 = ((f32[8,1,128]{2,1,0:T(1,128)}), f32[8,1,128]{2,1,0:T(1,128)S(1)}, u32[]{:S(2)}, u32[]{:S(2)}) async-start(f32[8,1,128]{2,1,0:T(1,128)} %reshape.279), calls=%async_computation.3 | async-start | bytes 8192 | tf_op jit(solution)/shard_map/all_to_all | solution.py:121
  166.1 4.4 %all-to-all-done.3 = f32[8,1,128]{2,1,0:T(1,128)S(1)} async-done(((f32[8,1,128]{2,1,0:T(1,128)}), f32[8,1,128]{2,1,0:T(1,128)S(1)}, u32[]{:S(2)}, u32[]{:S(2)}) %all-to-all-start.3) | async-done | bytes 4128 | tf_op jit(solution)/shard_map/all_to_all | solution.py:121
  178.4 3.1 gather_fusion
  181.6 3.1 gather_fusion.1
  184.9 4.5 %scatter_custom_fusion = f32[2,8192]{0,1:T(8,128)} fusion(s32[512]{0:T(512)S(1)} %bitcast.453, f32[512,2]{1,0:T(8,128)S(1)} %copy.48, f32[]{:T(128)} %constant.4.clone.1), kind=kCustom, calls=%fused_computation.5 | custom fusion | flops 1024 | bytes 65540 | tf_op jit(solution)/shard_map/scatter-add | solution.py:139
  189.4 2.8 copy.49
  192.3 4.5 %collective-permute-start.32 = (f32[2,1,128]{2,1,0:T(1,128)S(1)}, f32[2,1,128]{2,1,0:T(1,128)S(1)}, u32[]{:S(2)}, u32[]{:S(2)}) collective-permute-start(f32[2,1,128]{2,1,0:T(1,128)S(1)} %get-tuple-element.101), channel_id=1, source_target_pairs={{0,8},{8,16},{16,24},{1,9},{9,17},{17,25},{2,10},{10,18},{18,26},{... | collective-permute-start | bytes 3080 | tf_op jit(solution)/shard_map/ppermute | solution.py:20
  198.1 4.2 %collective-permute-done.33 = f32[2,1,128]{2,1,0:T(1,128)S(1)} collective-permute-done((f32[2,1,128]{2,1,0:T(1,128)S(1)}, f32[2,1,128]{2,1,0:T(1,128)S(1)}, u32[]{:S(2)}, u32[]{:S(2)}) %collective-permute-start.33) | collective-permute-done | bytes 1056 | tf_op jit(solution)/shard_map/ppermute | solution.py:22
  202.3 3.6 %collective-permute-start.34 = (f32[2,66,1]{2,1,0:T(8,128)S(1)}, f32[2,66,1]{2,1,0:T(8,128)S(1)}, u32[]{:S(2)}, u32[]{:S(2)}) collective-permute-start(f32[2,66,1]{2,1,0:T(8,128)S(1)} %get-tuple-element.65), channel_id=1, source_target_pairs={{0,1},{1,2},{2,3},{3,4},{4,5},{5,6},{6,7},{8,9},{9,10},{10,11},{11... | collective-permute-start | bytes 1592 | tf_op jit(solution)/shard_map/ppermute | solution.py:20
  210.5 4.6 %collective-permute-start.36 = (f32[2,1,128]{2,1,0:T(1,128)S(1)}, f32[2,1,128]{2,1,0:T(1,128)S(1)}, u32[]{:S(2)}, u32[]{:S(2)}) collective-permute-start(f32[2,1,128]{2,1,0:T(1,128)S(1)} %get-tuple-element.99), channel_id=1, source_target_pairs={{0,8},{8,16},{16,24},{1,9},{9,17},{17,25},{2,10},{10,18},{18,26},{... | collective-permute-start | bytes 3080 | tf_op jit(solution)/shard_map/ppermute | solution.py:20
  216.4 4.2 %collective-permute-done.37 = f32[2,1,128]{2,1,0:T(1,128)S(1)} collective-permute-done((f32[2,1,128]{2,1,0:T(1,128)S(1)}, f32[2,1,128]{2,1,0:T(1,128)S(1)}, u32[]{:S(2)}, u32[]{:S(2)}) %collective-permute-start.37) | collective-permute-done | bytes 1056 | tf_op jit(solution)/shard_map/ppermute | solution.py:22
  220.7 3.5 %collective-permute-start.38 = (f32[2,66,1]{2,1,0:T(8,128)S(1)}, f32[2,66,1]{2,1,0:T(8,128)S(1)}, u32[]{:S(2)}, u32[]{:S(2)}) collective-permute-start(f32[2,66,1]{2,1,0:T(8,128)S(1)} %get-tuple-element.63), channel_id=1, source_target_pairs={{0,1},{1,2},{2,3},{3,4},{4,5},{5,6},{6,7},{8,9},{9,10},{10,11},{11... | collective-permute-start | bytes 1592 | tf_op jit(solution)/shard_map/ppermute | solution.py:20
  225.5 2.7 collective-permute-done.39
  228.8 2.8 collective-permute-start.40
  233.0 4.2 %collective-permute-done.41 = f32[2,1,128]{2,1,0:T(1,128)S(1)} collective-permute-done((f32[2,1,128]{2,1,0:T(1,128)S(1)}, f32[2,1,128]{2,1,0:T(1,128)S(1)}, u32[]{:S(2)}, u32[]{:S(2)}) %collective-permute-start.41) | collective-permute-done | bytes 1056 | tf_op jit(solution)/shard_map/ppermute | solution.py:22
  237.2 3.5 %collective-permute-start.42 = (f32[2,66,1]{2,1,0:T(8,128)S(1)}, f32[2,66,1]{2,1,0:T(8,128)S(1)}, u32[]{:S(2)}, u32[]{:S(2)}) collective-permute-start(f32[2,66,1]{2,1,0:T(8,128)S(1)} %get-tuple-element.61), channel_id=1, source_target_pairs={{0,1},{1,2},{2,3},{3,4},{4,5},{5,6},{6,7},{8,9},{9,10},{10,11},{11... | collective-permute-start | bytes 1592 | tf_op jit(solution)/shard_map/ppermute | solution.py:20
  242.0 2.7 collective-permute-done.43
  245.4 2.8 collective-permute-start.44
  249.5 4.2 %collective-permute-done.45 = f32[2,1,128]{2,1,0:T(1,128)S(1)} collective-permute-done((f32[2,1,128]{2,1,0:T(1,128)S(1)}, f32[2,1,128]{2,1,0:T(1,128)S(1)}, u32[]{:S(2)}, u32[]{:S(2)}) %collective-permute-start.45) | collective-permute-done | bytes 1056 | tf_op jit(solution)/shard_map/ppermute | solution.py:22
  253.8 3.5 %collective-permute-start.46 = (f32[2,66,1]{2,1,0:T(8,128)S(1)}, f32[2,66,1]{2,1,0:T(8,128)S(1)}, u32[]{:S(2)}, u32[]{:S(2)}) collective-permute-start(f32[2,66,1]{2,1,0:T(8,128)S(1)} %get-tuple-element.59), channel_id=1, source_target_pairs={{0,1},{1,2},{2,3},{3,4},{4,5},{5,6},{6,7},{8,9},{9,10},{10,11},{11... | collective-permute-start | bytes 1592 | tf_op jit(solution)/shard_map/ppermute | solution.py:20
  258.6 2.7 collective-permute-done.47
  262.0 2.8 collective-permute-start.48
  266.1 4.2 %collective-permute-done.49 = f32[2,1,128]{2,1,0:T(1,128)S(1)} collective-permute-done((f32[2,1,128]{2,1,0:T(1,128)S(1)}, f32[2,1,128]{2,1,0:T(1,128)S(1)}, u32[]{:S(2)}, u32[]{:S(2)}) %collective-permute-start.49) | collective-permute-done | bytes 1056 | tf_op jit(solution)/shard_map/ppermute | solution.py:22
  270.4 3.5 %collective-permute-start.50 = (f32[2,66,1]{2,1,0:T(8,128)S(1)}, f32[2,66,1]{2,1,0:T(8,128)S(1)}, u32[]{:S(2)}, u32[]{:S(2)}) collective-permute-start(f32[2,66,1]{2,1,0:T(8,128)S(1)} %get-tuple-element.57), channel_id=1, source_target_pairs={{0,1},{1,2},{2,3},{3,4},{4,5},{5,6},{6,7},{8,9},{9,10},{10,11},{11... | collective-permute-start | bytes 1592 | tf_op jit(solution)/shard_map/ppermute | solution.py:20
  275.2 2.7 collective-permute-done.51
  278.5 2.8 collective-permute-start.52
  282.7 4.2 %collective-permute-done.53 = f32[2,1,128]{2,1,0:T(1,128)S(1)} collective-permute-done((f32[2,1,128]{2,1,0:T(1,128)S(1)}, f32[2,1,128]{2,1,0:T(1,128)S(1)}, u32[]{:S(2)}, u32[]{:S(2)}) %collective-permute-start.53) | collective-permute-done | bytes 1056 | tf_op jit(solution)/shard_map/ppermute | solution.py:22
  286.9 3.5 %collective-permute-start.54 = (f32[2,66,1]{2,1,0:T(8,128)S(1)}, f32[2,66,1]{2,1,0:T(8,128)S(1)}, u32[]{:S(2)}, u32[]{:S(2)}) collective-permute-start(f32[2,66,1]{2,1,0:T(8,128)S(1)} %get-tuple-element.55), channel_id=1, source_target_pairs={{0,1},{1,2},{2,3},{3,4},{4,5},{5,6},{6,7},{8,9},{9,10},{10,11},{11... | collective-permute-start | bytes 1592 | tf_op jit(solution)/shard_map/ppermute | solution.py:20
  295.1 2.8 collective-permute-start.56
  299.2 4.2 %collective-permute-done.57 = f32[2,1,128]{2,1,0:T(1,128)S(1)} collective-permute-done((f32[2,1,128]{2,1,0:T(1,128)S(1)}, f32[2,1,128]{2,1,0:T(1,128)S(1)}, u32[]{:S(2)}, u32[]{:S(2)}) %collective-permute-start.57) | collective-permute-done | bytes 1056 | tf_op jit(solution)/shard_map/ppermute | solution.py:22
  303.4 3.5 %collective-permute-start.58 = (f32[2,66,1]{2,1,0:T(8,128)S(1)}, f32[2,66,1]{2,1,0:T(8,128)S(1)}, u32[]{:S(2)}, u32[]{:S(2)}) collective-permute-start(f32[2,66,1]{2,1,0:T(8,128)S(1)} %get-tuple-element.53), channel_id=1, source_target_pairs={{0,1},{1,2},{2,3},{3,4},{4,5},{5,6},{6,7},{8,9},{9,10},{10,11},{11... | collective-permute-start | bytes 1592 | tf_op jit(solution)/shard_map/ppermute | solution.py:20
  312.2 7.6 %all_gather.6 = bf16[256,128]{1,0:T(8,128)(2,1)S(1)} all-gather(bf16[64,128]{1,0:T(8,128)(2,1)S(1)} %get-tuple-element.3), channel_id=1, replica_groups=mesh['grp'=4,'tile'=8] {'grp'}, dimensions={0}, use_global_device_ids=true | all-gather | bytes 81920 | tf_op jit(solution)/shard_map/all_gather | solution.py:148
  321.3 14.6 %psum.7 = f32[32]{0:T(128)S(1)} all-reduce(f32[32]{0:T(128)S(1)} %fusion.4), channel_id=1, replica_groups=mesh['grp'=4,'tile'=8] {'tile'}, use_global_device_ids=true, to_apply=%region_1.2 | all-reduce | flops 32 | bytes 256 | tf_op jit(solution)/shard_map/psum | solution.py:151
  336.1 9.4 %all-reduce = f32[128]{0:T(128)} all-reduce(f32[128]{0:T(128)S(1)} %dynamic-update-slice), channel_id=1, replica_groups=mesh['grp'=4,'tile'=8] {'grp'}, use_global_device_ids=true, to_apply=%add | all-reduce | flops 128 | bytes 1024
  (246 shorter events, 81.2 us)
Async XLA Ops:
  1.5 6.2 %collective-permute-start = (f32[2,2,128]{2,1,0:T(2,128)S(1)}, f32[2,2,128]{2,1,0:T(2,128)S(1)}, u32[]{:S(2)}, u32[]{:S(2)}) collective-permute-start(f32[2,2,128]{2,1,0:T(2,128)S(1)} %get-tuple-element.119), channel_id=1, source_target_pairs={{0,8},{8,16},{16,24},{1,9},{9,17},{17,25},{2,10},{10,18},{18,26},{... | collective-permute-start | bytes 6152 | tf_op jit(solution)/shard_map/ppermute | solution.py:20
  6.4 5.5 %collective-permute-start.1 = (f32[2,2,128]{2,1,0:T(2,128)S(1)}, f32[2,2,128]{2,1,0:T(2,128)S(1)}, u32[]{:S(2)}, u32[]{:S(2)}) collective-permute-start(f32[2,2,128]{2,1,0:T(2,128)S(1)} %get-tuple-element.120), channel_id=1, source_target_pairs={{8,0},{16,8},{24,16},{9,1},{17,9},{25,17},{10,2},{18,10},{26,18},{... | collective-permute-start | bytes 6152 | tf_op jit(solution)/shard_map/ppermute | solution.py:22
  12.7 2.8 collective-permute-start.2
  14.0 5.0 %collective-permute-start.3 = (f32[2,68,2]{2,1,0:T(8,128)S(1)}, f32[2,68,2]{2,1,0:T(8,128)S(1)}, u32[]{:S(2)}, u32[]{:S(2)}) collective-permute-start(f32[2,68,2]{2,1,0:T(8,128)S(1)} %get-tuple-element.88), channel_id=1, source_target_pairs={{1,0},{2,1},{3,2},{4,3},{5,4},{6,5},{7,6},{9,8},{10,9},{11,10},{12... | collective-permute-start | bytes 3272 | tf_op jit(solution)/shard_map/ppermute | solution.py:22
  21.5 5.6 %collective-permute-start.4 = (f32[2,1,128]{2,1,0:T(1,128)S(1)}, f32[2,1,128]{2,1,0:T(1,128)S(1)}, u32[]{:S(2)}, u32[]{:S(2)}) collective-permute-start(f32[2,1,128]{2,1,0:T(1,128)S(1)} %get-tuple-element.117), channel_id=1, source_target_pairs={{0,8},{8,16},{16,24},{1,9},{9,17},{17,25},{2,10},{10,18},{18,26},{... | collective-permute-start | bytes 3080 | tf_op jit(solution)/shard_map/ppermute | solution.py:20
  25.8 5.5 %collective-permute-start.5 = (f32[2,1,128]{2,1,0:T(1,128)S(1)}, f32[2,1,128]{2,1,0:T(1,128)S(1)}, u32[]{:S(2)}, u32[]{:S(2)}) collective-permute-start(f32[2,1,128]{2,1,0:T(1,128)S(1)} %get-tuple-element.118), channel_id=1, source_target_pairs={{8,0},{16,8},{24,16},{9,1},{17,9},{25,17},{10,2},{18,10},{26,18},{... | collective-permute-start | bytes 3080 | tf_op jit(solution)/shard_map/ppermute | solution.py:22
  31.3 4.8 %collective-permute-start.6 = (f32[2,66,1]{2,1,0:T(8,128)S(1)}, f32[2,66,1]{2,1,0:T(8,128)S(1)}, u32[]{:S(2)}, u32[]{:S(2)}) collective-permute-start(f32[2,66,1]{2,1,0:T(8,128)S(1)} %get-tuple-element.79), channel_id=1, source_target_pairs={{0,1},{1,2},{2,3},{3,4},{4,5},{5,6},{6,7},{8,9},{9,10},{10,11},{11... | collective-permute-start | bytes 1592 | tf_op jit(solution)/shard_map/ppermute | solution.py:20
  34.8 4.0 %collective-permute-start.7 = (f32[2,66,1]{2,1,0:T(8,128)S(1)}, f32[2,66,1]{2,1,0:T(8,128)S(1)}, u32[]{:S(2)}, u32[]{:S(2)}) collective-permute-start(f32[2,66,1]{2,1,0:T(8,128)S(1)} %get-tuple-element.80), channel_id=1, source_target_pairs={{1,0},{2,1},{3,2},{4,3},{5,4},{6,5},{7,6},{9,8},{10,9},{11,10},{12... | collective-permute-start | bytes 1592 | tf_op jit(solution)/shard_map/ppermute | solution.py:22
  39.5 4.7 %collective-permute-start.8 = (f32[2,1,128]{2,1,0:T(1,128)S(1)}, f32[2,1,128]{2,1,0:T(1,128)S(1)}, u32[]{:S(2)}, u32[]{:S(2)}) collective-permute-start(f32[2,1,128]{2,1,0:T(1,128)S(1)} %get-tuple-element.115), channel_id=1, source_target_pairs={{0,8},{8,16},{16,24},{1,9},{9,17},{17,25},{2,10},{10,18},{18,26},{... | collective-permute-start | bytes 3080 | tf_op jit(solution)/shard_map/ppermute | solution.py:20
  42.9 5.5 %collective-permute-start.9 = (f32[2,1,128]{2,1,0:T(1,128)S(1)}, f32[2,1,128]{2,1,0:T(1,128)S(1)}, u32[]{:S(2)}, u32[]{:S(2)}) collective-permute-start(f32[2,1,128]{2,1,0:T(1,128)S(1)} %get-tuple-element.116), channel_id=1, source_target_pairs={{8,0},{16,8},{24,16},{9,1},{17,9},{25,17},{10,2},{18,10},{26,18},{... | collective-permute-start | bytes 3080 | tf_op jit(solution)/shard_map/ppermute | solution.py:22
  48.5 4.8 %collective-permute-start.10 = (f32[2,66,1]{2,1,0:T(8,128)S(1)}, f32[2,66,1]{2,1,0:T(8,128)S(1)}, u32[]{:S(2)}, u32[]{:S(2)}) collective-permute-start(f32[2,66,1]{2,1,0:T(8,128)S(1)} %get-tuple-element.77), channel_id=1, source_target_pairs={{0,1},{1,2},{2,3},{3,4},{4,5},{5,6},{6,7},{8,9},{9,10},{10,11},{11... | collective-permute-start | bytes 1592 | tf_op jit(solution)/shard_map/ppermute | solution.py:20
  52.0 4.0 %collective-permute-start.11 = (f32[2,66,1]{2,1,0:T(8,128)S(1)}, f32[2,66,1]{2,1,0:T(8,128)S(1)}, u32[]{:S(2)}, u32[]{:S(2)}) collective-permute-start(f32[2,66,1]{2,1,0:T(8,128)S(1)} %get-tuple-element.78), channel_id=1, source_target_pairs={{1,0},{2,1},{3,2},{4,3},{5,4},{6,5},{7,6},{9,8},{10,9},{11,10},{12... | collective-permute-start | bytes 1592 | tf_op jit(solution)/shard_map/ppermute | solution.py:22
  56.6 4.1 %collective-permute-start.12 = (f32[2,1,128]{2,1,0:T(1,128)S(1)}, f32[2,1,128]{2,1,0:T(1,128)S(1)}, u32[]{:S(2)}, u32[]{:S(2)}) collective-permute-start(f32[2,1,128]{2,1,0:T(1,128)S(1)} %get-tuple-element.113), channel_id=1, source_target_pairs={{0,8},{8,16},{16,24},{1,9},{9,17},{17,25},{2,10},{10,18},{18,26},{... | collective-permute-start | bytes 3080 | tf_op jit(solution)/shard_map/ppermute | solution.py:20
  59.5 5.5 %collective-permute-start.13 = (f32[2,1,128]{2,1,0:T(1,128)S(1)}, f32[2,1,128]{2,1,0:T(1,128)S(1)}, u32[]{:S(2)}, u32[]{:S(2)}) collective-permute-start(f32[2,1,128]{2,1,0:T(1,128)S(1)} %get-tuple-element.114), channel_id=1, source_target_pairs={{8,0},{16,8},{24,16},{9,1},{17,9},{25,17},{10,2},{18,10},{26,18},{... | collective-permute-start | bytes 3080 | tf_op jit(solution)/shard_map/ppermute | solution.py:22
  65.0 4.8 %collective-permute-start.14 = (f32[2,66,1]{2,1,0:T(8,128)S(1)}, f32[2,66,1]{2,1,0:T(8,128)S(1)}, u32[]{:S(2)}, u32[]{:S(2)}) collective-permute-start(f32[2,66,1]{2,1,0:T(8,128)S(1)} %get-tuple-element.75), channel_id=1, source_target_pairs={{0,1},{1,2},{2,3},{3,4},{4,5},{5,6},{6,7},{8,9},{9,10},{10,11},{11... | collective-permute-start | bytes 1592 | tf_op jit(solution)/shard_map/ppermute | solution.py:20
  68.5 4.0 %collective-permute-start.15 = (f32[2,66,1]{2,1,0:T(8,128)S(1)}, f32[2,66,1]{2,1,0:T(8,128)S(1)}, u32[]{:S(2)}, u32[]{:S(2)}) collective-permute-start(f32[2,66,1]{2,1,0:T(8,128)S(1)} %get-tuple-element.76), channel_id=1, source_target_pairs={{1,0},{2,1},{3,2},{4,3},{5,4},{6,5},{7,6},{9,8},{10,9},{11,10},{12... | collective-permute-start | bytes 1592 | tf_op jit(solution)/shard_map/ppermute | solution.py:22
  73.2 4.1 %collective-permute-start.16 = (f32[2,1,128]{2,1,0:T(1,128)S(1)}, f32[2,1,128]{2,1,0:T(1,128)S(1)}, u32[]{:S(2)}, u32[]{:S(2)}) collective-permute-start(f32[2,1,128]{2,1,0:T(1,128)S(1)} %get-tuple-element.111), channel_id=1, source_target_pairs={{0,8},{8,16},{16,24},{1,9},{9,17},{17,25},{2,10},{10,18},{18,26},{... | collective-permute-start | bytes 3080 | tf_op jit(solution)/shard_map/ppermute | solution.py:20
  76.0 5.5 %collective-permute-start.17 = (f32[2,1,128]{2,1,0:T(1,128)S(1)}, f32[2,1,128]{2,1,0:T(1,128)S(1)}, u32[]{:S(2)}, u32[]{:S(2)}) collective-permute-start(f32[2,1,128]{2,1,0:T(1,128)S(1)} %get-tuple-element.112), channel_id=1, source_target_pairs={{8,0},{16,8},{24,16},{9,1},{17,9},{25,17},{10,2},{18,10},{26,18},{... | collective-permute-start | bytes 3080 | tf_op jit(solution)/shard_map/ppermute | solution.py:22
  81.6 4.8 %collective-permute-start.18 = (f32[2,66,1]{2,1,0:T(8,128)S(1)}, f32[2,66,1]{2,1,0:T(8,128)S(1)}, u32[]{:S(2)}, u32[]{:S(2)}) collective-permute-start(f32[2,66,1]{2,1,0:T(8,128)S(1)} %get-tuple-element.73), channel_id=1, source_target_pairs={{0,1},{1,2},{2,3},{3,4},{4,5},{5,6},{6,7},{8,9},{9,10},{10,11},{11... | collective-permute-start | bytes 1592 | tf_op jit(solution)/shard_map/ppermute | solution.py:20
  85.1 4.0 %collective-permute-start.19 = (f32[2,66,1]{2,1,0:T(8,128)S(1)}, f32[2,66,1]{2,1,0:T(8,128)S(1)}, u32[]{:S(2)}, u32[]{:S(2)}) collective-permute-start(f32[2,66,1]{2,1,0:T(8,128)S(1)} %get-tuple-element.74), channel_id=1, source_target_pairs={{1,0},{2,1},{3,2},{4,3},{5,4},{6,5},{7,6},{9,8},{10,9},{11,10},{12... | collective-permute-start | bytes 1592 | tf_op jit(solution)/shard_map/ppermute | solution.py:22
  89.8 4.1 %collective-permute-start.20 = (f32[2,1,128]{2,1,0:T(1,128)S(1)}, f32[2,1,128]{2,1,0:T(1,128)S(1)}, u32[]{:S(2)}, u32[]{:S(2)}) collective-permute-start(f32[2,1,128]{2,1,0:T(1,128)S(1)} %get-tuple-element.109), channel_id=1, source_target_pairs={{0,8},{8,16},{16,24},{1,9},{9,17},{17,25},{2,10},{10,18},{18,26},{... | collective-permute-start | bytes 3080 | tf_op jit(solution)/shard_map/ppermute | solution.py:20
  92.6 5.5 %collective-permute-start.21 = (f32[2,1,128]{2,1,0:T(1,128)S(1)}, f32[2,1,128]{2,1,0:T(1,128)S(1)}, u32[]{:S(2)}, u32[]{:S(2)}) collective-permute-start(f32[2,1,128]{2,1,0:T(1,128)S(1)} %get-tuple-element.110), channel_id=1, source_target_pairs={{8,0},{16,8},{24,16},{9,1},{17,9},{25,17},{10,2},{18,10},{26,18},{... | collective-permute-start | bytes 3080 | tf_op jit(solution)/shard_map/ppermute | solution.py:22
  98.8 13.3 %collective-permute-start.22 = (f32[2,66,1]{2,1,0:T(8,128)}, f32[2,66,1]{2,1,0:T(8,128)S(1)}, u32[]{:S(2)}, u32[]{:S(2)}) collective-permute-start(f32[2,66,1]{2,1,0:T(8,128)} %get-tuple-element.71), channel_id=1, source_target_pairs={{0,1},{1,2},{2,3},{3,4},{4,5},{5,6},{6,7},{8,9},{9,10},{10,11},{11... | collective-permute-start | bytes 1592 | tf_op jit(solution)/shard_map/ppermute | solution.py:20
  102.3 9.8 %collective-permute-start.23 = (f32[2,66,1]{2,1,0:T(8,128)S(1)}, f32[2,66,1]{2,1,0:T(8,128)S(1)}, u32[]{:S(2)}, u32[]{:S(2)}) collective-permute-start(f32[2,66,1]{2,1,0:T(8,128)S(1)} %get-tuple-element.72), channel_id=1, source_target_pairs={{1,0},{2,1},{3,2},{4,3},{5,4},{6,5},{7,6},{9,8},{10,9},{11,10},{12... | collective-permute-start | bytes 1592 | tf_op jit(solution)/shard_map/ppermute | solution.py:22
  104.3 12.4 %all-to-all-start.1 = ((s32[1,1,1,8]{2,1,0,3:T(1,128)}), s32[1,1,1,8]{2,1,0,3:T(1,128)S(1)}, u32[]{:S(2)}, u32[]{:S(2)}) async-start(s32[1,1,1,8]{2,1,0,3:T(1,128)} %copy.44), calls=%async_computation.1 | async-start | bytes 8192 | tf_op jit(solution)/shard_map/all_to_all | solution.py:126
  116.7 14.0 %all-to-all-start = ((s32[1,1,1,512]{2,1,0,3:T(1,128)}), s32[1,1,1,512]{2,1,0,3:T(1,128)}, u32[]{:S(2)}, u32[]{:S(2)}) async-start(s32[1,1,1,512]{2,1,0,3:T(1,128)} %copy.43), calls=%async_computation | async-start | bytes 524288 | tf_op jit(solution)/shard_map/all_to_all | solution.py:125
  120.7 25.1 %collective-permute-start.24 = (f32[2,1,128]{2,1,0:T(1,128)S(1)}, f32[2,1,128]{2,1,0:T(1,128)S(1)}, u32[]{:S(2)}, u32[]{:S(2)}) collective-permute-start(f32[2,1,128]{2,1,0:T(1,128)S(1)} %get-tuple-element.107), channel_id=1, source_target_pairs={{0,8},{8,16},{16,24},{1,9},{9,17},{17,25},{2,10},{10,18},{18,26},{... | collective-permute-start | bytes 3080 | tf_op jit(solution)/shard_map/ppermute | solution.py:20
  123.6 22.2 %collective-permute-start.25 = (f32[2,1,128]{2,1,0:T(1,128)S(1)}, f32[2,1,128]{2,1,0:T(1,128)S(1)}, u32[]{:S(2)}, u32[]{:S(2)}) collective-permute-start(f32[2,1,128]{2,1,0:T(1,128)S(1)} %get-tuple-element.108), channel_id=1, source_target_pairs={{8,0},{16,8},{24,16},{9,1},{17,9},{25,17},{10,2},{18,10},{26,18},{... | collective-permute-start | bytes 3080 | tf_op jit(solution)/shard_map/ppermute | solution.py:22
  130.7 28.4 %all-to-all-start.2 = ((f32[1,1,1,512]{2,1,0,3:T(1,128)}), f32[1,1,1,512]{2,1,0,3:T(1,128)S(1)}, u32[]{:S(2)}, u32[]{:S(2)}) async-start(f32[1,1,1,512]{2,1,0,3:T(1,128)} %copy.45), calls=%async_computation.2 | async-start | bytes 524288 | tf_op jit(solution)/shard_map/all_to_all | solution.py:122
  145.9 3.7 %collective-permute-start.26 = (f32[2,66,1]{2,1,0:T(8,128)S(1)}, f32[2,66,1]{2,1,0:T(8,128)S(1)}, u32[]{:S(2)}, u32[]{:S(2)}) collective-permute-start(f32[2,66,1]{2,1,0:T(8,128)S(1)} %get-tuple-element.69), channel_id=1, source_target_pairs={{0,1},{1,2},{2,3},{3,4},{4,5},{5,6},{6,7},{8,9},{9,10},{10,11},{11... | collective-permute-start | bytes 1592 | tf_op jit(solution)/shard_map/ppermute | solution.py:20
  148.3 4.3 %collective-permute-start.27 = (f32[2,66,1]{2,1,0:T(8,128)S(1)}, f32[2,66,1]{2,1,0:T(8,128)S(1)}, u32[]{:S(2)}, u32[]{:S(2)}) collective-permute-start(f32[2,66,1]{2,1,0:T(8,128)S(1)} %get-tuple-element.70), channel_id=1, source_target_pairs={{1,0},{2,1},{3,2},{4,3},{5,4},{6,5},{7,6},{9,8},{10,9},{11,10},{12... | collective-permute-start | bytes 1592 | tf_op jit(solution)/shard_map/ppermute | solution.py:22
  153.2 18.5 %collective-permute-start.28 = (f32[2,1,128]{2,1,0:T(1,128)S(1)}, f32[2,1,128]{2,1,0:T(1,128)S(1)}, u32[]{:S(2)}, u32[]{:S(2)}) collective-permute-start(f32[2,1,128]{2,1,0:T(1,128)S(1)} %get-tuple-element.105), channel_id=1, source_target_pairs={{0,8},{8,16},{16,24},{1,9},{9,17},{17,25},{2,10},{10,18},{18,26},{... | collective-permute-start | bytes 3080 | tf_op jit(solution)/shard_map/ppermute | solution.py:20
  157.8 14.0 %collective-permute-start.29 = (f32[2,1,128]{2,1,0:T(1,128)S(1)}, f32[2,1,128]{2,1,0:T(1,128)S(1)}, u32[]{:S(2)}, u32[]{:S(2)}) collective-permute-start(f32[2,1,128]{2,1,0:T(1,128)S(1)} %get-tuple-element.106), channel_id=1, source_target_pairs={{8,0},{16,8},{24,16},{9,1},{17,9},{25,17},{10,2},{18,10},{26,18},{... | collective-permute-start | bytes 3080 | tf_op jit(solution)/shard_map/ppermute | solution.py:22
  159.1 11.5 %all-to-all-start.3 = ((f32[8,1,128]{2,1,0:T(1,128)}), f32[8,1,128]{2,1,0:T(1,128)S(1)}, u32[]{:S(2)}, u32[]{:S(2)}) async-start(f32[8,1,128]{2,1,0:T(1,128)} %reshape.279), calls=%async_computation.3 | async-start | bytes 8192 | tf_op jit(solution)/shard_map/all_to_all | solution.py:121
  172.5 3.4 collective-permute-start.30
  174.2 3.5 %collective-permute-start.31 = (f32[2,66,1]{2,1,0:T(8,128)S(1)}, f32[2,66,1]{2,1,0:T(8,128)S(1)}, u32[]{:S(2)}, u32[]{:S(2)}) collective-permute-start(f32[2,66,1]{2,1,0:T(8,128)S(1)} %get-tuple-element.68), channel_id=1, source_target_pairs={{1,0},{2,1},{3,2},{4,3},{5,4},{6,5},{7,6},{9,8},{10,9},{11,10},{12... | collective-permute-start | bytes 1592 | tf_op jit(solution)/shard_map/ppermute | solution.py:22
  192.3 5.8 %collective-permute-start.32 = (f32[2,1,128]{2,1,0:T(1,128)S(1)}, f32[2,1,128]{2,1,0:T(1,128)S(1)}, u32[]{:S(2)}, u32[]{:S(2)}) collective-permute-start(f32[2,1,128]{2,1,0:T(1,128)S(1)} %get-tuple-element.101), channel_id=1, source_target_pairs={{0,8},{8,16},{16,24},{1,9},{9,17},{17,25},{2,10},{10,18},{18,26},{... | collective-permute-start | bytes 3080 | tf_op jit(solution)/shard_map/ppermute | solution.py:20
  196.8 5.5 %collective-permute-start.33 = (f32[2,1,128]{2,1,0:T(1,128)S(1)}, f32[2,1,128]{2,1,0:T(1,128)S(1)}, u32[]{:S(2)}, u32[]{:S(2)}) collective-permute-start(f32[2,1,128]{2,1,0:T(1,128)S(1)} %get-tuple-element.102), channel_id=1, source_target_pairs={{8,0},{16,8},{24,16},{9,1},{17,9},{25,17},{10,2},{18,10},{26,18},{... | collective-permute-start | bytes 3080 | tf_op jit(solution)/shard_map/ppermute | solution.py:22
  202.3 4.9 %collective-permute-start.34 = (f32[2,66,1]{2,1,0:T(8,128)S(1)}, f32[2,66,1]{2,1,0:T(8,128)S(1)}, u32[]{:S(2)}, u32[]{:S(2)}) collective-permute-start(f32[2,66,1]{2,1,0:T(8,128)S(1)} %get-tuple-element.65), channel_id=1, source_target_pairs={{0,1},{1,2},{2,3},{3,4},{4,5},{5,6},{6,7},{8,9},{9,10},{10,11},{11... | collective-permute-start | bytes 1592 | tf_op jit(solution)/shard_map/ppermute | solution.py:20
  205.9 4.0 %collective-permute-start.35 = (f32[2,66,1]{2,1,0:T(8,128)S(1)}, f32[2,66,1]{2,1,0:T(8,128)S(1)}, u32[]{:S(2)}, u32[]{:S(2)}) collective-permute-start(f32[2,66,1]{2,1,0:T(8,128)S(1)} %get-tuple-element.66), channel_id=1, source_target_pairs={{1,0},{2,1},{3,2},{4,3},{5,4},{6,5},{7,6},{9,8},{10,9},{11,10},{12... | collective-permute-start | bytes 1592 | tf_op jit(solution)/shard_map/ppermute | solution.py:22
  210.5 5.9 %collective-permute-start.36 = (f32[2,1,128]{2,1,0:T(1,128)S(1)}, f32[2,1,128]{2,1,0:T(1,128)S(1)}, u32[]{:S(2)}, u32[]{:S(2)}) collective-permute-start(f32[2,1,128]{2,1,0:T(1,128)S(1)} %get-tuple-element.99), channel_id=1, source_target_pairs={{0,8},{8,16},{16,24},{1,9},{9,17},{17,25},{2,10},{10,18},{18,26},{... | collective-permute-start | bytes 3080 | tf_op jit(solution)/shard_map/ppermute | solution.py:20
  215.1 5.5 %collective-permute-start.37 = (f32[2,1,128]{2,1,0:T(1,128)S(1)}, f32[2,1,128]{2,1,0:T(1,128)S(1)}, u32[]{:S(2)}, u32[]{:S(2)}) collective-permute-start(f32[2,1,128]{2,1,0:T(1,128)S(1)} %get-tuple-element.100), channel_id=1, source_target_pairs={{8,0},{16,8},{24,16},{9,1},{17,9},{25,17},{10,2},{18,10},{26,18},{... | collective-permute-start | bytes 3080 | tf_op jit(solution)/shard_map/ppermute | solution.py:22
  220.7 4.8 %collective-permute-start.38 = (f32[2,66,1]{2,1,0:T(8,128)S(1)}, f32[2,66,1]{2,1,0:T(8,128)S(1)}, u32[]{:S(2)}, u32[]{:S(2)}) collective-permute-start(f32[2,66,1]{2,1,0:T(8,128)S(1)} %get-tuple-element.63), channel_id=1, source_target_pairs={{0,1},{1,2},{2,3},{3,4},{4,5},{5,6},{6,7},{8,9},{9,10},{10,11},{11... | collective-permute-start | bytes 1592 | tf_op jit(solution)/shard_map/ppermute | solution.py:20
  224.2 4.0 %collective-permute-start.39 = (f32[2,66,1]{2,1,0:T(8,128)S(1)}, f32[2,66,1]{2,1,0:T(8,128)S(1)}, u32[]{:S(2)}, u32[]{:S(2)}) collective-permute-start(f32[2,66,1]{2,1,0:T(8,128)S(1)} %get-tuple-element.64), channel_id=1, source_target_pairs={{1,0},{2,1},{3,2},{4,3},{5,4},{6,5},{7,6},{9,8},{10,9},{11,10},{12... | collective-permute-start | bytes 1592 | tf_op jit(solution)/shard_map/ppermute | solution.py:22
  228.8 4.1 %collective-permute-start.40 = (f32[2,1,128]{2,1,0:T(1,128)S(1)}, f32[2,1,128]{2,1,0:T(1,128)S(1)}, u32[]{:S(2)}, u32[]{:S(2)}) collective-permute-start(f32[2,1,128]{2,1,0:T(1,128)S(1)} %get-tuple-element.97), channel_id=1, source_target_pairs={{0,8},{8,16},{16,24},{1,9},{9,17},{17,25},{2,10},{10,18},{18,26},{... | collective-permute-start | bytes 3080 | tf_op jit(solution)/shard_map/ppermute | solution.py:20
  231.7 5.5 %collective-permute-start.41 = (f32[2,1,128]{2,1,0:T(1,128)S(1)}, f32[2,1,128]{2,1,0:T(1,128)S(1)}, u32[]{:S(2)}, u32[]{:S(2)}) collective-permute-start(f32[2,1,128]{2,1,0:T(1,128)S(1)} %get-tuple-element.98), channel_id=1, source_target_pairs={{8,0},{16,8},{24,16},{9,1},{17,9},{25,17},{10,2},{18,10},{26,18},{... | collective-permute-start | bytes 3080 | tf_op jit(solution)/shard_map/ppermute | solution.py:22
  237.2 4.8 %collective-permute-start.42 = (f32[2,66,1]{2,1,0:T(8,128)S(1)}, f32[2,66,1]{2,1,0:T(8,128)S(1)}, u32[]{:S(2)}, u32[]{:S(2)}) collective-permute-start(f32[2,66,1]{2,1,0:T(8,128)S(1)} %get-tuple-element.61), channel_id=1, source_target_pairs={{0,1},{1,2},{2,3},{3,4},{4,5},{5,6},{6,7},{8,9},{9,10},{10,11},{11... | collective-permute-start | bytes 1592 | tf_op jit(solution)/shard_map/ppermute | solution.py:20
  240.7 4.0 %collective-permute-start.43 = (f32[2,66,1]{2,1,0:T(8,128)S(1)}, f32[2,66,1]{2,1,0:T(8,128)S(1)}, u32[]{:S(2)}, u32[]{:S(2)}) collective-permute-start(f32[2,66,1]{2,1,0:T(8,128)S(1)} %get-tuple-element.62), channel_id=1, source_target_pairs={{1,0},{2,1},{3,2},{4,3},{5,4},{6,5},{7,6},{9,8},{10,9},{11,10},{12... | collective-permute-start | bytes 1592 | tf_op jit(solution)/shard_map/ppermute | solution.py:22
  245.4 4.1 %collective-permute-start.44 = (f32[2,1,128]{2,1,0:T(1,128)S(1)}, f32[2,1,128]{2,1,0:T(1,128)S(1)}, u32[]{:S(2)}, u32[]{:S(2)}) collective-permute-start(f32[2,1,128]{2,1,0:T(1,128)S(1)} %get-tuple-element.95), channel_id=1, source_target_pairs={{0,8},{8,16},{16,24},{1,9},{9,17},{17,25},{2,10},{10,18},{18,26},{... | collective-permute-start | bytes 3080 | tf_op jit(solution)/shard_map/ppermute | solution.py:20
  248.2 5.5 %collective-permute-start.45 = (f32[2,1,128]{2,1,0:T(1,128)S(1)}, f32[2,1,128]{2,1,0:T(1,128)S(1)}, u32[]{:S(2)}, u32[]{:S(2)}) collective-permute-start(f32[2,1,128]{2,1,0:T(1,128)S(1)} %get-tuple-element.96), channel_id=1, source_target_pairs={{8,0},{16,8},{24,16},{9,1},{17,9},{25,17},{10,2},{18,10},{26,18},{... | collective-permute-start | bytes 3080 | tf_op jit(solution)/shard_map/ppermute | solution.py:22
  253.8 4.8 %collective-permute-start.46 = (f32[2,66,1]{2,1,0:T(8,128)S(1)}, f32[2,66,1]{2,1,0:T(8,128)S(1)}, u32[]{:S(2)}, u32[]{:S(2)}) collective-permute-start(f32[2,66,1]{2,1,0:T(8,128)S(1)} %get-tuple-element.59), channel_id=1, source_target_pairs={{0,1},{1,2},{2,3},{3,4},{4,5},{5,6},{6,7},{8,9},{9,10},{10,11},{11... | collective-permute-start | bytes 1592 | tf_op jit(solution)/shard_map/ppermute | solution.py:20
  257.3 4.0 %collective-permute-start.47 = (f32[2,66,1]{2,1,0:T(8,128)S(1)}, f32[2,66,1]{2,1,0:T(8,128)S(1)}, u32[]{:S(2)}, u32[]{:S(2)}) collective-permute-start(f32[2,66,1]{2,1,0:T(8,128)S(1)} %get-tuple-element.60), channel_id=1, source_target_pairs={{1,0},{2,1},{3,2},{4,3},{5,4},{6,5},{7,6},{9,8},{10,9},{11,10},{12... | collective-permute-start | bytes 1592 | tf_op jit(solution)/shard_map/ppermute | solution.py:22
  262.0 4.1 %collective-permute-start.48 = (f32[2,1,128]{2,1,0:T(1,128)S(1)}, f32[2,1,128]{2,1,0:T(1,128)S(1)}, u32[]{:S(2)}, u32[]{:S(2)}) collective-permute-start(f32[2,1,128]{2,1,0:T(1,128)S(1)} %get-tuple-element.93), channel_id=1, source_target_pairs={{0,8},{8,16},{16,24},{1,9},{9,17},{17,25},{2,10},{10,18},{18,26},{... | collective-permute-start | bytes 3080 | tf_op jit(solution)/shard_map/ppermute | solution.py:20
  264.8 5.5 %collective-permute-start.49 = (f32[2,1,128]{2,1,0:T(1,128)S(1)}, f32[2,1,128]{2,1,0:T(1,128)S(1)}, u32[]{:S(2)}, u32[]{:S(2)}) collective-permute-start(f32[2,1,128]{2,1,0:T(1,128)S(1)} %get-tuple-element.94), channel_id=1, source_target_pairs={{8,0},{16,8},{24,16},{9,1},{17,9},{25,17},{10,2},{18,10},{26,18},{... | collective-permute-start | bytes 3080 | tf_op jit(solution)/shard_map/ppermute | solution.py:22
  270.4 4.8 %collective-permute-start.50 = (f32[2,66,1]{2,1,0:T(8,128)S(1)}, f32[2,66,1]{2,1,0:T(8,128)S(1)}, u32[]{:S(2)}, u32[]{:S(2)}) collective-permute-start(f32[2,66,1]{2,1,0:T(8,128)S(1)} %get-tuple-element.57), channel_id=1, source_target_pairs={{0,1},{1,2},{2,3},{3,4},{4,5},{5,6},{6,7},{8,9},{9,10},{10,11},{11... | collective-permute-start | bytes 1592 | tf_op jit(solution)/shard_map/ppermute | solution.py:20
  273.8 4.0 %collective-permute-start.51 = (f32[2,66,1]{2,1,0:T(8,128)S(1)}, f32[2,66,1]{2,1,0:T(8,128)S(1)}, u32[]{:S(2)}, u32[]{:S(2)}) collective-permute-start(f32[2,66,1]{2,1,0:T(8,128)S(1)} %get-tuple-element.58), channel_id=1, source_target_pairs={{1,0},{2,1},{3,2},{4,3},{5,4},{6,5},{7,6},{9,8},{10,9},{11,10},{12... | collective-permute-start | bytes 1592 | tf_op jit(solution)/shard_map/ppermute | solution.py:22
  278.5 4.1 %collective-permute-start.52 = (f32[2,1,128]{2,1,0:T(1,128)S(1)}, f32[2,1,128]{2,1,0:T(1,128)S(1)}, u32[]{:S(2)}, u32[]{:S(2)}) collective-permute-start(f32[2,1,128]{2,1,0:T(1,128)S(1)} %get-tuple-element.91), channel_id=1, source_target_pairs={{0,8},{8,16},{16,24},{1,9},{9,17},{17,25},{2,10},{10,18},{18,26},{... | collective-permute-start | bytes 3080 | tf_op jit(solution)/shard_map/ppermute | solution.py:20
  281.3 5.5 %collective-permute-start.53 = (f32[2,1,128]{2,1,0:T(1,128)S(1)}, f32[2,1,128]{2,1,0:T(1,128)S(1)}, u32[]{:S(2)}, u32[]{:S(2)}) collective-permute-start(f32[2,1,128]{2,1,0:T(1,128)S(1)} %get-tuple-element.92), channel_id=1, source_target_pairs={{8,0},{16,8},{24,16},{9,1},{17,9},{25,17},{10,2},{18,10},{26,18},{... | collective-permute-start | bytes 3080 | tf_op jit(solution)/shard_map/ppermute | solution.py:22
  286.9 4.8 %collective-permute-start.54 = (f32[2,66,1]{2,1,0:T(8,128)S(1)}, f32[2,66,1]{2,1,0:T(8,128)S(1)}, u32[]{:S(2)}, u32[]{:S(2)}) collective-permute-start(f32[2,66,1]{2,1,0:T(8,128)S(1)} %get-tuple-element.55), channel_id=1, source_target_pairs={{0,1},{1,2},{2,3},{3,4},{4,5},{5,6},{6,7},{8,9},{9,10},{10,11},{11... | collective-permute-start | bytes 1592 | tf_op jit(solution)/shard_map/ppermute | solution.py:20
  290.4 4.0 %collective-permute-start.55 = (f32[2,66,1]{2,1,0:T(8,128)S(1)}, f32[2,66,1]{2,1,0:T(8,128)S(1)}, u32[]{:S(2)}, u32[]{:S(2)}) collective-permute-start(f32[2,66,1]{2,1,0:T(8,128)S(1)} %get-tuple-element.56), channel_id=1, source_target_pairs={{1,0},{2,1},{3,2},{4,3},{5,4},{6,5},{7,6},{9,8},{10,9},{11,10},{12... | collective-permute-start | bytes 1592 | tf_op jit(solution)/shard_map/ppermute | solution.py:22
  295.1 4.1 %collective-permute-start.56 = (f32[2,1,128]{2,1,0:T(1,128)S(1)}, f32[2,1,128]{2,1,0:T(1,128)S(1)}, u32[]{:S(2)}, u32[]{:S(2)}) collective-permute-start(f32[2,1,128]{2,1,0:T(1,128)S(1)} %get-tuple-element.89), channel_id=1, source_target_pairs={{0,8},{8,16},{16,24},{1,9},{9,17},{17,25},{2,10},{10,18},{18,26},{... | collective-permute-start | bytes 3080 | tf_op jit(solution)/shard_map/ppermute | solution.py:20
  297.9 5.5 %collective-permute-start.57 = (f32[2,1,128]{2,1,0:T(1,128)S(1)}, f32[2,1,128]{2,1,0:T(1,128)S(1)}, u32[]{:S(2)}, u32[]{:S(2)}) collective-permute-start(f32[2,1,128]{2,1,0:T(1,128)S(1)} %get-tuple-element.90), channel_id=1, source_target_pairs={{8,0},{16,8},{24,16},{9,1},{17,9},{25,17},{10,2},{18,10},{26,18},{... | collective-permute-start | bytes 3080 | tf_op jit(solution)/shard_map/ppermute | solution.py:22
  303.4 6.1 %collective-permute-start.58 = (f32[2,66,1]{2,1,0:T(8,128)S(1)}, f32[2,66,1]{2,1,0:T(8,128)S(1)}, u32[]{:S(2)}, u32[]{:S(2)}) collective-permute-start(f32[2,66,1]{2,1,0:T(8,128)S(1)} %get-tuple-element.53), channel_id=1, source_target_pairs={{0,1},{1,2},{2,3},{3,4},{4,5},{5,6},{6,7},{8,9},{9,10},{10,11},{11... | collective-permute-start | bytes 1592 | tf_op jit(solution)/shard_map/ppermute | solution.py:20
  306.9 4.0 %collective-permute-start.59 = (f32[2,66,1]{2,1,0:T(8,128)S(1)}, f32[2,66,1]{2,1,0:T(8,128)S(1)}, u32[]{:S(2)}, u32[]{:S(2)}) collective-permute-start(f32[2,66,1]{2,1,0:T(8,128)S(1)} %get-tuple-element.54), channel_id=1, source_target_pairs={{1,0},{2,1},{3,2},{4,3},{5,4},{6,5},{7,6},{9,8},{10,9},{11,10},{12... | collective-permute-start | bytes 1592 | tf_op jit(solution)/shard_map/ppermute | solution.py:22
  (8 other events, 665.3 us)
where the time goes:
time: 348 us; the launch traced here: 346 us
  starting transfers between devices  160 us (46%)
  waiting for transfers between devices  99.5 us (29%)
  other arithmetic  31.6 us (9%)
  blocking collectives  31.6 us (9%)
  local copies, waits for them, and re-layouts  18.6 us (5%)
    ppermute x30, starting transfers between devices, with_halo(): lax.ppermute(tail, axis, [(i, (i + 1) % count) for i in range(ends)])  98.9 us
    ppermute x30, waiting for transfers between devices, with_halo(): lax.ppermute(head, axis, [((i + 1) % count, i) for i in range(ends)])  91 us
    ppermute x30, starting transfers between devices, with_halo(): lax.ppermute(head, axis, [((i + 1) % count, i) for i in range(ends)])  39 us
    psum x1, blocking collectives, on_device(): summed = lax.psum(partial_sum, 'tile')  14.6 us
    all_to_all x1, other arithmetic, on_device(): lax.all_to_all(pixel_cell, 'tile', split_axis=3, concat_axis=1, tiled=True)  10.1 us
    unnamed x1, blocking collectives  9.4 us
    all_gather x1, blocking collectives, on_device(): lax.all_gather(probe_low, 'grp', axis=0, tiled=True).reshape(-1)  7.63 us
  transfers between devices with their start and end apart: 64, of which 29 were waited for; matrix products, arithmetic and copies ran while one was open for 6% of the time, Pallas kernels for 0%

commit v1 on v0

v1 whole, which is shorter than its diff:
```python
import functools

import jax
import jax.numpy as jnp
from jax import lax
from jax.experimental import pallas as pl
from jax.experimental.pallas import tpu as pltpu
from jax.sharding import PartitionSpec as P

SWEEPS = 8
RELAX = 0.8
CAP = 64
CHUNK = 6
HALO = 16
FIELDS = 4
STRIPS = 8
F32 = jnp.float32
BF16 = jnp.bfloat16


def lanes(shape=(8, 128)):
    return lax.broadcasted_iota(jnp.int32, shape, len(shape) - 1)


def fetch(sources, targets, sems):
    copies = [pltpu.make_async_copy(s, d, sems.at[i]) for i, (s, d) in enumerate(zip(sources, targets))]
    for copy in copies:
        copy.start()
    return copies


def pack_tiles_kernel(n_tile, *refs):
    sources, (out_ref, fields_ref), targets, sems = refs[:8], refs[8:10], refs[10:18], refs[18]
    copies = fetch(sources, targets, sems)
    bv_ref, visc_ref, fric_ref, fp_ref, los_ref, weight_ref, cell_ref, count_ref = targets
    t = lax.axis_index("tile")
    parity = lax.rem(t, 2)
    rows = visc_ref.shape[0]
    half = rows // 2
    for copy in copies:
        copy.wait()
    probe = fp_ref[...]
    fields = [-(probe * bv_ref[0]), -(probe * bv_ref[1]), visc_ref[...], fric_ref[...]]
    for f, field in enumerate(fields):
        fields_ref[f] = field
    lane = lanes((half, 128))

    def fold(first_lane):
        packed = jnp.zeros((half, 128), F32)
        for part in range(2):
            for f, field in enumerate(fields):
                start = part * 64 + f * HALO
                piece = field[part * half : (part + 1) * half]
                piece = pltpu.roll(piece, (start - first_lane) % 128, 1)
                packed = jnp.where((lane >= start) & (lane < start + HALO), piece, packed)
        return packed

    @pl.when(t < n_tile - 1)
    def _():
        out_ref[t + 1, 0:half, :] = fold(128 - HALO)

    @pl.when(t > 0)
    def _():
        out_ref[t - 1, 0:half, :] = fold(0)

    row_lane = lanes((1, 128))
    low = lanes((4, 128)) < CAP
    straight, turned = [], []
    for j in range(n_tile // 2):
        at = pl.ds(j * 128, 128)
        count = jnp.where(
            row_lane < CAP, count_ref[0, 0, :, 2 * j : 2 * j + 1], count_ref[0, 0, :, 2 * j + 1 : 2 * j + 2]
        )
        live = (row_lane & (CAP - 1)) < count
        weight = jnp.where(live, weight_ref[0, 0, :, at], 0.0)
        cell = cell_ref[0, 0, :, at].astype(F32)
        block = jnp.concatenate([los_ref[0, 0, :, at], weight, cell], axis=0)
        straight.append(block)
        turned.append(pltpu.roll(block, CAP, 1))
    nothing = jnp.zeros((4, 128), F32)
    in_half = (lanes((4, 128)) // CAP) == parity

    def placed(owner, side):
        if owner < 0 or owner >= n_tile:
            return nothing
        return (straight if owner % 2 == side else turned)[owner // 2]

    for d in range(n_tile):
        solo = jnp.where(parity == d % 2, straight[d // 2], turned[d // 2])
        solo = jnp.where(in_half, solo, 0.0)
        pair = jnp.where(low, placed(d - 1, 0), placed(d + 1, 1))
        out_ref[d, half : half + 8, :] = jnp.concatenate([solo, pair], axis=0)


def pack_rows_kernel(n_tile, fields_ref, got_ref, ext_ref, pix_ref, up_ref, down_ref):
    t = lax.axis_index("tile")
    rows = fields_ref.shape[1]
    half = rows // 2
    fields = [fields_ref[f] for f in range(FIELDS)]
    lane = lanes((half, 128))
    right = jnp.where(t < n_tile - 1, got_ref[jnp.minimum(t + 1, n_tile - 1), 0:half, :], 0.0)
    left = jnp.where(t > 0, got_ref[jnp.maximum(t - 1, 0), 0:half, :], 0.0)
    band = lanes((HALO, 128))
    edge_up = jnp.zeros((HALO, 128), F32)
    edge_down = jnp.zeros((HALO, 128), F32)
    for f, field in enumerate(fields):
        ext_ref[f, :, 0:128] = field
        up_ref[f * HALO : (f + 1) * HALO, :] = field[0:HALO]
        down_ref[f * HALO : (f + 1) * HALO, :] = field[rows - HALO :]
        edges = []
        for part in range(2):
            start = part * 64 + f * HALO
            edge = jnp.where(
                lane < HALO,
                pltpu.roll(right, (0 - start) % 128, 1),
                jnp.where(lane >= 128 - HALO, pltpu.roll(left, (128 - HALO - start) % 128, 1), 0.0),
            )
            ext_ref[f, part * half : (part + 1) * half, 128:256] = edge
            edges.append(edge)
        here = (band >= 2 * f * HALO) & (band < 2 * (f + 1) * HALO)
        turn = (2 * f + 1) * HALO % 128
        edge_up = jnp.where(here, pltpu.roll(edges[0][0:HALO], turn, 1), edge_up)
        edge_down = jnp.where(here, pltpu.roll(edges[1][half - HALO :], turn, 1), edge_down)
    base = FIELDS * HALO
    up_ref[base : base + HALO, :] = edge_up
    down_ref[base : base + HALO, :] = edge_down
    base = base + HALO
    for s in range(n_tile):
        block = got_ref[s, half : half + 8, :]
        pix_ref[8 * s : 8 * s + 8, :] = block
        up_ref[base + 8 * s : base + 8 * s + 8, :] = block
        down_ref[base + 8 * s : base + 8 * s + 8, :] = block


def solve_kernel(
    n_grp, n_tile, ext_ref, pix_ref, above_ref, below_ref, bv_hbm, panels_hbm,
    inc_ref, hess_ref, low_ref, panels_ref,
    plane_ref, coef_ref, src_ref, w_ref, table_ref, hot_ref, acc_ref, out_ref, bv_ref, sems,
):
    copies = fetch((bv_hbm, panels_hbm), (bv_ref, panels_ref), sems)
    g = lax.axis_index("grp")
    t = lax.axis_index("tile")
    rows = ext_ref.shape[1]
    span = rows + 2 * HALO
    groups = span // STRIPS
    lane = lanes()
    first_lane = lane == 0
    last_lane = lane == 127

    band = lanes((HALO, 128))
    for f in range(FIELDS):
        for h in range(2):
            plane_ref[f, h, HALO : HALO + rows, :] = ext_ref[f, :, h * 128 : (h + 1) * 128]
        for ref, at in ((above_ref, 0), (below_ref, HALO + rows)):
            plane_ref[f, 0, at : at + HALO, :] = ref[f * HALO : (f + 1) * HALO, :]
            edge = pltpu.roll(ref[FIELDS * HALO : (FIELDS + 1) * HALO, :], (0 - (2 * f + 1) * HALO) % 128, 1)
            plane_ref[f, 1, at : at + HALO, :] = jnp.where((band < HALO) | (band >= 128 - HALO), edge, 0.0)

    def strided(f, h, v):
        return plane_ref[f, h, pl.ds(v, STRIPS, stride=groups), :]

    def beside(pair):
        a, b = pair
        ra, rb = pltpu.roll(a, 1, 1), pltpu.roll(b, 1, 1)
        before = (jnp.where(first_lane, rb, ra), jnp.where(first_lane, ra, rb))
        ra, rb = pltpu.roll(a, 127, 1), pltpu.roll(b, 127, 1)
        after = (jnp.where(last_lane, rb, ra), jnp.where(last_lane, ra, rb))
        return before, pair, after

    def row(load, v):
        if v < 0:
            return beside(tuple(pltpu.roll(load(h, groups - 1), 1, 0) for h in range(2)))
        if v == groups:
            return beside(tuple(pltpu.roll(load(h, 0), STRIPS - 1, 0) for h in range(2)))
        return beside(tuple(load(h, v) for h in range(2)))

    strip = lax.broadcasted_iota(jnp.int32, (8, 128), 0)
    col_in = [
        None,
        ((lane < HALO) & (t < n_tile - 1)) | ((lane >= 128 - HALO) & (t > 0)),
    ]
    load_visc = functools.partial(strided, 2)
    prev, cur = row(load_visc, -1), row(load_visc, 0)
    for v in range(groups):
        nxt = row(load_visc, v + 1)
        place = g * rows - HALO + strip * groups + v
        row_in = (place >= 0) & (place < n_grp * rows)
        at = pl.ds(v * 8, 8)
        for h in range(2):
            centre = cur[1][h]
            east = 0.5 * (centre + nxt[1][h])
            west = 0.5 * (centre + prev[1][h])
            north = 0.5 * (centre + cur[2][h])
            south = 0.5 * (centre + cur[0][h])
            node_pp = 0.25 * (centre + nxt[1][h] + cur[2][h] + nxt[2][h])
            node_mm = 0.25 * (centre + prev[1][h] + cur[0][h] + prev[0][h])
            node_pm = 0.25 * (centre + nxt[1][h] + cur[0][h] + nxt[0][h])
            node_mp = 0.25 * (centre + prev[1][h] + cur[2][h] + prev[2][h])
            fric = strided(3, h, v)
            diag_x = fric + 2.0 * (east + west) + (north + south)
            diag_y = fric + (east + west) + 2.0 * (north + south)
            inside = row_in if col_in[h] is None else row_in & col_in[h]
            inv_x = jnp.where(inside, RELAX / jnp.where(inside, diag_x, 1.0), 0.0)
            inv_y = jnp.where(inside, RELAX / jnp.where(inside, diag_y, 1.0), 0.0)
            cols = pl.ds(h * 128, 128)
            for i, plane in enumerate(
                (east, west, north, south, 0.25 * node_pp, 0.25 * node_mm, 0.25 * node_pm, 0.25 * node_mp, inv_x, inv_y)
            ):
                coef_ref[i, at, cols] = plane
            src_ref[0, at, cols] = inv_x * strided(0, h, v)
            src_ref[1, at, cols] = inv_y * strided(1, h, v)
        prev, cur = cur, nxt

    def relax():
        w_ref[0] = src_ref[...]

        def sweep(i, _):
            now = lax.rem(i, 2)
            later = 1 - now

            def load(c, h, v):
                return w_ref[now, c, pl.ds(v * 8, 8), pl.ds(h * 128, 128)]

            def both(v):
                return tuple(row(functools.partial(load, c), v) for c in range(2))

            prev, cur = both(-1), both(0)
            for v in range(groups):
                nxt = both(v + 1)
                at = pl.ds(v * 8, 8)
                for h in range(2):
                    cols = pl.ds(h * 128, 128)
                    east, west, north, south, pp, mm, pm, mp, inv_x, inv_y = (
                        coef_ref[i, at, cols] for i in range(10)
                    )

                    def along(c):
                        return (
                            east * nxt[c][1][h] + west * prev[c][1][h],
                            north * cur[c][2][h] + south * cur[c][0][h],
                        )

                    def cross(c):
                        return (
                            pp * nxt[c][2][h] + mm * prev[c][0][h] - pm * nxt[c][0][h] - mp * prev[c][2][h]
                        )

                    one, two = along(0)
                    sum_x = 2.0 * one + two + cross(1)
                    one, two = along(1)
                    sum_y = one + 2.0 * two + cross(0)
                    w_ref[later, 0, at, cols] = (
                        (1.0 - RELAX) * cur[0][1][h] + src_ref[0, at, cols] + inv_x * sum_x
                    )
                    w_ref[later, 1, at, cols] = (
                        (1.0 - RELAX) * cur[1][1][h] + src_ref[1, at, cols] + inv_y * sum_y
                    )
                prev, cur = cur, nxt
            return 0

        lax.fori_loop(0, SWEEPS - 1, sweep, 0)

    relax()
    last = (SWEEPS - 1) % 2
    for c in range(2):
        for v in range(groups):
            out_ref[c, pl.ds(v, STRIPS, stride=groups), :] = w_ref[last, c, pl.ds(v * 8, 8), 0:128]
        inc_ref[c] = out_ref[c, HALO : HALO + rows, :]

    low = lanes((1, 128)) < 64

    def tabulate(slot, block, delta, beyond):
        cell = block[3:4].astype(jnp.int32)
        r = lax.shift_right_logical(cell, 7)
        c = cell & 127
        place = r + HALO + rows * delta
        s = lax.shift_right_arithmetic(place * ((1 << 16) // groups + 1), 16)
        m = (place - s * groups) * 8 + s
        if beyond:
            col_ok = (c < HALO) & (~low) | (c >= 128 - HALO) & low
        else:
            col_ok = c >= 0
        ok = (place >= 0) & (place < span) & col_ok
        weight = jnp.where(ok, block[2:3], 0.0)
        table_ref[slot, 0:8, :] = jnp.concatenate(
            [block[0:2], weight, m.astype(F32), c.astype(F32), jnp.zeros((3, 128), F32)], axis=0
        )

    base = (FIELDS + 1) * HALO
    near, far = 0, 3 * n_tile // 2
    for ref, start, delta in ((pix_ref, 0, 0), (above_ref, base, -1), (below_ref, base, 1)):
        for s in range(0, n_tile, 2):
            one = ref[start + 8 * s : start + 8 * s + 8, :]
            two = ref[start + 8 * s + 8 : start + 8 * s + 16, :]
            tabulate(near, jnp.where(low, one[0:4], two[0:4]), delta, False)
            tabulate(far, one[4:8], delta, True)
            tabulate(far + 1, two[4:8], delta, True)
            near, far = near + 1, far + 2

    acc_ref[...] = jnp.zeros_like(acc_ref)
    for h in range(2):
        field = jnp.concatenate([w_ref[last, c, :, h * 128 : (h + 1) * 128] for c in range(2)], axis=0)
        high = field.astype(BF16)
        hot_ref[h] = jnp.concatenate([high, (field - high.astype(F32)).astype(BF16)], axis=1)
    wide = CHUNK * 128
    row_id = lax.broadcasted_iota(jnp.int32, (span, wide), 0).astype(F32)
    lane_id = lax.broadcasted_iota(jnp.int32, (128, wide), 0).astype(F32)

    def pixels(h, first, j, _):
        data = jnp.concatenate([table_ref[first + j * CHUNK + i] for i in range(CHUNK)], axis=1)
        los_x, los_y, weight = data[0:1], data[1:2], data[2:3]
        hot = jnp.where(lane_id == data[4:5], 1.0, 0.0).astype(BF16)
        got = jnp.dot(hot_ref[h], jnp.concatenate([hot, hot], axis=0), preferred_element_type=F32)
        here = row_id == data[3:4]
        got_x = jnp.sum(jnp.where(here, got[0:span], 0.0), axis=0, keepdims=True)
        got_y = jnp.sum(jnp.where(here, got[span:], 0.0), axis=0, keepdims=True)
        amount = weight * (los_x * got_x + los_y * got_y)
        total = acc_ref[h]
        parts = [amount * los_x, amount * los_y]
        highs = [p.astype(BF16).astype(F32) for p in parts]
        for terms in (highs, [p - q for p, q in zip(parts, highs)]):
            spread = jnp.concatenate([jnp.where(here, p, 0.0).astype(BF16) for p in terms], axis=0)
            total = total + lax.dot_general(
                spread, hot, (((1,), (1,)), ((), ())), preferred_element_type=F32
            )
        acc_ref[h] = total
        return 0

    split = 3 * n_tile // 2
    lax.fori_loop(0, split // CHUNK, functools.partial(pixels, 0, 0), 0)
    lax.fori_loop(0, 2 * split // CHUNK, functools.partial(pixels, 1, split), 0)

    for h in range(2):
        cols = pl.ds(h * 128, 128)
        for c in range(2):
            src_ref[c, :, cols] = coef_ref[8 + c, :, cols] * acc_ref[h, c * span : (c + 1) * span, :]
    relax()
    for c in range(2):
        for v in range(groups):
            out_ref[c, pl.ds(v, STRIPS, stride=groups), :] = w_ref[last, c, pl.ds(v * 8, 8), 0:128]
    for copy in copies:
        copy.wait()
    hess = -(bv_ref[0] * out_ref[0, HALO : HALO + rows, :] + bv_ref[1] * out_ref[1, HALO : HALO + rows, :])
    hess_ref[...] = hess
    low_ref[...] = hess.astype(BF16)


def project_kernel(panels_ref, probe_ref, out_ref):
    count = panels_ref.shape[0]
    probe = probe_ref[...].astype(F32)
    sums = []
    for k in range(count):
        product = panels_ref[k].astype(F32) * probe
        sums.append(jnp.sum(product, axis=0, keepdims=True))
    sums.append(jnp.zeros((128 - count, 128), F32))
    table = jnp.concatenate(sums, axis=0)
    line = lax.dot_general(
        jnp.ones((8, 128), F32), table, (((1,), (1,)), ((), ())),
        precision=lax.Precision.HIGHEST, preferred_element_type=F32,
    )
    line = pltpu.roll(line, lax.axis_index("grp") * count, 1)[0:1]
    out_ref[...] = jnp.broadcast_to(line[None], out_ref.shape)


def add_lines_kernel(lines_ref, out_ref):
    out_ref[...] = jnp.sum(lines_ref[...], axis=0)


def vmem(n):
    return [pl.BlockSpec(memory_space=pltpu.VMEM)] * n


def on_device(
    base_velocity, viscosity, friction, friction_probe, pixel_los, pixel_weight, pixel_cell, pixel_count, panels
):
    n_grp, n_tile = lax.axis_size("grp"), lax.axis_size("tile")
    rows, columns = viscosity.shape
    half = rows // 2
    span = rows + 2 * HALO
    params = pltpu.CompilerParams(vmem_limit_bytes=32 * 2**20)

    inputs = [
        pltpu.with_memory_space_constraint(x, pltpu.HBM)
        for x in (
            base_velocity, viscosity, friction, friction_probe, pixel_los, pixel_weight, pixel_cell, pixel_count
        )
    ]
    slots, fields = pl.pallas_call(
        functools.partial(pack_tiles_kernel, n_tile),
        out_shape=(
            jax.ShapeDtypeStruct((n_tile, half + 8, 128), F32),
            jax.ShapeDtypeStruct((FIELDS, rows, columns), F32),
        ),
        in_specs=[pl.BlockSpec(memory_space=pltpu.HBM)] * len(inputs),
        out_specs=tuple(vmem(2)),
        scratch_shapes=[pltpu.VMEM(x.shape, x.dtype) for x in inputs] + [pltpu.SemaphoreType.DMA((len(inputs),))],
        compiler_params=params,
        name="pack_tiles",
    )(*inputs)
    got = lax.all_to_all(slots, "tile", split_axis=0, concat_axis=0, tiled=True)

    packet = (FIELDS + 1) * HALO + 8 * n_tile
    ext, pix, up, down = pl.pallas_call(
        functools.partial(pack_rows_kernel, n_tile),
        out_shape=(
            jax.ShapeDtypeStruct((FIELDS, rows, 256), F32),
            jax.ShapeDtypeStruct((8 * n_tile, 128), F32),
            jax.ShapeDtypeStruct((packet, 128), F32),
            jax.ShapeDtypeStruct((packet, 128), F32),
        ),
        in_specs=vmem(2),
        out_specs=tuple(vmem(4)),
        compiler_params=params,
        name="pack_rows",
    )(fields, got)
    above = lax.ppermute(down, "grp", [(i, i + 1) for i in range(n_grp - 1)])
    below = lax.ppermute(up, "grp", [(i + 1, i) for i in range(n_grp - 1)])

    tiles = 9 * n_tile // 2
    increment, hessian_probe, probe_low, panels_near = pl.pallas_call(
        functools.partial(solve_kernel, n_grp, n_tile),
        out_shape=(
            jax.ShapeDtypeStruct((2, rows, columns), F32),
            jax.ShapeDtypeStruct((rows, columns), F32),
            jax.ShapeDtypeStruct((rows, columns), BF16),
            jax.ShapeDtypeStruct(panels.shape, BF16),
        ),
        in_specs=vmem(4) + [pl.BlockSpec(memory_space=pltpu.HBM)] * 2,
        out_specs=tuple(vmem(4)),
        scratch_shapes=[
            pltpu.VMEM((FIELDS, 2, span, 128), F32),
            pltpu.VMEM((10, span, 256), F32),
            pltpu.VMEM((2, span, 256), F32),
            pltpu.VMEM((2, 2, span, 256), F32),
            pltpu.VMEM((tiles, 8, 128), F32),
            pltpu.VMEM((2, 2 * span, 256), BF16),
            pltpu.VMEM((2, 2 * span, 128), F32),
            pltpu.VMEM((2, span, 128), F32),
            pltpu.VMEM(base_velocity.shape, F32),
            pltpu.SemaphoreType.DMA((2,)),
        ],
        compiler_params=params,
        name="solve",
    )(ext, pix, above, below, inputs[0], pltpu.with_memory_space_constraint(panels, pltpu.HBM))

    column = lax.all_gather(probe_low, "grp", axis=0, tiled=True)
    partial = pl.pallas_call(
        project_kernel,
        out_shape=jax.ShapeDtypeStruct((n_grp * n_tile, 1, 128), F32),
        in_specs=vmem(2),
        out_specs=pl.BlockSpec(memory_space=pltpu.VMEM),
        compiler_params=params,
        name="project",
    )(panels_near, column)
    everyone = lax.all_to_all(partial, ("grp", "tile"), split_axis=0, concat_axis=0, tiled=True)
    coefficients = pl.pallas_call(
        add_lines_kernel,
        out_shape=jax.ShapeDtypeStruct((1, 128), F32),
        in_specs=vmem(1),
        out_specs=pl.BlockSpec(memory_space=pltpu.VMEM),
        compiler_params=params,
        name="add_lines",
    )(everyone)
    return increment, hessian_probe, coefficients.reshape(128)


def solution(mesh):
    in_specs = (
        P(None, "grp", "tile"),
        P("grp", "tile"),
        P("grp", "tile"),
        P("grp", "tile"),
        P("grp", "tile", None, None),
        P("grp", "tile", None, None),
        P("grp", "tile", None, None),
        P("grp", "tile", None, None),
        P("grp", None, "tile"),
    )
    out_specs = (P(None, "grp", "tile"), P("grp", "tile"), P())
    return jax.shard_map(
        on_device, mesh=mesh, in_specs=in_specs, out_specs=out_specs, check_vma=False
    )
```

time: 348 us -> 53.4 us (0.15)
  starting transfers between devices: 160 us -> 4.69 us
  waiting for transfers between devices: 99.5 us -> 4.95 us
  other arithmetic: 31.6 us -> 0 us
  local copies, waits for them, and re-layouts: 18.6 us -> 0 us
  Pallas kernels: 0 us -> 10.4 us
    ppermute x60 -> x2, starting transfers between devices: 138 us -> 4.69 us  [the longest x1 3.4 us: on_device(): above = lax.ppermute(down, 'grp', [(i, i + 1) for i in range(n_grp - 1)])]
    ppermute x60 -> x2, waiting for transfers between devices: 91.1 us -> 4.95 us  [the longest x1 4.29 us: on_device(): below = lax.ppermute(up, 'grp', [(i + 1, i) for i in range(n_grp - 1)])]
    all_to_all x0 -> x2, blocking collectives: none -> 23.3 us  [the longest x1 13.4 us: on_device(): got = lax.all_to_all(slots, 'tile', split_axis=0, concat_axis=0, tiled=True)]
    all_to_all x4 -> x0, starting transfers between devices: 21.9 us -> none  [the longest x1 6.93 us: on_device(): lax.all_to_all(pixel_count, 'tile', split_axis=3, concat_axis=1, tiled=True)]
    psum x1 -> x0, blocking collectives: 14.6 us -> none  [on_device(): summed = lax.psum(partial_sum, 'tile')]
    all_to_all x4 -> x0, other arithmetic: 12 us -> none  [the longest x1 10.1 us: on_device(): lax.all_to_all(pixel_cell, 'tile', split_axis=3, concat_axis=1, tiled=True)]
    pallas_call x0 -> x5, Pallas kernels: none -> 10.4 us  [the longest x1 7.82 us: on_device(): pl.pallas_call(functools.partial(solve_kernel, n_grp, n_tile), out_shape=...]
    unnamed x1 -> x0, blocking collectives: 9.4 us -> none
  transfers between devices with their start and end apart: 64 -> 2, of which waited for: 29 -> 2; matrix products, arithmetic and copies ran while one was open for 6% -> 0% of each run, Pallas kernels for 0% -> 0%
where the time goes in v1:
time: 53.4 us; the launch traced here: 53.1 us
  blocking collectives  32.4 us (61%)
  Pallas kernels  10.4 us (19%)
  waiting for transfers between devices  4.95 us (9%)
  starting transfers between devices  4.69 us (9%)
  between operations  0.67 us (1%)
    all_to_all x1, blocking collectives, on_device(): got = lax.all_to_all(slots, 'tile', split_axis=0, concat_axis=0, tiled=True)  13.4 us
    all_to_all x1, blocking collectives, on_device(): lax.all_to_all(partial, ('grp', 'tile'), split_axis=0, concat_axis=0, til...  9.89 us
    all_gather x1, blocking collectives, on_device(): column = lax.all_gather(probe_low, 'grp', axis=0, tiled=True)  9.12 us
    pallas_call x1, Pallas kernels, on_device(): pl.pallas_call(functools.partial(solve_kernel, n_grp, n_tile), out_shape=...  7.82 us
    ppermute x1, waiting for transfers between devices, on_device(): below = lax.ppermute(up, 'grp', [(i + 1, i) for i in range(n_grp - 1)])  4.29 us
    ppermute x1, starting transfers between devices, on_device(): above = lax.ppermute(down, 'grp', [(i, i + 1) for i in range(n_grp - 1)])  3.4 us
    ppermute x1, starting transfers between devices, on_device(): below = lax.ppermute(up, 'grp', [(i + 1, i) for i in range(n_grp - 1)])  1.29 us
    pallas_call x1, Pallas kernels, on_device(): pl.pallas_call(functools.partial(pack_tiles_kernel, n_tile), out_shape=(j...  1.18 us
  transfers between devices with their start and end apart: 2, of which 2 were waited for; matrix products, arithmetic and copies ran while one was open for 0% of the time, Pallas kernels for 0%

profile of v1, /device:TPU:0, one launch (start us, length us, event | category | flops | bytes accessed | tf_op | source)
XLA Modules:
  0.0 53.1 jit_solution(14027506335934764851)
XLA Ops:
  0.6 1.2 %pack_tiles.1 = (f32[8,40,128]{2,1,0:T(8,128)S(1)}, f32[4,64,128]{2,1,0:T(8,128)S(1)}) custom-call(f32[2,64,128]{2,1,0:T(8,128)} %bv_hbm.1, f32[64,128]{1,0:T(8,128)} %refs_1_.1, f32[64,128]{1,0:T(8,128)} %refs_2_.1, f32[64,128]{1,0:T(8,128)} %refs_3_.1, f32[1,1,2,512]{3,2,1,0:T(2,128)} %refs_4_.1, f32[1,1,1,512]{3,2,1,0:T(1,128)} %refs_5_.1, ...), custom_call_target="tpu_custom_call" | custom-call | tf_op jit(solution)/shard_map/pack_tiles/pallas_call | solution.py:388
  1.8 13.4 %all_to_all.10.got_ref = f32[8,40,128]{2,1,0:T(8,128)S(1)} all-to-all(f32[8,40,128]{2,1,0:T(8,128)S(1)} %get-tuple-element.14), channel_id=1, replica_groups=mesh['grp'=4,'tile'=8] {'tile'}, dimensions={0} | all-to-all | bytes 327680 | tf_op jit(solution)/shard_map/all_to_all | solution.py:400
  15.3 0.2 pack_rows.1
  15.4 3.4 %collective-permute-start = (f32[144,128]{1,0:T(8,128)S(1)}, f32[144,128]{1,0:T(8,128)S(1)}, u32[]{:S(2)}, u32[]{:S(2)}) collective-permute-start(f32[144,128]{1,0:T(8,128)S(1)} %get-tuple-element.17), channel_id=1, source_target_pairs={{0,8},{8,16},{16,24},{1,9},{9,17},{17,25},{2,10},{10,18},{18,26},{... | collective-permute-start | bytes 221192 | tf_op jit(solution)/shard_map/ppermute | solution.py:416
  18.8 1.3 %collective-permute-start.1 = (f32[144,128]{1,0:T(8,128)S(1)}, f32[144,128]{1,0:T(8,128)S(1)}, u32[]{:S(2)}, u32[]{:S(2)}) collective-permute-start(f32[144,128]{1,0:T(8,128)S(1)} %get-tuple-element.18), channel_id=1, source_target_pairs={{8,0},{16,8},{24,16},{9,1},{17,9},{25,17},{10,2},{18,10},{26,18},{... | collective-permute-start | bytes 221192 | tf_op jit(solution)/shard_map/ppermute | solution.py:417
  20.1 0.7 %collective-permute-done.above_ref = f32[144,128]{1,0:T(8,128)S(1)} collective-permute-done((f32[144,128]{1,0:T(8,128)S(1)}, f32[144,128]{1,0:T(8,128)S(1)}, u32[]{:S(2)}, u32[]{:S(2)}) %collective-permute-start) | collective-permute-done | bytes 73760 | tf_op jit(solution)/shard_map/ppermute | solution.py:416
  20.8 4.3 %collective-permute-done.1.below_ref = f32[144,128]{1,0:T(8,128)S(1)} collective-permute-done((f32[144,128]{1,0:T(8,128)S(1)}, f32[144,128]{1,0:T(8,128)S(1)}, u32[]{:S(2)}, u32[]{:S(2)}) %collective-permute-start.1) | collective-permute-done | bytes 73760 | tf_op jit(solution)/shard_map/ppermute | solution.py:417
  25.1 7.8 %solve.1 = (f32[2,64,128]{2,1,0:T(8,128)}, f32[64,128]{1,0:T(8,128)}, bf16[64,128]{1,0:T(8,128)(2,1)S(1)}, bf16[32,256,128]{2,1,0:T(8,128)(2,1)S(1)}) custom-call(f32[4,64,256]{2,1,0:T(8,128)S(1)} %get-tuple-element.15.ext_ref, f32[64,128]{1,0:T(8,128)S(1)} %get-tuple-element.16.pix_ref, f32[144,128]{1,0:T(8,128)S(1)} %collective-permute-done.above_ref, ...), custom_call_target="tpu_custom_call" | custom-call | tf_op jit(solution)/shard_map/solve/pallas_call | solution.py:420
  32.9 9.1 %all_gather.3.probe_ref = bf16[256,128]{1,0:T(8,128)(2,1)S(1)} all-gather(bf16[64,128]{1,0:T(8,128)(2,1)S(1)} %get-tuple-element.22), channel_id=1, replica_groups=mesh['grp'=4,'tile'=8] {'grp'}, dimensions={0}, use_global_device_ids=true | all-gather | bytes 81920 | tf_op jit(solution)/shard_map/all_gather | solution.py:446
  42.0 0.6 %project.1 = f32[32,1,128]{2,1,0:T(1,128)S(1)} custom-call(bf16[32,256,128]{2,1,0:T(8,128)(2,1)S(1)} %get-tuple-element.21.panels_ref, bf16[256,128]{1,0:T(8,128)(2,1)S(1)} %all_gather.3.probe_ref), custom_call_target="tpu_custom_call" | custom-call | tf_op jit(solution)/shard_map/project/pallas_call | solution.py:447
  42.7 9.9 %all_to_all.11.lines_ref = f32[32,1,128]{2,1,0:T(1,128)S(1)} all-to-all(f32[32,1,128]{2,1,0:T(1,128)S(1)} %project.1), channel_id=1, replica_groups=mesh['grp'=4,'tile'=8] {'grp','tile'}, dimensions={0} | all-to-all | bytes 32768 | tf_op jit(solution)/shard_map/all_to_all | solution.py:455
  52.6 0.5 %add_lines.1 = f32[1,128]{1,0:T(1,128)} custom-call(f32[32,1,128]{2,1,0:T(1,128)S(1)} %all_to_all.11.lines_ref), custom_call_target="tpu_custom_call" | custom-call | tf_op jit(solution)/shard_map/add_lines/pallas_call | solution.py:456
Async XLA Ops:
  15.4 5.4 %collective-permute-start = (f32[144,128]{1,0:T(8,128)S(1)}, f32[144,128]{1,0:T(8,128)S(1)}, u32[]{:S(2)}, u32[]{:S(2)}) collective-permute-start(f32[144,128]{1,0:T(8,128)S(1)} %get-tuple-element.17), channel_id=1, source_target_pairs={{0,8},{8,16},{16,24},{1,9},{9,17},{17,25},{2,10},{10,18},{18,26},{... | collective-permute-start | bytes 221192 | tf_op jit(solution)/shard_map/ppermute | solution.py:416
  18.8 6.2 %collective-permute-start.1 = (f32[144,128]{1,0:T(8,128)S(1)}, f32[144,128]{1,0:T(8,128)S(1)}, u32[]{:S(2)}, u32[]{:S(2)}) collective-permute-start(f32[144,128]{1,0:T(8,128)S(1)} %get-tuple-element.18), channel_id=1, source_target_pairs={{8,0},{16,8},{24,16},{9,1},{17,9},{25,17},{10,2},{18,10},{26,18},{... | collective-permute-start | bytes 221192 | tf_op jit(solution)/shard_map/ppermute | solution.py:417

commit v2 on v1

v2 whole, which is shorter than its diff:
```python
import functools

import jax
import jax.numpy as jnp
from jax import lax
from jax.experimental import pallas as pl
from jax.experimental.pallas import tpu as pltpu
from jax.sharding import PartitionSpec as P

SWEEPS = 8
RELAX = 0.8
CAP = 64
HALO = 16
EDGE = 8
FIELDS = 4
STRIPS = 8
F32 = jnp.float32
BF16 = jnp.bfloat16


def lanes(shape=(8, 128)):
    return lax.broadcasted_iota(jnp.int32, shape, len(shape) - 1)


def fetch(sources, targets, sems):
    copies = [pltpu.make_async_copy(s, d, sems.at[i]) for i, (s, d) in enumerate(zip(sources, targets))]
    for copy in copies:
        copy.start()
    return copies


def pack_tiles_kernel(n_tile, *refs):
    sources, (out_ref, fields_ref), targets, sems = refs[:8], refs[8:10], refs[10:18], refs[18]
    copies = fetch(sources, targets, sems)
    bv_ref, visc_ref, fric_ref, fp_ref, los_ref, weight_ref, cell_ref, count_ref = targets
    t = lax.axis_index("tile")
    parity = lax.rem(t, 2)
    rows = visc_ref.shape[0]
    half = rows // 2
    for copy in copies[4:]:
        copy.wait()
    row_lane = lanes((1, 128))
    low = lanes() < CAP
    straight, turned = [], []
    for j in range(n_tile // 2):
        at = pl.ds(j * 128, 128)
        count = jnp.where(
            row_lane < CAP, count_ref[0, 0, :, 2 * j : 2 * j + 1], count_ref[0, 0, :, 2 * j + 1 : 2 * j + 2]
        )
        live = (row_lane & (CAP - 1)) < count
        weight = jnp.where(live, weight_ref[0, 0, :, at], 0.0)
        scaled = jnp.sqrt(weight) * los_ref[0, 0, :, at]
        high = scaled.astype(BF16).astype(F32)
        cell = cell_ref[0, 0, :, at]
        block = jnp.concatenate(
            [
                high, scaled - high,
                lax.shift_right_logical(cell, 7).astype(F32), (cell & 127).astype(F32), jnp.zeros((2, 128), F32),
            ],
            axis=0,
        )
        straight.append(block)
        turned.append(pltpu.roll(block, CAP, 1))
    nothing = jnp.zeros((8, 128), F32)
    in_half = (lanes() // CAP) == parity

    def placed(owner, side):
        if owner < 0 or owner >= n_tile:
            return nothing
        return (straight if owner % 2 == side else turned)[owner // 2]

    for d in range(n_tile):
        solo = jnp.where(parity == d % 2, straight[d // 2], turned[d // 2])
        solo = jnp.where(in_half, solo, 0.0)
        pair = jnp.where(low, placed(d - 1, 0), placed(d + 1, 1))
        out_ref[d, half : half + 16, :] = jnp.concatenate([solo, pair], axis=0).astype(BF16)

    for copy in copies[:4]:
        copy.wait()
    probe = fp_ref[...]
    fields = [-(probe * bv_ref[0]), -(probe * bv_ref[1]), visc_ref[...], fric_ref[...]]
    for f, field in enumerate(fields):
        fields_ref[f] = field
    lane = lanes((half, 128))

    def fold(first_lane):
        packed = jnp.zeros((half, 128), F32)
        for part in range(2):
            for f, field in enumerate(fields):
                start = part * 64 + f * HALO
                piece = field[part * half : (part + 1) * half]
                piece = pltpu.roll(piece, (start - first_lane) % 128, 1)
                packed = jnp.where((lane >= start) & (lane < start + HALO), piece, packed)
        return packed

    @pl.when(t < n_tile - 1)
    def _():
        out_ref[t + 1, 0:half, :] = fold(128 - HALO).astype(BF16)

    @pl.when(t > 0)
    def _():
        out_ref[t - 1, 0:half, :] = fold(0).astype(BF16)


def pack_rows_kernel(n_grp, n_tile, fields_ref, got_ref, ext_ref, pix_ref, out_ref):
    g = lax.axis_index("grp")
    t = lax.axis_index("tile")
    rows = fields_ref.shape[1]
    half = rows // 2
    fields = [fields_ref[f] for f in range(FIELDS)]
    lane = lanes((half, 128))
    right = jnp.where(t < n_tile - 1, got_ref[jnp.minimum(t + 1, n_tile - 1), 0:half, :].astype(F32), 0.0)
    left = jnp.where(t > 0, got_ref[jnp.maximum(t - 1, 0), 0:half, :].astype(F32), 0.0)
    band = lanes((HALO, 128))
    edge_up = jnp.zeros((HALO, 128), F32)
    edge_down = jnp.zeros((HALO, 128), F32)
    for f, field in enumerate(fields):
        ext_ref[f, :, 0:128] = field
        edges = []
        for part in range(2):
            start = part * 64 + f * HALO
            edge = jnp.where(
                lane < HALO,
                pltpu.roll(right, (0 - start) % 128, 1),
                jnp.where(lane >= 128 - HALO, pltpu.roll(left, (128 - HALO - start) % 128, 1), 0.0),
            )
            ext_ref[f, part * half : (part + 1) * half, 128:256] = edge
            edges.append(edge)
        here = (band >= 2 * f * HALO) & (band < 2 * (f + 1) * HALO)
        turn = (2 * f + 1) * HALO % 128
        edge_up = jnp.where(here, pltpu.roll(edges[0][0:HALO], turn, 1), edge_up)
        edge_down = jnp.where(here, pltpu.roll(edges[1][half - HALO :], turn, 1), edge_down)
    low = lanes() < CAP
    near, far = [], []
    for s in range(0, n_tile, 2):
        one = got_ref[s, half : half + 16, :].astype(F32)
        two = got_ref[s + 1, half : half + 16, :].astype(F32)
        near.append(jnp.where(low, one[0:8], two[0:8]))
        far += [one[8:16], two[8:16]]
    blocks = near + far
    pixels = jnp.concatenate(
        [b[0:1] + b[2:3] for b in blocks]
        + [b[1:2] + b[3:4] for b in blocks]
        + [b[4:5] for b in blocks]
        + [b[5:6] for b in blocks],
        axis=0,
    )
    pix_ref[...] = pixels
    pixels = pixels.astype(BF16)

    def send(slot, first, edge):
        for f, field in enumerate(fields):
            out_ref[slot, f * HALO : (f + 1) * HALO, :] = field[first : first + HALO].astype(BF16)
        base = FIELDS * HALO
        out_ref[slot, base : base + HALO, :] = edge.astype(BF16)
        base = base + HALO
        out_ref[slot, base:, :] = pixels

    @pl.when(g > 0)
    def _():
        send(g - 1, 0, edge_up)

    @pl.when(g < n_grp - 1)
    def _():
        send(g + 1, rows - HALO, edge_down)


def solve_kernel(
    n_grp, n_tile, ext_ref, pix_ref, got_ref, bv_hbm, panels_hbm,
    inc_ref, hess_ref, low_ref, panels_ref,
    plane_ref, coef_ref, src_ref, w_ref, nat_ref, bv_ref, sems,
):
    copies = fetch((bv_hbm, panels_hbm), (bv_ref, panels_ref), sems)
    g = lax.axis_index("grp")
    t = lax.axis_index("tile")
    rows = ext_ref.shape[1]
    span = rows + 2 * HALO
    groups = span // STRIPS
    lane = lanes()

    def above(first, size):
        return jnp.where(g > 0, got_ref[jnp.maximum(g - 1, 0), first : first + size, :].astype(F32), 0.0)

    def below(first, size):
        return jnp.where(g < n_grp - 1, got_ref[jnp.minimum(g + 1, n_grp - 1), first : first + size, :].astype(F32), 0.0)

    first_lane = lane == 0
    last_lane = lane == 127

    band = lanes((HALO, 128))
    for f in range(FIELDS):
        for h in range(2):
            plane_ref[f, h, HALO : HALO + rows, :] = ext_ref[f, :, h * 128 : (h + 1) * 128]
        for load, at in ((above, 0), (below, HALO + rows)):
            plane_ref[f, 0, at : at + HALO, :] = load(f * HALO, HALO)
            edge = pltpu.roll(load(FIELDS * HALO, HALO), (0 - (2 * f + 1) * HALO) % 128, 1)
            plane_ref[f, 1, at : at + HALO, :] = jnp.where((band < HALO) | (band >= 128 - HALO), edge, 0.0)

    def strided(f, h, v):
        return plane_ref[f, h, pl.ds(v, STRIPS, stride=groups), :]

    def beside(pair):
        a, b = pair
        ra, rb = pltpu.roll(a, 1, 1), pltpu.roll(b, 1, 1)
        before = (jnp.where(first_lane, rb, ra), jnp.where(first_lane, ra, rb))
        ra, rb = pltpu.roll(a, 127, 1), pltpu.roll(b, 127, 1)
        after = (jnp.where(last_lane, rb, ra), jnp.where(last_lane, ra, rb))
        return before, pair, after

    def row(load, v):
        if v < 0:
            return beside(tuple(pltpu.roll(load(h, groups - 1), 1, 0) for h in range(2)))
        if v == groups:
            return beside(tuple(pltpu.roll(load(h, 0), STRIPS - 1, 0) for h in range(2)))
        return beside(tuple(load(h, v) for h in range(2)))

    strip = lax.broadcasted_iota(jnp.int32, (8, 128), 0)
    col_in = [
        None,
        ((lane < HALO) & (t < n_tile - 1)) | ((lane >= 128 - HALO) & (t > 0)),
    ]
    load_visc = functools.partial(strided, 2)
    prev, cur = row(load_visc, -1), row(load_visc, 0)
    for v in range(groups):
        nxt = row(load_visc, v + 1)
        place = g * rows - HALO + strip * groups + v
        row_in = (place >= 0) & (place < n_grp * rows)
        at = pl.ds(v * 8, 8)
        for h in range(2):
            centre = cur[1][h]
            east = 0.5 * (centre + nxt[1][h])
            west = 0.5 * (centre + prev[1][h])
            north = 0.5 * (centre + cur[2][h])
            south = 0.5 * (centre + cur[0][h])
            node_pp = 0.25 * (centre + nxt[1][h] + cur[2][h] + nxt[2][h])
            node_mm = 0.25 * (centre + prev[1][h] + cur[0][h] + prev[0][h])
            node_pm = 0.25 * (centre + nxt[1][h] + cur[0][h] + nxt[0][h])
            node_mp = 0.25 * (centre + prev[1][h] + cur[2][h] + prev[2][h])
            fric = strided(3, h, v)
            diag_x = fric + 2.0 * (east + west) + (north + south)
            diag_y = fric + (east + west) + 2.0 * (north + south)
            inside = row_in if col_in[h] is None else row_in & col_in[h]
            inv_x = jnp.where(inside, RELAX / jnp.where(inside, diag_x, 1.0), 0.0)
            inv_y = jnp.where(inside, RELAX / jnp.where(inside, diag_y, 1.0), 0.0)
            cols = pl.ds(h * 128, 128)
            for i, plane in enumerate(
                (east, west, north, south, 0.25 * node_pp, 0.25 * node_mm, 0.25 * node_pm, 0.25 * node_mp, inv_x, inv_y)
            ):
                coef_ref[i, at, cols] = plane
            src_ref[0, at, cols] = inv_x * strided(0, h, v)
            src_ref[1, at, cols] = inv_y * strided(1, h, v)
        prev, cur = cur, nxt

    def natural(h, v):
        return (h, pl.ds(v, STRIPS, stride=groups), slice(None))

    def sweep(i, carry):
        now, later = w_ref.at[i & 1], w_ref.at[1 - (i & 1)]

        def both(v):
            return tuple(row(lambda h, u, c=c: now[c, pl.ds(u * 8, 8), pl.ds(h * 128, 128)], v) for c in range(2))

        prev, cur = both(-1), both(0)
        for v in range(groups):
            nxt = both(v + 1)
            at = pl.ds(v * 8, 8)
            for h in range(2):
                cols = pl.ds(h * 128, 128)
                east, west, north, south, pp, mm, pm, mp, inv_x, inv_y = (coef_ref[k, at, cols] for k in range(10))

                def along(c):
                    return (
                        east * nxt[c][1][h] + west * prev[c][1][h],
                        north * cur[c][2][h] + south * cur[c][0][h],
                    )

                def cross(c):
                    return pp * nxt[c][2][h] + mm * prev[c][0][h] - pm * nxt[c][0][h] - mp * prev[c][2][h]

                one, two = along(0)
                sum_x = 2.0 * one + two + cross(1)
                one, two = along(1)
                sum_y = one + 2.0 * two + cross(0)
                for c, new in ((0, inv_x * sum_x), (1, inv_y * sum_y)):
                    later[c, at, cols] = (1.0 - RELAX) * cur[c][1][h] + src_ref[c, at, cols] + new
            prev, cur = cur, nxt
        return carry

    def solve(phase, carry):
        w_ref[0] = src_ref[...]
        lax.fori_loop(0, SWEEPS - 1, sweep, 0)
        for v in range(groups):
            for h in range(2):
                for c in range(2):
                    nat_ref[(c,) + natural(h, v)] = w_ref[
                        (SWEEPS - 1) % 2, c, pl.ds(v * 8, 8), pl.ds(h * 128, 128)
                    ]

        @pl.when(phase == 0)
        def _():
            for c in range(2):
                inc_ref[c] = nat_ref[c, 0, HALO : HALO + rows, :]
            misfit()

        return carry

    def misfit():
        n_near, n_all = n_tile // 2, 3 * n_tile // 2
        low = lanes((n_tile, 128)) < CAP
        spans = ((0, HALO, rows), (-1, HALO - EDGE, EDGE), (1, HALO + rows, EDGE))
        rim_lane = lanes((2 * rows, 128))
        jobs = []
        for delta, first, size in spans:
            if delta == 0:
                values = pix_ref[...]
            else:
                base = (FIELDS + 1) * HALO
                values = (above if delta < 0 else below)(base, 4 * n_all)
            los_x, los_y, r, c = (values[q * n_all : (q + 1) * n_all] for q in range(4))
            if delta < 0:
                r = r - (rows - EDGE)
            in_rim = c[n_near:] + jnp.where(low, float(EDGE) - 128.0, float(EDGE))
            for h, begin, count, lane_of in ((0, 0, n_near, c[0:n_near]), (1, n_near, n_tile, in_rim)):
                parts = []
                for comp in range(2):
                    part = nat_ref[comp, h, first : first + size, :]
                    parts.append(part if h == 0 else pltpu.roll(part, EDGE, 1))
                field = jnp.concatenate(parts, axis=0)
                high = field.astype(BF16).astype(F32)
                rest = field - high
                if h == 0:
                    stacked = jnp.concatenate([high.astype(BF16), rest.astype(BF16)], axis=1)
                else:
                    lane_here = rim_lane[0 : 2 * size]
                    stacked = jnp.where(lane_here < 2 * EDGE, high, pltpu.roll(rest, 2 * EDGE, 1))
                    stacked = jnp.where(lane_here < 4 * EDGE, stacked, 0.0).astype(BF16)
                jobs.append((h, first, size, begin, count, lane_of, los_x, los_y, r, stacked))

        nat_ref[...] = jnp.zeros_like(nat_ref)
        for h, first, size, begin, count, lane_of, los_x, los_y, r, stacked in jobs:
            chunk = 4 if h == 0 else 8
            depth = 128 if h == 0 else 2 * EDGE
            wide = chunk * 128
            row_id = lax.broadcasted_iota(jnp.int32, (size, wide), 0).astype(F32)
            lane_id = lax.broadcasted_iota(jnp.int32, (depth, wide), 0).astype(F32)
            total = jnp.zeros((4 * size, 128), F32)
            for j in range(0, count, chunk):

                def line(table, offset):
                    return jnp.concatenate([table[offset + i : offset + i + 1] for i in range(j, j + chunk)], axis=1)

                line_x, line_y = line(los_x, begin), line(los_y, begin)
                hot = jnp.where(lane_id == line(lane_of, 0), 1.0, 0.0).astype(BF16)
                here = row_id == line(r, begin)
                twice = [hot, hot]
                if h == 1:
                    twice.append(jnp.zeros((128 - 2 * depth, wide), BF16))
                    hot = jnp.concatenate([hot, jnp.zeros((128 - depth, wide), BF16)], axis=0)
                got = jnp.dot(stacked, jnp.concatenate(twice, axis=0), preferred_element_type=F32)
                got_x = jnp.sum(jnp.where(here, got[0:size], 0.0), axis=0, keepdims=True)
                got_y = jnp.sum(jnp.where(here, got[size:], 0.0), axis=0, keepdims=True)
                amount = line_x * got_x + line_y * got_y
                terms = [amount * line_x, amount * line_y]
                highs = [p.astype(BF16).astype(F32) for p in terms]
                terms = highs + [p - q for p, q in zip(terms, highs)]
                spread = jnp.concatenate([jnp.where(here, p, 0.0) for p in terms], axis=0).astype(BF16)
                total = total + lax.dot_general(spread, hot, (((1,), (1,)), ((), ())), preferred_element_type=F32)
            total = total[0 : 2 * size] + total[2 * size :]
            if h == 1:
                total = pltpu.roll(total, 128 - EDGE, 1)
            for c in range(2):
                nat_ref[c, h, first : first + size, :] = total[c * size : (c + 1) * size]

        for v in range(groups):
            at = pl.ds(v * 8, 8)
            for h in range(2):
                cols = pl.ds(h * 128, 128)
                for c in range(2):
                    src_ref[c, at, cols] = coef_ref[8 + c, at, cols] * nat_ref[(c,) + natural(h, v)]

    lax.fori_loop(0, 2, solve, 0)
    for copy in copies:
        copy.wait()
    hess = -(bv_ref[0] * nat_ref[0, 0, HALO : HALO + rows, :] + bv_ref[1] * nat_ref[1, 0, HALO : HALO + rows, :])
    hess_ref[...] = hess
    low_ref[...] = jnp.broadcast_to(hess.astype(BF16)[None], low_ref.shape)


def project_kernel(panels_ref, probe_ref, out_ref, sums_ref):
    count = panels_ref.shape[0]
    probe = probe_ref[...].reshape(panels_ref.shape[1:])

    def some(i, carry):
        for k in range(4):
            product = panels_ref[4 * i + k].astype(F32) * probe.astype(F32)
            sums_ref[4 * i + k] = jnp.sum(product.reshape(-1, 8, 128), axis=0)
        return carry

    lax.fori_loop(0, count // 4, some, 0)
    table = jnp.sum(sums_ref[...], axis=1)
    table = jnp.concatenate([table, jnp.zeros((128 - count, 128), F32)], axis=0)
    line = lax.dot_general(
        jnp.ones((8, 128), F32), table, (((1,), (1,)), ((), ())),
        precision=lax.Precision.HIGHEST, preferred_element_type=F32,
    )
    line = pltpu.roll(line, lax.axis_index("grp") * count, 1)[0:1]
    out_ref[...] = jnp.broadcast_to(line[None], out_ref.shape)


def add_lines_kernel(lines_ref, out_ref):
    out_ref[...] = jnp.sum(lines_ref[...], axis=0)


def vmem(n):
    return [pl.BlockSpec(memory_space=pltpu.VMEM)] * n


def on_device(
    base_velocity, viscosity, friction, friction_probe, pixel_los, pixel_weight, pixel_cell, pixel_count, panels
):
    n_grp, n_tile = lax.axis_size("grp"), lax.axis_size("tile")
    rows, columns = viscosity.shape
    half = rows // 2
    span = rows + 2 * HALO
    params = pltpu.CompilerParams(vmem_limit_bytes=32 * 2**20)

    inputs = [
        pltpu.with_memory_space_constraint(x, pltpu.HBM)
        for x in (
            base_velocity, viscosity, friction, friction_probe, pixel_los, pixel_weight, pixel_cell, pixel_count
        )
    ]
    slots, fields = pl.pallas_call(
        functools.partial(pack_tiles_kernel, n_tile),
        out_shape=(
            jax.ShapeDtypeStruct((n_tile, half + 16, 128), BF16),
            jax.ShapeDtypeStruct((FIELDS, rows, columns), F32),
        ),
        in_specs=[pl.BlockSpec(memory_space=pltpu.HBM)] * len(inputs),
        out_specs=tuple(vmem(2)),
        scratch_shapes=[pltpu.VMEM(x.shape, x.dtype) for x in inputs] + [pltpu.SemaphoreType.DMA((len(inputs),))],
        compiler_params=params,
        name="pack_tiles",
    )(*inputs)
    got = lax.all_to_all(slots, "tile", split_axis=0, concat_axis=0, tiled=True)

    packet = (FIELDS + 1) * HALO + 6 * n_tile
    ext, pix, packets = pl.pallas_call(
        functools.partial(pack_rows_kernel, n_grp, n_tile),
        out_shape=(
            jax.ShapeDtypeStruct((FIELDS, rows, 256), F32),
            jax.ShapeDtypeStruct((6 * n_tile, 128), F32),
            jax.ShapeDtypeStruct((n_grp, packet, 128), BF16),
        ),
        in_specs=vmem(2),
        out_specs=tuple(vmem(3)),
        compiler_params=params,
        name="pack_rows",
    )(fields, got)
    rims = lax.all_to_all(packets, "grp", split_axis=0, concat_axis=0, tiled=True)

    increment, hessian_probe, probe_low, panels_near = pl.pallas_call(
        functools.partial(solve_kernel, n_grp, n_tile),
        out_shape=(
            jax.ShapeDtypeStruct((2, rows, columns), F32),
            jax.ShapeDtypeStruct((rows, columns), F32),
            jax.ShapeDtypeStruct((n_grp, rows, columns), BF16),
            jax.ShapeDtypeStruct(panels.shape, BF16),
        ),
        in_specs=vmem(3) + [pl.BlockSpec(memory_space=pltpu.HBM)] * 2,
        out_specs=tuple(vmem(4)),
        scratch_shapes=[
            pltpu.VMEM((FIELDS, 2, span, 128), F32),
            pltpu.VMEM((10, span, 256), F32),
            pltpu.VMEM((2, span, 256), F32),
            pltpu.VMEM((2, 2, span, 256), F32),
            pltpu.VMEM((2, 2, span, 128), F32),
            pltpu.VMEM(base_velocity.shape, F32),
            pltpu.SemaphoreType.DMA((2,)),
        ],
        compiler_params=params,
        name="solve",
    )(ext, pix, rims, inputs[0], pltpu.with_memory_space_constraint(panels, pltpu.HBM))

    column = lax.all_to_all(probe_low, "grp", split_axis=0, concat_axis=0, tiled=True)
    partial = pl.pallas_call(
        project_kernel,
        out_shape=jax.ShapeDtypeStruct((n_grp * n_tile, 1, 128), F32),
        in_specs=vmem(2),
        out_specs=pl.BlockSpec(memory_space=pltpu.VMEM),
        scratch_shapes=[pltpu.VMEM((panels.shape[0], 8, 128), F32)],
        compiler_params=params,
        name="project",
    )(panels_near, column)
    everyone = lax.all_to_all(partial, ("grp", "tile"), split_axis=0, concat_axis=0, tiled=True)
    coefficients = pl.pallas_call(
        add_lines_kernel,
        out_shape=jax.ShapeDtypeStruct((1, 128), F32),
        in_specs=vmem(1),
        out_specs=pl.BlockSpec(memory_space=pltpu.VMEM),
        compiler_params=params,
        name="add_lines",
    )(everyone)
    return increment, hessian_probe, coefficients.reshape(128)


def solution(mesh):
    in_specs = (
        P(None, "grp", "tile"),
        P("grp", "tile"),
        P("grp", "tile"),
        P("grp", "tile"),
        P("grp", "tile", None, None),
        P("grp", "tile", None, None),
        P("grp", "tile", None, None),
        P("grp", "tile", None, None),
        P("grp", None, "tile"),
    )
    out_specs = (P(None, "grp", "tile"), P("grp", "tile"), P())
    return jax.shard_map(
        on_device, mesh=mesh, in_specs=in_specs, out_specs=out_specs, check_vma=False
    )
```

time: 53.4 us -> 45.8 us (0.86)
  waiting for transfers between devices: 4.95 us -> 0 us
  blocking collectives: 32.4 us -> 37.1 us
  starting transfers between devices: 4.69 us -> 0 us
  Pallas kernels: 10.4 us -> 7.7 us
    all_to_all x0 -> x2, blocking collectives: none -> 15.7 us  [the longest x1 8.54 us: on_device(): lax.all_to_all(packets, 'grp', split_axis=0, concat_axis=0, tiled=True)]
    all_gather x1 -> x0, blocking collectives: 9.12 us -> none  [on_device(): column = lax.all_gather(probe_low, 'grp', axis=0, tiled=True)]
    ppermute x2 -> x0, waiting for transfers between devices: 4.95 us -> none  [the longest x1 4.29 us: on_device(): below = lax.ppermute(up, 'grp', [(i + 1, i) for i in range(n_grp - 1)])]
    ppermute x2 -> x0, starting transfers between devices: 4.69 us -> none  [the longest x1 3.4 us: on_device(): above = lax.ppermute(down, 'grp', [(i, i + 1) for i in range(n_grp - 1)])]
    pallas_call x1, Pallas kernels: 7.82 us -> 5.05 us  [on_device(): pl.pallas_call(functools.partial(solve_kernel, n_grp, n_tile), out_shape=...]
    all_to_all x1, blocking collectives: 9.89 us -> 8.83 us  [on_device(): lax.all_to_all(partial, ('grp', 'tile'), split_axis=0, concat_axis=0, til...]
    all_to_all x1, blocking collectives: 13.4 us -> 12.5 us  [on_device(): got = lax.all_to_all(slots, 'tile', split_axis=0, concat_axis=0, tiled=True)]
  transfers between devices with their start and end apart: 2 -> 0, of which waited for: 2 -> 0; matrix products, arithmetic and copies ran while one was open for 0% -> 0% of each run, Pallas kernels for 0% -> 0%
where the time goes in v2:
time: 45.8 us; the launch traced here: 45.5 us
  blocking collectives  37.1 us (81%)
  Pallas kernels  7.7 us (17%)
  between operations  0.66 us (1%)
    all_to_all x1, blocking collectives, on_device(): got = lax.all_to_all(slots, 'tile', split_axis=0, concat_axis=0, tiled=True)  12.5 us
    all_to_all x1, blocking collectives, on_device(): lax.all_to_all(partial, ('grp', 'tile'), split_axis=0, concat_axis=0, til...  8.83 us
    all_to_all x1, blocking collectives, on_device(): lax.all_to_all(packets, 'grp', split_axis=0, concat_axis=0, tiled=True)  8.54 us
    all_to_all x1, blocking collectives, on_device(): lax.all_to_all(probe_low, 'grp', split_axis=0, concat_axis=0, tiled=True)  7.21 us
    pallas_call x1, Pallas kernels, on_device(): pl.pallas_call(functools.partial(solve_kernel, n_grp, n_tile), out_shape=...  5.05 us
    pallas_call x1, Pallas kernels, on_device(): pl.pallas_call(functools.partial(pack_tiles_kernel, n_tile), out_shape=(j...  1.14 us

profile of v2, /device:TPU:0, one launch (start us, length us, event | category | flops | bytes accessed | tf_op | source)
XLA Modules:
  0.0 45.5 jit_solution(8568169015940604959)
XLA Ops:
  0.6 1.1 %pack_tiles.1 = (bf16[8,48,128]{2,1,0:T(8,128)(2,1)S(1)}, f32[4,64,128]{2,1,0:T(8,128)S(1)}) custom-call(f32[2,64,128]{2,1,0:T(8,128)} %bv_hbm.1, f32[64,128]{1,0:T(8,128)} %refs_1_.1, f32[64,128]{1,0:T(8,128)} %refs_2_.1, f32[64,128]{1,0:T(8,128)} %refs_3_.1, f32[1,1,2,512]{3,2,1,0:T(2,128)} %refs_4_.1, f32[1,1,1,512]{3,2,1,0:T(1,128)} %refs_5_.1, ...), custom_call_target="tpu_custom_call" | custom-call | tf_op jit(solution)/shard_map/pack_tiles/pallas_call | solution.py:433
  1.8 12.5 %all_to_all.20.got_ref = bf16[8,48,128]{2,1,0:T(8,128)(2,1)S(1)} all-to-all(bf16[8,48,128]{2,1,0:T(8,128)(2,1)S(1)} %get-tuple-element.13), channel_id=1, replica_groups=mesh['grp'=4,'tile'=8] {'tile'}, dimensions={0} | all-to-all | bytes 196608 | tf_op jit(solution)/shard_map/all_to_all | solution.py:445
  14.3 0.2 pack_rows.1
  14.5 8.5 %all_to_all.21.got_ref = bf16[4,128,128]{2,1,0:T(8,128)(2,1)S(1)} all-to-all(bf16[4,128,128]{2,1,0:T(8,128)(2,1)S(1)} %get-tuple-element.16), channel_id=1, replica_groups=mesh['grp'=4,'tile'=8] {'grp'}, dimensions={0} | all-to-all | bytes 262144 | tf_op jit(solution)/shard_map/all_to_all | solution.py:460
  23.0 5.1 %solve.1 = (f32[2,64,128]{2,1,0:T(8,128)}, f32[64,128]{1,0:T(8,128)}, bf16[4,64,128]{2,1,0:T(8,128)(2,1)S(1)}, bf16[32,256,128]{2,1,0:T(8,128)(2,1)S(1)}) custom-call(f32[4,64,256]{2,1,0:T(8,128)S(1)} %get-tuple-element.14.ext_ref, f32[48,128]{1,0:T(8,128)S(1)} %get-tuple-element.15.pix_ref, bf16[4,128,128]{2,1,0:T(8,128)(2,1)S(1)} %all_to_all.21.got_ref, ...), custom_call_target="tpu_custom_call" | custom-call | tf_op jit(solution)/shard_map/solve/pallas_call | solution.py:462
  28.1 7.2 %all_to_all.22.probe_ref = bf16[4,64,128]{2,1,0:T(8,128)(2,1)S(1)} all-to-all(bf16[4,64,128]{2,1,0:T(8,128)(2,1)S(1)} %get-tuple-element.20), channel_id=1, replica_groups=mesh['grp'=4,'tile'=8] {'grp'}, dimensions={0} | all-to-all | bytes 131072 | tf_op jit(solution)/shard_map/all_to_all | solution.py:485
  35.3 0.8 %project.1 = f32[32,1,128]{2,1,0:T(1,128)S(1)} custom-call(bf16[32,256,128]{2,1,0:T(8,128)(2,1)S(1)} %get-tuple-element.19.panels_ref, bf16[4,64,128]{2,1,0:T(8,128)(2,1)S(1)} %all_to_all.22.probe_ref), custom_call_target="tpu_custom_call" | custom-call | tf_op jit(solution)/shard_map/project/pallas_call | solution.py:486
  36.1 8.8 %all_to_all.23.lines_ref = f32[32,1,128]{2,1,0:T(1,128)S(1)} all-to-all(f32[32,1,128]{2,1,0:T(1,128)S(1)} %project.1), channel_id=1, replica_groups=mesh['grp'=4,'tile'=8] {'grp','tile'}, dimensions={0} | all-to-all | bytes 32768 | tf_op jit(solution)/shard_map/all_to_all | solution.py:495
  44.9 0.5 %add_lines.1 = f32[1,128]{1,0:T(1,128)} custom-call(f32[32,1,128]{2,1,0:T(1,128)S(1)} %all_to_all.23.lines_ref), custom_call_target="tpu_custom_call" | custom-call | tf_op jit(solution)/shard_map/add_lines/pallas_call | solution.py:496

commit v3 on v2

--- a/solution.py
+++ b/solution.py
@@ -254,47 +254,61 @@
     def natural(h, v):
         return (h, pl.ds(v, STRIPS, stride=groups), slice(None))
 
-    def sweep(i, carry):
-        now, later = w_ref.at[i & 1], w_ref.at[1 - (i & 1)]
-
-        def both(v):
-            return tuple(row(lambda h, u, c=c: now[c, pl.ds(u * 8, 8), pl.ds(h * 128, 128)], v) for c in range(2))
-
-        prev, cur = both(-1), both(0)
-        for v in range(groups):
-            nxt = both(v + 1)
-            at = pl.ds(v * 8, 8)
-            for h in range(2):
-                cols = pl.ds(h * 128, 128)
-                east, west, north, south, pp, mm, pm, mp, inv_x, inv_y = (coef_ref[k, at, cols] for k in range(10))
-
-                def along(c):
-                    return (
-                        east * nxt[c][1][h] + west * prev[c][1][h],
-                        north * cur[c][2][h] + south * cur[c][0][h],
+    def relax():
+        w_ref[0] = src_ref[...]
+
+        def sweep(now, later, start):
+            rows_seen = {}
+
+            def both(v):
+                if v not in rows_seen:
+                    rows_seen[v] = tuple(
+                        row(lambda h, u, c=c: now[c, pl.ds(u * 8, 8), pl.ds(h * 128, 128)], v) for c in range(2)
                     )
-
-                def cross(c):
-                    return pp * nxt[c][2][h] + mm * prev[c][0][h] - pm * nxt[c][0][h] - mp * prev[c][2][h]
-
-                one, two = along(0)
-                sum_x = 2.0 * one + two + cross(1)
-                one, two = along(1)
-                sum_y = one + 2.0 * two + cross(0)
-                for c, new in ((0, inv_x * sum_x), (1, inv_y * sum_y)):
-                    later[c, at, cols] = (1.0 - RELAX) * cur[c][1][h] + src_ref[c, at, cols] + new
-            prev, cur = cur, nxt
-        return carry
+                return rows_seen[v]
+
+            for p in range(groups):
+                v = (p + start) % groups
+                prev, cur, nxt = both(v - 1), both(v), both(v + 1)
+                at = pl.ds(v * 8, 8)
+                for h in range(2):
+                    cols = pl.ds(h * 128, 128)
+                    east, west, north, south, pp, mm, pm, mp, inv_x, inv_y = (
+                        coef_ref[i, at, cols] for i in range(10)
+                    )
+
+                    def along(c):
+                        return (
+                            east * nxt[c][1][h] + west * prev[c][1][h],
+                            north * cur[c][2][h] + south * cur[c][0][h],
+                        )
+
+                    def cross(c):
+                        return (
+                            pp * nxt[c][2][h] + mm * prev[c][0][h] - pm * nxt[c][0][h] - mp * prev[c][2][h]
+                        )
+
+                    one, two = along(0)
+                    sum_x = 2.0 * one + two + cross(1)
+                    one, two = along(1)
+                    sum_y = one + 2.0 * two + cross(0)
+                    for c, new in ((0, inv_x * sum_x), (1, inv_y * sum_y)):
+                        new = (1.0 - RELAX) * cur[c][1][h] + src_ref[c, at, cols] + new
+                        if later is None:
+                            nat_ref[(c,) + natural(h, v)] = new
+                        else:
+                            later[c, at, cols] = new
+
+        def two_sweeps(_, carry):
+            sweep(w_ref.at[0], w_ref.at[1], 0)
+            sweep(w_ref.at[1], w_ref.at[0], 1)
+            return carry
+
+        lax.fori_loop(0, (SWEEPS - 2) // 2, two_sweeps, 0)
+        sweep(w_ref.at[0], None, 0)
 
     def solve(phase, carry):
-        w_ref[0] = src_ref[...]
-        lax.fori_loop(0, SWEEPS - 1, sweep, 0)
-        for v in range(groups):
-            for h in range(2):
-                for c in range(2):
-                    nat_ref[(c,) + natural(h, v)] = w_ref[
-                        (SWEEPS - 1) % 2, c, pl.ds(v * 8, 8), pl.ds(h * 128, 128)
-                    ]
+        relax()
 
         @pl.when(phase == 0)
         def _():
@@ -386,19 +400,15 @@
     low_ref[...] = jnp.broadcast_to(hess.astype(BF16)[None], low_ref.shape)
 
 
-def project_kernel(panels_ref, probe_ref, out_ref, sums_ref):
+def project_kernel(panels_ref, probe_ref, out_ref):
     count = panels_ref.shape[0]
-    probe = probe_ref[...].reshape(panels_ref.shape[1:])
-
-    def some(i, carry):
-        for k in range(4):
-            product = panels_ref[4 * i + k].astype(F32) * probe.astype(F32)
-            sums_ref[4 * i + k] = jnp.sum(product.reshape(-1, 8, 128), axis=0)
-        return carry
-
-    lax.fori_loop(0, count // 4, some, 0)
-    table = jnp.sum(sums_ref[...], axis=1)
-    table = jnp.concatenate([table, jnp.zeros((128 - count, 128), F32)], axis=0)
+    probe = probe_ref[...].astype(F32).reshape(panels_ref.shape[1:])
+    sums = []
+    for k in range(count):
+        product = panels_ref[k].astype(F32) * probe
+        sums.append(jnp.sum(product, axis=0, keepdims=True))
+    sums.append(jnp.zeros((128 - count, 128), F32))
+    table = jnp.concatenate(sums, axis=0)
     line = lax.dot_general(
         jnp.ones((8, 128), F32), table, (((1,), (1,)), ((), ())),
         precision=lax.Precision.HIGHEST, preferred_element_type=F32,
@@ -488,7 +498,6 @@
         out_shape=jax.ShapeDtypeStruct((n_grp * n_tile, 1, 128), F32),
         in_specs=vmem(2),
         out_specs=pl.BlockSpec(memory_space=pltpu.VMEM),
-        scratch_shapes=[pltpu.VMEM((panels.shape[0], 8, 128), F32)],
         compiler_params=params,
         name="project",
     )(panels_near, column)

time: 45.8 us -> 45.2 us (0.987)
  Pallas kernels: 7.7 us -> 7.15 us
where the time goes in v3:
time: 45.2 us; the launch traced here: 44.9 us
  blocking collectives  37.1 us (82%)
  Pallas kernels  7.15 us (16%)
  between operations  0.66 us (1%)
    all_to_all x1, blocking collectives, on_device(): got = lax.all_to_all(slots, 'tile', split_axis=0, concat_axis=0, tiled=True)  12.5 us
    all_to_all x1, blocking collectives, on_device(): lax.all_to_all(partial, ('grp', 'tile'), split_axis=0, concat_axis=0, til...  8.83 us
    all_to_all x1, blocking collectives, on_device(): lax.all_to_all(packets, 'grp', split_axis=0, concat_axis=0, tiled=True)  8.54 us
    all_to_all x1, blocking collectives, on_device(): lax.all_to_all(probe_low, 'grp', split_axis=0, concat_axis=0, tiled=True)  7.21 us
    pallas_call x1, Pallas kernels, on_device(): pl.pallas_call(functools.partial(solve_kernel, n_grp, n_tile), out_shape=...  4.67 us
    pallas_call x1, Pallas kernels, on_device(): pl.pallas_call(functools.partial(pack_tiles_kernel, n_tile), out_shape=(j...  1.14 us

profile of v3, /device:TPU:0, one launch (start us, length us, event | category | flops | bytes accessed | tf_op | source)
XLA Modules:
  0.0 44.9 jit_solution(13402480753501970571)
XLA Ops:
  0.6 1.1 %pack_tiles.1 = (bf16[8,48,128]{2,1,0:T(8,128)(2,1)S(1)}, f32[4,64,128]{2,1,0:T(8,128)S(1)}) custom-call(f32[2,64,128]{2,1,0:T(8,128)} %bv_hbm.1, f32[64,128]{1,0:T(8,128)} %refs_1_.1, f32[64,128]{1,0:T(8,128)} %refs_2_.1, f32[64,128]{1,0:T(8,128)} %refs_3_.1, f32[1,1,2,512]{3,2,1,0:T(2,128)} %refs_4_.1, f32[1,1,1,512]{3,2,1,0:T(1,128)} %refs_5_.1, ...), custom_call_target="tpu_custom_call" | custom-call | tf_op jit(solution)/shard_map/pack_tiles/pallas_call | solution.py:443
  1.8 12.5 %all_to_all.20.got_ref = bf16[8,48,128]{2,1,0:T(8,128)(2,1)S(1)} all-to-all(bf16[8,48,128]{2,1,0:T(8,128)(2,1)S(1)} %get-tuple-element.13), channel_id=1, replica_groups=mesh['grp'=4,'tile'=8] {'tile'}, dimensions={0} | all-to-all | bytes 196608 | tf_op jit(solution)/shard_map/all_to_all | solution.py:455
  14.3 0.2 pack_rows.1
  14.5 8.5 %all_to_all.21.got_ref = bf16[4,128,128]{2,1,0:T(8,128)(2,1)S(1)} all-to-all(bf16[4,128,128]{2,1,0:T(8,128)(2,1)S(1)} %get-tuple-element.16), channel_id=1, replica_groups=mesh['grp'=4,'tile'=8] {'grp'}, dimensions={0} | all-to-all | bytes 262144 | tf_op jit(solution)/shard_map/all_to_all | solution.py:470
  23.0 4.7 %solve.1 = (f32[2,64,128]{2,1,0:T(8,128)}, f32[64,128]{1,0:T(8,128)}, bf16[4,64,128]{2,1,0:T(8,128)(2,1)S(1)}, bf16[32,256,128]{2,1,0:T(8,128)(2,1)S(1)}) custom-call(f32[4,64,256]{2,1,0:T(8,128)S(1)} %get-tuple-element.14.ext_ref, f32[48,128]{1,0:T(8,128)S(1)} %get-tuple-element.15.pix_ref, bf16[4,128,128]{2,1,0:T(8,128)(2,1)S(1)} %all_to_all.21.got_ref, ...), custom_call_target="tpu_custom_call" | custom-call | tf_op jit(solution)/shard_map/solve/pallas_call | solution.py:472
  27.7 7.2 %all_to_all.22.probe_ref = bf16[4,64,128]{2,1,0:T(8,128)(2,1)S(1)} all-to-all(bf16[4,64,128]{2,1,0:T(8,128)(2,1)S(1)} %get-tuple-element.20), channel_id=1, replica_groups=mesh['grp'=4,'tile'=8] {'grp'}, dimensions={0} | all-to-all | bytes 131072 | tf_op jit(solution)/shard_map/all_to_all | solution.py:495
  34.9 0.6 %project.1 = f32[32,1,128]{2,1,0:T(1,128)S(1)} custom-call(bf16[32,256,128]{2,1,0:T(8,128)(2,1)S(1)} %get-tuple-element.19.panels_ref, bf16[4,64,128]{2,1,0:T(8,128)(2,1)S(1)} %all_to_all.22.probe_ref), custom_call_target="tpu_custom_call" | custom-call | tf_op jit(solution)/shard_map/project/pallas_call | solution.py:496
  35.6 8.8 %all_to_all.23.lines_ref = f32[32,1,128]{2,1,0:T(1,128)S(1)} all-to-all(f32[32,1,128]{2,1,0:T(1,128)S(1)} %project.1), channel_id=1, replica_groups=mesh['grp'=4,'tile'=8] {'grp','tile'}, dimensions={0} | all-to-all | bytes 32768 | tf_op jit(solution)/shard_map/all_to_all | solution.py:504
  44.4 0.5 %add_lines.1 = f32[1,128]{1,0:T(1,128)} custom-call(f32[32,1,128]{2,1,0:T(1,128)S(1)} %all_to_all.23.lines_ref), custom_call_target="tpu_custom_call" | custom-call | tf_op jit(solution)/shard_map/add_lines/pallas_call | solution.py:505

commit v4 on v3

--- a/solution.py
+++ b/solution.py
@@ -102,8 +102,7 @@
         out_ref[t - 1, 0:half, :] = fold(0).astype(BF16)
 
 
-def pack_rows_kernel(n_grp, n_tile, fields_ref, got_ref, ext_ref, pix_ref, out_ref):
-    g = lax.axis_index("grp")
+def pack_rows_kernel(n_tile, fields_ref, got_ref, ext_ref, pix_ref, up_ref, down_ref):
     t = lax.axis_index("tile")
     rows = fields_ref.shape[1]
     half = rows // 2
@@ -148,25 +147,16 @@
     pix_ref[...] = pixels
     pixels = pixels.astype(BF16)
 
-    def send(slot, first, edge):
+    for ref, first, edge in ((up_ref, 0, edge_up), (down_ref, rows - HALO, edge_down)):
         for f, field in enumerate(fields):
-            out_ref[slot, f * HALO : (f + 1) * HALO, :] = field[first : first + HALO].astype(BF16)
+            ref[f * HALO : (f + 1) * HALO, :] = field[first : first + HALO].astype(BF16)
         base = FIELDS * HALO
-        out_ref[slot, base : base + HALO, :] = edge.astype(BF16)
-        base = base + HALO
-        out_ref[slot, base:, :] = pixels
-
-    @pl.when(g > 0)
-    def _():
-        send(g - 1, 0, edge_up)
-
-    @pl.when(g < n_grp - 1)
-    def _():
-        send(g + 1, rows - HALO, edge_down)
+        ref[base : base + HALO, :] = edge.astype(BF16)
+        ref[base + HALO :, :] = pixels
 
 
 def solve_kernel(
-    n_grp, n_tile, ext_ref, pix_ref, got_ref, bv_hbm, panels_hbm,
+    n_grp, n_tile, ext_ref, pix_ref, above_ref, below_ref, bv_hbm, panels_hbm,
     inc_ref, hess_ref, low_ref, panels_ref,
     plane_ref, coef_ref, src_ref, w_ref, nat_ref, bv_ref, sems,
 ):
@@ -179,10 +169,10 @@
     lane = lanes()
 
     def above(first, size):
-        return jnp.where(g > 0, got_ref[jnp.maximum(g - 1, 0), first : first + size, :].astype(F32), 0.0)
+        return jnp.where(g > 0, above_ref[first : first + size, :].astype(F32), 0.0)
 
     def below(first, size):
-        return jnp.where(g < n_grp - 1, got_ref[jnp.minimum(g + 1, n_grp - 1), first : first + size, :].astype(F32), 0.0)
+        return jnp.where(g < n_grp - 1, below_ref[first : first + size, :].astype(F32), 0.0)
 
     first_lane = lane == 0
     last_lane = lane == 127
@@ -299,12 +289,12 @@
                         else:
                             later[c, at, cols] = new
 
-        def two_sweeps(_, carry):
-            sweep(w_ref.at[0], w_ref.at[1], 0)
-            sweep(w_ref.at[1], w_ref.at[0], 1)
+        def three_sweeps(_, carry):
+            for k in range(3):
+                sweep(w_ref.at[k], w_ref.at[(k + 1) % 3], k)
             return carry
 
-        lax.fori_loop(0, (SWEEPS - 2) // 2, two_sweeps, 0)
+        lax.fori_loop(0, (SWEEPS - 2) // 3, three_sweeps, 0)
         sweep(w_ref.at[0], None, 0)
 
     def solve(phase, carry):
@@ -397,11 +387,14 @@
         copy.wait()
     hess = -(bv_ref[0] * nat_ref[0, 0, HALO : HALO + rows, :] + bv_ref[1] * nat_ref[1, 0, HALO : HALO + rows, :])
     hess_ref[...] = hess
-    low_ref[...] = jnp.broadcast_to(hess.astype(BF16)[None], low_ref.shape)
-
-
-def project_kernel(panels_ref, probe_ref, out_ref):
+    low_ref[...] = hess.astype(BF16)
+
+
+def project_kernel(panels_ref, *refs):
+    blocks, out_ref, probe_ref = refs[:-2], refs[-2], refs[-1]
     count = panels_ref.shape[0]
+    for k, block in enumerate(blocks):
+        probe_ref[lax.rem(lax.axis_index("grp") + len(blocks) - k, len(blocks))] = block[...]
     probe = probe_ref[...].astype(F32).reshape(panels_ref.shape[1:])
     sums = []
     for k in range(count):
@@ -455,52 +448,57 @@
     got = lax.all_to_all(slots, "tile", split_axis=0, concat_axis=0, tiled=True)
 
     packet = (FIELDS + 1) * HALO + 6 * n_tile
-    ext, pix, packets = pl.pallas_call(
-        functools.partial(pack_rows_kernel, n_grp, n_tile),
+    ext, pix, up, down = pl.pallas_call(
+        functools.partial(pack_rows_kernel, n_tile),
         out_shape=(
             jax.ShapeDtypeStruct((FIELDS, rows, 256), F32),
             jax.ShapeDtypeStruct((6 * n_tile, 128), F32),
-            jax.ShapeDtypeStruct((n_grp, packet, 128), BF16),
+            jax.ShapeDtypeStruct((packet, 128), BF16),
+            jax.ShapeDtypeStruct((packet, 128), BF16),
         ),
         in_specs=vmem(2),
-        out_specs=tuple(vmem(3)),
+        out_specs=tuple(vmem(4)),
         compiler_params=params,
         name="pack_rows",
     )(fields, got)
-    rims = lax.all_to_all(packets, "grp", split_axis=0, concat_axis=0, tiled=True)
+    above = lax.ppermute(down, "grp", [(i, (i + 1) % n_grp) for i in range(n_grp)])
+    below = lax.ppermute(up, "grp", [((i + 1) % n_grp, i) for i in range(n_grp)])
 
     increment, hessian_probe, probe_low, panels_near = pl.pallas_call(
         functools.partial(solve_kernel, n_grp, n_tile),
         out_shape=(
             jax.ShapeDtypeStruct((2, rows, columns), F32),
             jax.ShapeDtypeStruct((rows, columns), F32),
-            jax.ShapeDtypeStruct((n_grp, rows, columns), BF16),
+            jax.ShapeDtypeStruct((rows, columns), BF16),
             jax.ShapeDtypeStruct(panels.shape, BF16),
         ),
-        in_specs=vmem(3) + [pl.BlockSpec(memory_space=pltpu.HBM)] * 2,
+        in_specs=vmem(4) + [pl.BlockSpec(memory_space=pltpu.HBM)] * 2,
         out_specs=tuple(vmem(4)),
         scratch_shapes=[
             pltpu.VMEM((FIELDS, 2, span, 128), F32),
             pltpu.VMEM((10, span, 256), F32),
             pltpu.VMEM((2, span, 256), F32),
-            pltpu.VMEM((2, 2, span, 256), F32),
+            pltpu.VMEM((3, 2, span, 256), F32),
             pltpu.VMEM((2, 2, span, 128), F32),
             pltpu.VMEM(base_velocity.shape, F32),
             pltpu.SemaphoreType.DMA((2,)),
         ],
         compiler_params=params,
         name="solve",
-    )(ext, pix, rims, inputs[0], pltpu.with_memory_space_constraint(panels, pltpu.HBM))
-
-    column = lax.all_to_all(probe_low, "grp", split_axis=0, concat_axis=0, tiled=True)
+    )(ext, pix, above, below, inputs[0], pltpu.with_memory_space_constraint(panels, pltpu.HBM))
+
+    column = [probe_low] + [
+        lax.ppermute(probe_low, "grp", [(i, (i + k) % n_grp) for i in range(n_grp)]) for k in range(1, n_grp)
+    ]
     partial = pl.pallas_call(
         project_kernel,
         out_shape=jax.ShapeDtypeStruct((n_grp * n_tile, 1, 128), F32),
-        in_specs=vmem(2),
+        in_specs=vmem(1 + n_grp),
         out_specs=pl.BlockSpec(memory_space=pltpu.VMEM),
+        scratch_shapes=[pltpu.VMEM((n_grp, rows, columns), BF16)],
         compiler_params=params,
         name="project",
-    )(panels_near, column)
+    )(panels_near, *column)
     everyone = lax.all_to_all(partial, ("grp", "tile"), split_axis=0, concat_axis=0, tiled=True)
     coefficients = pl.pallas_call(
         add_lines_kernel,

time: 45.2 us -> 43.3 us (0.958)
  blocking collectives: 37.1 us -> 21.4 us
  waiting for transfers between devices: 0 us -> 7.11 us
  starting transfers between devices: 0 us -> 6.88 us
    all_to_all x2 -> x0, blocking collectives: 15.7 us -> none  [the longest x1 8.54 us: on_device(): lax.all_to_all(packets, 'grp', split_axis=0, concat_axis=0, tiled=True)]
    ppermute x0 -> x5, waiting for transfers between devices: none -> 7.11 us  [the longest x3 4.63 us: on_device(): lax.ppermute(probe_low, 'grp', [(i, (i + k) % n_grp) for i in range(n_grp)])]
    ppermute x0 -> x5, starting transfers between devices: none -> 6.88 us  [the longest x3 3.91 us: on_device(): lax.ppermute(probe_low, 'grp', [(i, (i + k) % n_grp) for i in range(n_grp)])]
  transfers between devices with their start and end apart: 0 -> 5, of which waited for: 0 -> 5; matrix products, arithmetic and copies ran while one was open for 0% -> 0% of each run, Pallas kernels for 0% -> 0%
where the time goes in v4:
time: 43.3 us; the launch traced here: 43.1 us
  blocking collectives  21.4 us (49%)
  waiting for transfers between devices  7.11 us (16%)
  Pallas kernels  7.06 us (16%)
  starting transfers between devices  6.88 us (16%)
  between operations  0.66 us (2%)
    all_to_all x1, blocking collectives, on_device(): got = lax.all_to_all(slots, 'tile', split_axis=0, concat_axis=0, tiled=True)  12.5 us
    all_to_all x1, blocking collectives, on_device(): lax.all_to_all(partial, ('grp', 'tile'), split_axis=0, concat_axis=0, til...  8.83 us
    ppermute x3, waiting for transfers between devices, on_device(): lax.ppermute(probe_low, 'grp', [(i, (i + k) % n_grp) for i in range(n_grp)])  4.63 us
    pallas_call x1, Pallas kernels, on_device(): pl.pallas_call(functools.partial(solve_kernel, n_grp, n_tile), out_shape=...  4.55 us
    ppermute x3, starting transfers between devices, on_device(): lax.ppermute(probe_low, 'grp', [(i, (i + k) % n_grp) for i in range(n_grp)])  3.91 us
    ppermute x1, waiting for transfers between devices, on_device(): lax.ppermute(down, 'grp', [(i, (i + 1) % n_grp) for i in range(n_grp)])  2.18 us
    ppermute x1, starting transfers between devices, on_device(): lax.ppermute(down, 'grp', [(i, (i + 1) % n_grp) for i in range(n_grp)])  1.54 us
    ppermute x1, starting transfers between devices, on_device(): lax.ppermute(up, 'grp', [((i + 1) % n_grp, i) for i in range(n_grp)])  1.43 us
  transfers between devices with their start and end apart: 5, of which 5 were waited for; matrix products, arithmetic and copies ran while one was open for 0% of the time, Pallas kernels for 0%

profile of v4, /device:TPU:0, one launch (start us, length us, event | category | flops | bytes accessed | tf_op | source)
XLA Modules:
  0.0 43.1 jit_solution(5976865946523679163)
XLA Ops:
  0.6 1.1 %pack_tiles.1 = (bf16[8,48,128]{2,1,0:T(8,128)(2,1)S(1)}, f32[4,64,128]{2,1,0:T(8,128)S(1)}) custom-call(f32[2,64,128]{2,1,0:T(8,128)} %bv_hbm.1, f32[64,128]{1,0:T(8,128)} %refs_1_.1, f32[64,128]{1,0:T(8,128)} %refs_2_.1, f32[64,128]{1,0:T(8,128)} %refs_3_.1, f32[1,1,2,512]{3,2,1,0:T(2,128)} %refs_4_.1, f32[1,1,1,512]{3,2,1,0:T(1,128)} %refs_5_.1, ...), custom_call_target="tpu_custom_call" | custom-call | tf_op jit(solution)/shard_map/pack_tiles/pallas_call | solution.py:436
  1.8 12.5 %all_to_all.10.got_ref = bf16[8,48,128]{2,1,0:T(8,128)(2,1)S(1)} all-to-all(bf16[8,48,128]{2,1,0:T(8,128)(2,1)S(1)} %get-tuple-element.14), channel_id=1, replica_groups=mesh['grp'=4,'tile'=8] {'tile'}, dimensions={0} | all-to-all | bytes 196608 | tf_op jit(solution)/shard_map/all_to_all | solution.py:448
  14.3 0.2 pack_rows.1
  14.5 1.5 %collective-permute-start = (bf16[128,128]{1,0:T(8,128)(2,1)S(1)}, bf16[128,128]{1,0:T(8,128)(2,1)S(1)}, u32[]{:S(2)}, u32[]{:S(2)}) collective-permute-start(bf16[128,128]{1,0:T(8,128)(2,1)S(1)} %get-tuple-element.17), channel_id=1, source_target_pairs={{0,8},{8,16},{16,24},{24,0},{1,9},{9,17},{17,25},{25,1},{2,10},{10... | collective-permute-start | bytes 98312 | tf_op jit(solution)/shard_map/ppermute | solution.py:464
  16.0 1.4 %collective-permute-start.1 = (bf16[128,128]{1,0:T(8,128)(2,1)S(1)}, bf16[128,128]{1,0:T(8,128)(2,1)S(1)}, u32[]{:S(2)}, u32[]{:S(2)}) collective-permute-start(bf16[128,128]{1,0:T(8,128)(2,1)S(1)} %get-tuple-element.18), channel_id=1, source_target_pairs={{8,0},{16,8},{24,16},{0,24},{9,1},{17,9},{25,17},{1,25},{10,2},{18... | collective-permute-start | bytes 98312 | tf_op jit(solution)/shard_map/ppermute | solution.py:465
  17.5 2.2 %collective-permute-done.above_ref = bf16[128,128]{1,0:T(8,128)(2,1)S(1)} collective-permute-done((bf16[128,128]{1,0:T(8,128)(2,1)S(1)}, bf16[128,128]{1,0:T(8,128)(2,1)S(1)}, u32[]{:S(2)}, u32[]{:S(2)}) %collective-permute-start) | collective-permute-done | bytes 32800 | tf_op jit(solution)/shard_map/ppermute | solution.py:464
  19.7 0.3 collective-permute-done.1.below_ref
  20.0 4.5 %solve.1 = (f32[2,64,128]{2,1,0:T(8,128)}, f32[64,128]{1,0:T(8,128)}, bf16[64,128]{1,0:T(8,128)(2,1)S(1)}, bf16[32,256,128]{2,1,0:T(8,128)(2,1)S(1)}) custom-call(f32[4,64,256]{2,1,0:T(8,128)S(1)} %get-tuple-element.15.ext_ref, f32[48,128]{1,0:T(8,128)S(1)} %get-tuple-element.16.pix_ref, bf16[128,128]{1,0:T(8,128)(2,1)S(1)} %collective-permute-done.above_ref, ...), custom_call_target="tpu_custom_call" | custom-call | tf_op jit(solution)/shard_map/solve/pallas_call | solution.py:467
  24.5 2.4 %collective-permute-start.4 = (bf16[64,128]{1,0:T(8,128)(2,1)S(1)}, bf16[64,128]{1,0:T(8,128)(2,1)S(1)}, u32[]{:S(2)}, u32[]{:S(2)}) collective-permute-start(bf16[64,128]{1,0:T(8,128)(2,1)S(1)} %get-tuple-element.22.refs_0_), channel_id=1, source_target_pairs={{0,24},{8,0},{16,8},{24,16},{1,25},{9,1},{17,9},{25,17},{2,26},{10... | collective-permute-start | bytes 49160 | tf_op jit(solution)/shard_map/ppermute | solution.py:491
  26.9 1.5 %collective-permute-start.3 = (bf16[64,128]{1,0:T(8,128)(2,1)S(1)}, bf16[64,128]{1,0:T(8,128)(2,1)S(1)}, u32[]{:S(2)}, u32[]{:S(2)}) collective-permute-start(bf16[64,128]{1,0:T(8,128)(2,1)S(1)} %get-tuple-element.22.refs_0_), channel_id=1, source_target_pairs={{0,16},{8,24},{16,0},{24,8},{1,17},{9,25},{17,1},{25,9},{2,18},{10... | collective-permute-start | bytes 49160 | tf_op jit(solution)/shard_map/ppermute | solution.py:491
  28.4 0.0 collective-permute-start.2
  28.4 0.3 collective-permute-done.4.refs_3_
  28.7 2.0 %collective-permute-done.3.refs_2_ = bf16[64,128]{1,0:T(8,128)(2,1)S(1)} collective-permute-done((bf16[64,128]{1,0:T(8,128)(2,1)S(1)}, bf16[64,128]{1,0:T(8,128)(2,1)S(1)}, u32[]{:S(2)}, u32[]{:S(2)}) %collective-permute-start.3) | collective-permute-done | bytes 16416 | tf_op jit(solution)/shard_map/ppermute | solution.py:491
  30.6 2.4 %collective-permute-done.2.refs_1_ = bf16[64,128]{1,0:T(8,128)(2,1)S(1)} collective-permute-done((bf16[64,128]{1,0:T(8,128)(2,1)S(1)}, bf16[64,128]{1,0:T(8,128)(2,1)S(1)}, u32[]{:S(2)}, u32[]{:S(2)}) %collective-permute-start.2) | collective-permute-done | bytes 16416 | tf_op jit(solution)/shard_map/ppermute | solution.py:491
  33.1 0.7 %project.1 = f32[32,1,128]{2,1,0:T(1,128)S(1)} custom-call(bf16[32,256,128]{2,1,0:T(8,128)(2,1)S(1)} %get-tuple-element.21.panels_ref, bf16[64,128]{1,0:T(8,128)(2,1)S(1)} %get-tuple-element.22.refs_0_, bf16[64,128]{1,0:T(8,128)(2,1)S(1)} %collective-permute-done.2.refs_1_, bf16[64,128]{1,0:T(8,128)(2,1)S(1)} %collective-permute-done.3.refs_2_, ...), custom_call_target="tpu_custom_call" | custom-call | tf_op jit(solution)/shard_map/project/pallas_call | solution.py:493
  33.7 8.8 %all_to_all.11.lines_ref = f32[32,1,128]{2,1,0:T(1,128)S(1)} all-to-all(f32[32,1,128]{2,1,0:T(1,128)S(1)} %project.1), channel_id=1, replica_groups=mesh['grp'=4,'tile'=8] {'grp','tile'}, dimensions={0} | all-to-all | bytes 32768 | tf_op jit(solution)/shard_map/all_to_all | solution.py:502
  42.6 0.5 %add_lines.1 = f32[1,128]{1,0:T(1,128)} custom-call(f32[32,1,128]{2,1,0:T(1,128)S(1)} %all_to_all.11.lines_ref), custom_call_target="tpu_custom_call" | custom-call | tf_op jit(solution)/shard_map/add_lines/pallas_call | solution.py:503
Async XLA Ops:
  14.5 5.2 %collective-permute-start = (bf16[128,128]{1,0:T(8,128)(2,1)S(1)}, bf16[128,128]{1,0:T(8,128)(2,1)S(1)}, u32[]{:S(2)}, u32[]{:S(2)}) collective-permute-start(bf16[128,128]{1,0:T(8,128)(2,1)S(1)} %get-tuple-element.17), channel_id=1, source_target_pairs={{0,8},{8,16},{16,24},{24,0},{1,9},{9,17},{17,25},{25,1},{2,10},{10... | collective-permute-start | bytes 98312 | tf_op jit(solution)/shard_map/ppermute | solution.py:464
  16.0 3.9 %collective-permute-start.1 = (bf16[128,128]{1,0:T(8,128)(2,1)S(1)}, bf16[128,128]{1,0:T(8,128)(2,1)S(1)}, u32[]{:S(2)}, u32[]{:S(2)}) collective-permute-start(bf16[128,128]{1,0:T(8,128)(2,1)S(1)} %get-tuple-element.18), channel_id=1, source_target_pairs={{8,0},{16,8},{24,16},{0,24},{9,1},{17,9},{25,17},{1,25},{10,2},{18... | collective-permute-start | bytes 98312 | tf_op jit(solution)/shard_map/ppermute | solution.py:465
  24.5 4.2 %collective-permute-start.4 = (bf16[64,128]{1,0:T(8,128)(2,1)S(1)}, bf16[64,128]{1,0:T(8,128)(2,1)S(1)}, u32[]{:S(2)}, u32[]{:S(2)}) collective-permute-start(bf16[64,128]{1,0:T(8,128)(2,1)S(1)} %get-tuple-element.22.refs_0_), channel_id=1, source_target_pairs={{0,24},{8,0},{16,8},{24,16},{1,25},{9,1},{17,9},{25,17},{2,26},{10... | collective-permute-start | bytes 49160 | tf_op jit(solution)/shard_map/ppermute | solution.py:491
  26.9 3.7 %collective-permute-start.3 = (bf16[64,128]{1,0:T(8,128)(2,1)S(1)}, bf16[64,128]{1,0:T(8,128)(2,1)S(1)}, u32[]{:S(2)}, u32[]{:S(2)}) collective-permute-start(bf16[64,128]{1,0:T(8,128)(2,1)S(1)} %get-tuple-element.22.refs_0_), channel_id=1, source_target_pairs={{0,16},{8,24},{16,0},{24,8},{1,17},{9,25},{17,1},{25,9},{2,18},{10... | collective-permute-start | bytes 49160 | tf_op jit(solution)/shard_map/ppermute | solution.py:491
  28.4 4.6 %collective-permute-start.2 = (bf16[64,128]{1,0:T(8,128)(2,1)S(1)}, bf16[64,128]{1,0:T(8,128)(2,1)S(1)}, u32[]{:S(2)}, u32[]{:S(2)}) collective-permute-start(bf16[64,128]{1,0:T(8,128)(2,1)S(1)} %get-tuple-element.22.refs_0_), channel_id=1, source_target_pairs={{0,8},{8,16},{16,24},{24,0},{1,9},{9,17},{17,25},{25,1},{2,10},{10... | collective-permute-start | bytes 49160 | tf_op jit(solution)/shard_map/ppermute | solution.py:491

commit v5 on v4

--- a/solution.py
+++ b/solution.py
@@ -102,7 +102,8 @@
         out_ref[t - 1, 0:half, :] = fold(0).astype(BF16)
 
 
-def pack_rows_kernel(n_tile, fields_ref, got_ref, ext_ref, pix_ref, up_ref, down_ref):
+def pack_rows_kernel(n_tile, fields_ref, got_ref, ext_ref, pix_ref, even_ref, odd_ref):
+    g = lax.axis_index("grp")
     t = lax.axis_index("tile")
     rows = fields_ref.shape[1]
     half = rows // 2
@@ -147,16 +148,23 @@
     pix_ref[...] = pixels
     pixels = pixels.astype(BF16)
 
-    for ref, first, edge in ((up_ref, 0, edge_up), (down_ref, rows - HALO, edge_down)):
-        for f, field in enumerate(fields):
-            ref[f * HALO : (f + 1) * HALO, :] = field[first : first + HALO].astype(BF16)
-        base = FIELDS * HALO
-        ref[base : base + HALO, :] = edge.astype(BF16)
-        ref[base + HALO :, :] = pixels
+    even = lax.rem(g, 2) == 0
+
+    def choose(one, two):
+        even_ref_value, odd_ref_value = jnp.where(even, one, two), jnp.where(even, two, one)
+        return even_ref_value.astype(BF16), odd_ref_value.astype(BF16)
+
+    for f, field in enumerate(fields):
+        at = pl.ds(f * HALO, HALO)
+        even_ref[at, :], odd_ref[at, :] = choose(field[rows - HALO :], field[0:HALO])
+    at = pl.ds(FIELDS * HALO, HALO)
+    even_ref[at, :], odd_ref[at, :] = choose(edge_down, edge_up)
+    for ref in (even_ref, odd_ref):
+        ref[(FIELDS + 1) * HALO :, :] = pixels
 
 
 def solve_kernel(
-    n_grp, n_tile, ext_ref, pix_ref, above_ref, below_ref, bv_hbm, panels_hbm,
+    n_grp, n_tile, ext_ref, pix_ref, even_ref, odd_ref, bv_hbm, panels_hbm,
     inc_ref, hess_ref, low_ref, panels_ref,
     plane_ref, coef_ref, src_ref, w_ref, nat_ref, bv_ref, sems,
 ):
@@ -168,11 +176,17 @@
     groups = span // STRIPS
     lane = lanes()
 
+    even = lax.rem(g, 2) == 0
+
     def above(first, size):
-        return jnp.where(g > 0, above_ref[first : first + size, :].astype(F32), 0.0)
+        at = pl.ds(first, size)
+        got = jnp.where(even, odd_ref[at, :].astype(F32), even_ref[at, :].astype(F32))
+        return jnp.where(g > 0, got, 0.0)
 
     def below(first, size):
-        return jnp.where(g < n_grp - 1, below_ref[first : first + size, :].astype(F32), 0.0)
+        at = pl.ds(first, size)
+        got = jnp.where(even, even_ref[at, :].astype(F32), odd_ref[at, :].astype(F32))
+        return jnp.where(g < n_grp - 1, got, 0.0)
 
     first_lane = lane == 0
     last_lane = lane == 127
@@ -394,7 +408,7 @@
     blocks, out_ref, probe_ref = refs[:-2], refs[-2], refs[-1]
     count = panels_ref.shape[0]
     for k, block in enumerate(blocks):
-        probe_ref[lax.rem(lax.axis_index("grp") + len(blocks) - k, len(blocks))] = block[...]
+        probe_ref[lax.axis_index("grp") ^ (len(blocks) - 1 - k)] = block[...]
     probe = probe_ref[...].astype(F32).reshape(panels_ref.shape[1:])
     sums = []
     for k in range(count):
@@ -448,7 +462,7 @@
     got = lax.all_to_all(slots, "tile", split_axis=0, concat_axis=0, tiled=True)
 
     packet = (FIELDS + 1) * HALO + 6 * n_tile
-    ext, pix, up, down = pl.pallas_call(
+    ext, pix, even, odd = pl.pallas_call(
         functools.partial(pack_rows_kernel, n_tile),
         out_shape=(
             jax.ShapeDtypeStruct((FIELDS, rows, 256), F32),
@@ -461,8 +475,8 @@
         compiler_params=params,
         name="pack_rows",
     )(fields, got)
-    above = lax.ppermute(down, "grp", [(i, (i + 1) % n_grp) for i in range(n_grp)])
-    below = lax.ppermute(up, "grp", [((i + 1) % n_grp, i) for i in range(n_grp)])
+    odd = lax.ppermute(odd, "grp", [(i, (i - 1 + 2 * (i % 2)) % n_grp) for i in range(n_grp)])
+    even = lax.ppermute(even, "grp", [(i, i ^ 1) for i in range(n_grp)])
 
     increment, hessian_probe, probe_low, panels_near = pl.pallas_call(
         functools.partial(solve_kernel, n_grp, n_tile),
@@ -485,11 +499,11 @@
         ],
         compiler_params=params,
         name="solve",
-    )(ext, pix, above, below, inputs[0], pltpu.with_memory_space_constraint(panels, pltpu.HBM))
-
-    column = [probe_low] + [
-        lax.ppermute(probe_low, "grp", [(i, (i + k) % n_grp) for i in range(n_grp)]) for k in range(1, n_grp)
-    ]
+    )(ext, pix, even, odd, inputs[0], pltpu.with_memory_space_constraint(panels, pltpu.HBM))
+
+    column = [
+        lax.ppermute(probe_low, "grp", [(i, i ^ k) for i in range(n_grp)]) for k in range(n_grp - 1, 0, -1)
+    ] + [probe_low]
     partial = pl.pallas_call(
         project_kernel,
         out_shape=jax.ShapeDtypeStruct((n_grp * n_tile, 1, 128), F32),

time: 43.3 us -> 43 us (level)
  waiting for transfers between devices: 7.11 us -> 6.53 us
  blocking collectives: 21.4 us -> 21.9 us
    ppermute x5, waiting for transfers between devices: 7.11 us -> 6.53 us  [the longest x3 3.21 us: on_device(): lax.ppermute(probe_low, 'grp', [(i, i ^ k) for i in range(n_grp)])]
    all_to_all x1, blocking collectives: 8.83 us -> 9.39 us  [on_device(): lax.all_to_all(partial, ('grp', 'tile'), split_axis=0, concat_axis=0, til...]
where the time goes in v5:
time: 43 us; the launch traced here: 42.8 us
  blocking collectives  21.9 us (51%)
  Pallas kernels  7.05 us (16%)
  starting transfers between devices  6.6 us (15%)
  waiting for transfers between devices  6.53 us (15%)
  between operations  0.66 us (2%)
    all_to_all x1, blocking collectives, on_device(): got = lax.all_to_all(slots, 'tile', split_axis=0, concat_axis=0, tiled=True)  12.5 us
    all_to_all x1, blocking collectives, on_device(): lax.all_to_all(partial, ('grp', 'tile'), split_axis=0, concat_axis=0, til...  9.39 us
    pallas_call x1, Pallas kernels, on_device(): pl.pallas_call(functools.partial(solve_kernel, n_grp, n_tile), out_shape=...  4.54 us
    ppermute x3, starting transfers between devices, on_device(): lax.ppermute(probe_low, 'grp', [(i, i ^ k) for i in range(n_grp)])  3.55 us
    ppermute x3, waiting for transfers between devices, on_device(): lax.ppermute(probe_low, 'grp', [(i, i ^ k) for i in range(n_grp)])  3.21 us
    ppermute x1, waiting for transfers between devices, on_device(): lax.ppermute(odd, 'grp', [(i, (i - 1 + 2 * (i % 2)) % n_grp) for i in ran...  2.39 us
    ppermute x1, starting transfers between devices, on_device(): even = lax.ppermute(even, 'grp', [(i, i ^ 1) for i in range(n_grp)])  1.56 us
    ppermute x1, starting transfers between devices, on_device(): lax.ppermute(odd, 'grp', [(i, (i - 1 + 2 * (i % 2)) % n_grp) for i in ran...  1.49 us
  transfers between devices with their start and end apart: 5, of which 5 were waited for; matrix products, arithmetic and copies ran while one was open for 0% of the time, Pallas kernels for 0%

profile of v5, /device:TPU:0, one launch (start us, length us, event | category | flops | bytes accessed | tf_op | source)
XLA Modules:
  0.0 42.8 jit_solution(13763844988897265306)
XLA Ops:
  0.6 1.1 %pack_tiles.1 = (bf16[8,48,128]{2,1,0:T(8,128)(2,1)S(1)}, f32[4,64,128]{2,1,0:T(8,128)S(1)}) custom-call(f32[2,64,128]{2,1,0:T(8,128)} %bv_hbm.1, f32[64,128]{1,0:T(8,128)} %refs_1_.1, f32[64,128]{1,0:T(8,128)} %refs_2_.1, f32[64,128]{1,0:T(8,128)} %refs_3_.1, f32[1,1,2,512]{3,2,1,0:T(2,128)} %refs_4_.1, f32[1,1,1,512]{3,2,1,0:T(1,128)} %refs_5_.1, ...), custom_call_target="tpu_custom_call" | custom-call | tf_op jit(solution)/shard_map/pack_tiles/pallas_call | solution.py:450
  1.8 12.5 %all_to_all.10.got_ref = bf16[8,48,128]{2,1,0:T(8,128)(2,1)S(1)} all-to-all(bf16[8,48,128]{2,1,0:T(8,128)(2,1)S(1)} %get-tuple-element.14), channel_id=1, replica_groups=mesh['grp'=4,'tile'=8] {'tile'}, dimensions={0} | all-to-all | bytes 196608 | tf_op jit(solution)/shard_map/all_to_all | solution.py:462
  14.3 0.2 pack_rows.1
  14.5 1.6 %collective-permute-start = (bf16[128,128]{1,0:T(8,128)(2,1)S(1)}, bf16[128,128]{1,0:T(8,128)(2,1)S(1)}, u32[]{:S(2)}, u32[]{:S(2)}) collective-permute-start(bf16[128,128]{1,0:T(8,128)(2,1)S(1)} %get-tuple-element.17), channel_id=1, source_target_pairs={{0,8},{8,0},{16,24},{24,16},{1,9},{9,1},{17,25},{25,17},{2,10},{10... | collective-permute-start | bytes 98312 | tf_op jit(solution)/shard_map/ppermute | solution.py:479
  16.1 1.5 %collective-permute-start.1 = (bf16[128,128]{1,0:T(8,128)(2,1)S(1)}, bf16[128,128]{1,0:T(8,128)(2,1)S(1)}, u32[]{:S(2)}, u32[]{:S(2)}) collective-permute-start(bf16[128,128]{1,0:T(8,128)(2,1)S(1)} %get-tuple-element.18), channel_id=1, source_target_pairs={{0,24},{8,16},{16,8},{24,0},{1,25},{9,17},{17,9},{25,1},{2,26},{10... | collective-permute-start | bytes 98312 | tf_op jit(solution)/shard_map/ppermute | solution.py:478
  17.5 0.9 %collective-permute-done.even_ref = bf16[128,128]{1,0:T(8,128)(2,1)S(1)} collective-permute-done((bf16[128,128]{1,0:T(8,128)(2,1)S(1)}, bf16[128,128]{1,0:T(8,128)(2,1)S(1)}, u32[]{:S(2)}, u32[]{:S(2)}) %collective-permute-start) | collective-permute-done | bytes 32800 | tf_op jit(solution)/shard_map/ppermute | solution.py:479
  18.5 2.4 %collective-permute-done.1.odd_ref = bf16[128,128]{1,0:T(8,128)(2,1)S(1)} collective-permute-done((bf16[128,128]{1,0:T(8,128)(2,1)S(1)}, bf16[128,128]{1,0:T(8,128)(2,1)S(1)}, u32[]{:S(2)}, u32[]{:S(2)}) %collective-permute-start.1) | collective-permute-done | bytes 32800 | tf_op jit(solution)/shard_map/ppermute | solution.py:478
  20.9 4.5 %solve.1 = (f32[2,64,128]{2,1,0:T(8,128)}, f32[64,128]{1,0:T(8,128)}, bf16[64,128]{1,0:T(8,128)(2,1)S(1)}, bf16[32,256,128]{2,1,0:T(8,128)(2,1)S(1)}) custom-call(f32[4,64,256]{2,1,0:T(8,128)S(1)} %get-tuple-element.15.ext_ref, f32[48,128]{1,0:T(8,128)S(1)} %get-tuple-element.16.pix_ref, bf16[128,128]{1,0:T(8,128)(2,1)S(1)} %collective-permute-done.even_ref, ...), custom_call_target="tpu_custom_call" | custom-call | tf_op jit(solution)/shard_map/solve/pallas_call | solution.py:481
  25.4 0.6 %collective-permute-start.4 = (bf16[64,128]{1,0:T(8,128)(2,1)S(1)}, bf16[64,128]{1,0:T(8,128)(2,1)S(1)}, u32[]{:S(2)}, u32[]{:S(2)}) collective-permute-start(bf16[64,128]{1,0:T(8,128)(2,1)S(1)} %get-tuple-element.22.refs_3_), channel_id=1, source_target_pairs={{0,8},{8,0},{16,24},{24,16},{1,9},{9,1},{17,25},{25,17},{2,10},{10... | collective-permute-start | bytes 49160 | tf_op jit(solution)/shard_map/ppermute | solution.py:505
  26.0 1.5 %collective-permute-start.3 = (bf16[64,128]{1,0:T(8,128)(2,1)S(1)}, bf16[64,128]{1,0:T(8,128)(2,1)S(1)}, u32[]{:S(2)}, u32[]{:S(2)}) collective-permute-start(bf16[64,128]{1,0:T(8,128)(2,1)S(1)} %get-tuple-element.22.refs_3_), channel_id=1, source_target_pairs={{0,16},{8,24},{16,0},{24,8},{1,17},{9,25},{17,1},{25,9},{2,18},{10... | collective-permute-start | bytes 49160 | tf_op jit(solution)/shard_map/ppermute | solution.py:505
  27.5 1.4 %collective-permute-start.2 = (bf16[64,128]{1,0:T(8,128)(2,1)S(1)}, bf16[64,128]{1,0:T(8,128)(2,1)S(1)}, u32[]{:S(2)}, u32[]{:S(2)}) collective-permute-start(bf16[64,128]{1,0:T(8,128)(2,1)S(1)} %get-tuple-element.22.refs_3_), channel_id=1, source_target_pairs={{0,24},{8,16},{16,8},{24,0},{1,25},{9,17},{17,9},{25,1},{2,26},{10... | collective-permute-start | bytes 49160 | tf_op jit(solution)/shard_map/ppermute | solution.py:505
  29.0 0.2 collective-permute-done.4.refs_2_
  29.2 0.5 %collective-permute-done.3.refs_1_ = bf16[64,128]{1,0:T(8,128)(2,1)S(1)} collective-permute-done((bf16[64,128]{1,0:T(8,128)(2,1)S(1)}, bf16[64,128]{1,0:T(8,128)(2,1)S(1)}, u32[]{:S(2)}, u32[]{:S(2)}) %collective-permute-start.3) | collective-permute-done | bytes 16416 | tf_op jit(solution)/shard_map/ppermute | solution.py:505
  29.8 2.4 %collective-permute-done.2.refs_0_ = bf16[64,128]{1,0:T(8,128)(2,1)S(1)} collective-permute-done((bf16[64,128]{1,0:T(8,128)(2,1)S(1)}, bf16[64,128]{1,0:T(8,128)(2,1)S(1)}, u32[]{:S(2)}, u32[]{:S(2)}) %collective-permute-start.2) | collective-permute-done | bytes 16416 | tf_op jit(solution)/shard_map/ppermute | solution.py:505
  32.2 0.7 %project.1 = f32[32,1,128]{2,1,0:T(1,128)S(1)} custom-call(bf16[32,256,128]{2,1,0:T(8,128)(2,1)S(1)} %get-tuple-element.21.panels_ref, bf16[64,128]{1,0:T(8,128)(2,1)S(1)} %collective-permute-done.2.refs_0_, bf16[64,128]{1,0:T(8,128)(2,1)S(1)} %collective-permute-done.3.refs_1_, bf16[64,128]{1,0:T(8,128)(2,1)S(1)} %collective-permute-done.4.refs_2_, ...), custom_call_target="tpu_custom_call" | custom-call | tf_op jit(solution)/shard_map/project/pallas_call | solution.py:507
  32.8 9.4 %all_to_all.11.lines_ref = f32[32,1,128]{2,1,0:T(1,128)S(1)} all-to-all(f32[32,1,128]{2,1,0:T(1,128)S(1)} %project.1), channel_id=1, replica_groups=mesh['grp'=4,'tile'=8] {'grp','tile'}, dimensions={0} | all-to-all | bytes 32768 | tf_op jit(solution)/shard_map/all_to_all | solution.py:516
  42.2 0.5 %add_lines.1 = f32[1,128]{1,0:T(1,128)} custom-call(f32[32,1,128]{2,1,0:T(1,128)S(1)} %all_to_all.11.lines_ref), custom_call_target="tpu_custom_call" | custom-call | tf_op jit(solution)/shard_map/add_lines/pallas_call | solution.py:517
Async XLA Ops:
  14.5 4.0 %collective-permute-start = (bf16[128,128]{1,0:T(8,128)(2,1)S(1)}, bf16[128,128]{1,0:T(8,128)(2,1)S(1)}, u32[]{:S(2)}, u32[]{:S(2)}) collective-permute-start(bf16[128,128]{1,0:T(8,128)(2,1)S(1)} %get-tuple-element.17), channel_id=1, source_target_pairs={{0,8},{8,0},{16,24},{24,16},{1,9},{9,1},{17,25},{25,17},{2,10},{10... | collective-permute-start | bytes 98312 | tf_op jit(solution)/shard_map/ppermute | solution.py:479
  16.1 4.8 %collective-permute-start.1 = (bf16[128,128]{1,0:T(8,128)(2,1)S(1)}, bf16[128,128]{1,0:T(8,128)(2,1)S(1)}, u32[]{:S(2)}, u32[]{:S(2)}) collective-permute-start(bf16[128,128]{1,0:T(8,128)(2,1)S(1)} %get-tuple-element.18), channel_id=1, source_target_pairs={{0,24},{8,16},{16,8},{24,0},{1,25},{9,17},{17,9},{25,1},{2,26},{10... | collective-permute-start | bytes 98312 | tf_op jit(solution)/shard_map/ppermute | solution.py:478
  25.4 3.8 %collective-permute-start.4 = (bf16[64,128]{1,0:T(8,128)(2,1)S(1)}, bf16[64,128]{1,0:T(8,128)(2,1)S(1)}, u32[]{:S(2)}, u32[]{:S(2)}) collective-permute-start(bf16[64,128]{1,0:T(8,128)(2,1)S(1)} %get-tuple-element.22.refs_3_), channel_id=1, source_target_pairs={{0,8},{8,0},{16,24},{24,16},{1,9},{9,1},{17,25},{25,17},{2,10},{10... | collective-permute-start | bytes 49160 | tf_op jit(solution)/shard_map/ppermute | solution.py:505
  26.0 3.7 %collective-permute-start.3 = (bf16[64,128]{1,0:T(8,128)(2,1)S(1)}, bf16[64,128]{1,0:T(8,128)(2,1)S(1)}, u32[]{:S(2)}, u32[]{:S(2)}) collective-permute-start(bf16[64,128]{1,0:T(8,128)(2,1)S(1)} %get-tuple-element.22.refs_3_), channel_id=1, source_target_pairs={{0,16},{8,24},{16,0},{24,8},{1,17},{9,25},{17,1},{25,9},{2,18},{10... | collective-permute-start | bytes 49160 | tf_op jit(solution)/shard_map/ppermute | solution.py:505
  27.5 4.6 %collective-permute-start.2 = (bf16[64,128]{1,0:T(8,128)(2,1)S(1)}, bf16[64,128]{1,0:T(8,128)(2,1)S(1)}, u32[]{:S(2)}, u32[]{:S(2)}) collective-permute-start(bf16[64,128]{1,0:T(8,128)(2,1)S(1)} %get-tuple-element.22.refs_3_), channel_id=1, source_target_pairs={{0,24},{8,16},{16,8},{24,0},{1,25},{9,17},{17,9},{25,1},{2,26},{10... | collective-permute-start | bytes 49160 | tf_op jit(solution)/shard_map/ppermute | solution.py:505

commit v6 on v5

--- a/solution.py
+++ b/solution.py
@@ -164,11 +164,16 @@
 
 
 def solve_kernel(
-    n_grp, n_tile, ext_ref, pix_ref, even_ref, odd_ref, bv_hbm, panels_hbm,
+    n_grp, n_tile, ext_ref, pix_ref, odd_ref, even_ref, bv_hbm, panels_hbm,
     inc_ref, hess_ref, low_ref, panels_ref,
     plane_ref, coef_ref, src_ref, w_ref, nat_ref, bv_ref, sems,
 ):
-    copies = fetch((bv_hbm, panels_hbm), (bv_ref, panels_ref), sems)
+    size = panels_ref.shape[2]
+    copies = fetch(
+        [bv_hbm] + [panels_hbm.at[:, pl.ds(i * size, size), :] for i in range(n_grp)],
+        [bv_ref] + [panels_ref.at[:, i] for i in range(n_grp)],
+        sems,
+    )
     g = lax.axis_index("grp")
     t = lax.axis_index("tile")
     rows = ext_ref.shape[1]
@@ -404,16 +409,29 @@
     low_ref[...] = hess.astype(BF16)
 
 
+def distances(n_grp):
+    return [0] + list(range(2, n_grp)) + [1]
+
+
+def project_block(panels_ref, probe_ref, k, distance):
+    count, n_grp, rows, columns = panels_ref.shape
+    product = panels_ref[k, lax.axis_index("grp") ^ distance].astype(F32) * probe_ref[...].astype(F32)
+    return jnp.sum(product.reshape(-1, 8, columns), axis=0)
+
+
 def project_kernel(panels_ref, *refs):
-    blocks, out_ref, probe_ref = refs[:-2], refs[-2], refs[-1]
-    count = panels_ref.shape[0]
-    for k, block in enumerate(blocks):
-        probe_ref[lax.axis_index("grp") ^ (len(blocks) - 1 - k)] = block[...]
-    probe = probe_ref[...].astype(F32).reshape(panels_ref.shape[1:])
+    blocks, sums_ref = refs[:-1], refs[-1]
+    order = distances(panels_ref.shape[1])
+    for k in range(panels_ref.shape[0]):
+        sums_ref[k] = sum(project_block(panels_ref, block, k, i) for i, block in zip(order, blocks))
+
+
+def project_last_kernel(panels_ref, block_ref, sums_ref, out_ref):
+    count, n_grp = panels_ref.shape[:2]
     sums = []
     for k in range(count):
-        product = panels_ref[k].astype(F32) * probe
-        sums.append(jnp.sum(product, axis=0, keepdims=True))
+        total = sums_ref[k] + project_block(panels_ref, block_ref, k, distances(n_grp)[-1])
+        sums.append(jnp.sum(total, axis=0, keepdims=True))
     sums.append(jnp.zeros((128 - count, 128), F32))
     table = jnp.concatenate(sums, axis=0)
     line = lax.dot_general(
@@ -475,8 +493,8 @@
         compiler_params=params,
         name="pack_rows",
     )(fields, got)
+    even = lax.ppermute(even, "grp", [(i, i ^ 1) for i in range(n_grp)])
     odd = lax.ppermute(odd, "grp", [(i, (i - 1 + 2 * (i % 2)) % n_grp) for i in range(n_grp)])
-    even = lax.ppermute(even, "grp", [(i, i ^ 1) for i in range(n_grp)])
 
     increment, hessian_probe, probe_low, panels_near = pl.pallas_call(
         functools.partial(solve_kernel, n_grp, n_tile),
@@ -484,7 +502,7 @@
             jax.ShapeDtypeStruct((2, rows, columns), F32),
             jax.ShapeDtypeStruct((rows, columns), F32),
             jax.ShapeDtypeStruct((rows, columns), BF16),
-            jax.ShapeDtypeStruct(panels.shape, BF16),
+            jax.ShapeDtypeStruct((panels.shape[0], n_grp, rows, columns), BF16),
         ),
         in_specs=vmem(4) + [pl.BlockSpec(memory_space=pltpu.HBM)] * 2,
         out_specs=tuple(vmem(4)),
@@ -495,24 +513,34 @@
             pltpu.VMEM((3, 2, span, 256), F32),
             pltpu.VMEM((2, 2, span, 128), F32),
             pltpu.VMEM(base_velocity.shape, F32),
-            pltpu.SemaphoreType.DMA((2,)),
+            pltpu.SemaphoreType.DMA((1 + n_grp,)),
         ],
         compiler_params=params,
         name="solve",
-    )(ext, pix, even, odd, inputs[0], pltpu.with_memory_space_constraint(panels, pltpu.HBM))
-
-    column = [
-        lax.ppermute(probe_low, "grp", [(i, i ^ k) for i in range(n_grp)]) for k in range(n_grp - 1, 0, -1)
-    ] + [probe_low]
+    )(ext, pix, odd, even, inputs[0], pltpu.with_memory_space_constraint(panels, pltpu.HBM))
+
+    column = [probe_low] + [
+        lax.ppermute(probe_low, "grp", [(i, i ^ k) for i in range(n_grp)]) for k in distances(n_grp)[1:]
+    ]
+    sums = pl.pallas_call(
+        project_kernel,
+        out_shape=jax.ShapeDtypeStruct((panels.shape[0], 8, 128), F32),
+        in_specs=vmem(n_grp),
+        out_specs=pl.BlockSpec(memory_space=pltpu.VMEM),
+        compiler_params=params,
+        cost_estimate=pl.CostEstimate(
+            flops=2 * panels.size * (n_grp - 1) // n_grp, bytes_accessed=2 * panels.size, transcendentals=0
+        ),
+        name="project",
+    )(panels_near, *column[:-1])
     partial = pl.pallas_call(
-        project_kernel,
+        project_last_kernel,
         out_shape=jax.ShapeDtypeStruct((n_grp * n_tile, 1, 128), F32),
-        in_specs=vmem(1 + n_grp),
+        in_specs=vmem(3),
         out_specs=pl.BlockSpec(memory_space=pltpu.VMEM),
-        scratch_shapes=[pltpu.VMEM((n_grp, rows, columns), BF16)],
         compiler_params=params,
-        name="project",
-    )(panels_near, *column)
+        name="project_last",
+    )(panels_near, column[-1], sums)
     everyone = lax.all_to_all(partial, ("grp", "tile"), split_axis=0, concat_axis=0, tiled=True)
     coefficients = pl.pallas_call(
         add_lines_kernel,

time: 43 us -> 41.8 us (0.972)
  waiting for transfers between devices: 6.53 us -> 5.29 us
    ppermute x3, waiting for transfers between devices: 3.21 us -> 1.91 us  [on_device(): lax.ppermute(probe_low, 'grp', [(i, i ^ k) for i in range(n_grp)])]
    ppermute x1, starting transfers between devices: 1.49 us -> 2.51 us  [on_device(): lax.ppermute(odd, 'grp', [(i, (i - 1 + 2 * (i % 2)) % n_grp) for i in ran...]
    ppermute x1, starting transfers between devices: 1.56 us -> 0.54 us  [on_device(): even = lax.ppermute(even, 'grp', [(i, i ^ 1) for i in range(n_grp)])]
  transfers between devices with their start and end apart: 5 -> 5, of which waited for: 5 -> 5; matrix products, arithmetic and copies ran while one was open for 0% -> 0% of each run, Pallas kernels for 0% -> 1%
where the time goes in v6:
time: 41.8 us; the launch traced here: 41.6 us
  blocking collectives  21.9 us (52%)
  Pallas kernels  7.1 us (17%)
  starting transfers between devices  6.6 us (16%)
  waiting for transfers between devices  5.29 us (13%)
  between operations  0.66 us (2%)
    all_to_all x1, blocking collectives, on_device(): got = lax.all_to_all(slots, 'tile', split_axis=0, concat_axis=0, tiled=True)  12.5 us
    all_to_all x1, blocking collectives, on_device(): lax.all_to_all(partial, ('grp', 'tile'), split_axis=0, concat_axis=0, til...  9.39 us
    pallas_call x1, Pallas kernels, on_device(): pl.pallas_call(functools.partial(solve_kernel, n_grp, n_tile), out_shape=...  4.58 us
    ppermute x3, starting transfers between devices, on_device(): lax.ppermute(probe_low, 'grp', [(i, i ^ k) for i in range(n_grp)])  3.55 us
    ppermute x1, starting transfers between devices, on_device(): lax.ppermute(odd, 'grp', [(i, (i - 1 + 2 * (i % 2)) % n_grp) for i in ran...  2.51 us
    ppermute x1, waiting for transfers between devices, on_device(): lax.ppermute(odd, 'grp', [(i, (i - 1 + 2 * (i % 2)) % n_grp) for i in ran...  2.06 us
    ppermute x3, waiting for transfers between devices, on_device(): lax.ppermute(probe_low, 'grp', [(i, i ^ k) for i in range(n_grp)])  1.91 us
    ppermute x1, waiting for transfers between devices, on_device(): even = lax.ppermute(even, 'grp', [(i, i ^ 1) for i in range(n_grp)])  1.32 us
  transfers between devices with their start and end apart: 5, of which 5 were waited for; matrix products, arithmetic and copies ran while one was open for 0% of the time, Pallas kernels for 1%

profile of v6, /device:TPU:0, one launch (start us, length us, event | category | flops | bytes accessed | tf_op | source)
XLA Modules:
  0.0 41.6 jit_solution(14872604249189311775)
XLA Ops:
  0.6 1.1 %pack_tiles.1 = (bf16[8,48,128]{2,1,0:T(8,128)(2,1)S(1)}, f32[4,64,128]{2,1,0:T(8,128)S(1)}) custom-call(f32[2,64,128]{2,1,0:T(8,128)} %bv_hbm.1, f32[64,128]{1,0:T(8,128)} %refs_1_.1, f32[64,128]{1,0:T(8,128)} %refs_2_.1, f32[64,128]{1,0:T(8,128)} %refs_3_.1, f32[1,1,2,512]{3,2,1,0:T(2,128)} %refs_4_.1, f32[1,1,1,512]{3,2,1,0:T(1,128)} %refs_5_.1, ...), custom_call_target="tpu_custom_call" | custom-call | tf_op jit(solution)/shard_map/pack_tiles/pallas_call | solution.py:468
  1.8 12.5 %all_to_all.10.got_ref = bf16[8,48,128]{2,1,0:T(8,128)(2,1)S(1)} all-to-all(bf16[8,48,128]{2,1,0:T(8,128)(2,1)S(1)} %get-tuple-element.14), channel_id=1, replica_groups=mesh['grp'=4,'tile'=8] {'tile'}, dimensions={0} | all-to-all | bytes 196608 | tf_op jit(solution)/shard_map/all_to_all | solution.py:480
  14.3 0.2 pack_rows.1
  14.5 2.5 %collective-permute-start = (bf16[128,128]{1,0:T(8,128)(2,1)S(1)}, bf16[128,128]{1,0:T(8,128)(2,1)S(1)}, u32[]{:S(2)}, u32[]{:S(2)}) collective-permute-start(bf16[128,128]{1,0:T(8,128)(2,1)S(1)} %get-tuple-element.17), channel_id=1, source_target_pairs={{0,24},{8,16},{16,8},{24,0},{1,25},{9,17},{17,9},{25,1},{2,26},{10... | collective-permute-start | bytes 98312 | tf_op jit(solution)/shard_map/ppermute | solution.py:497
  17.0 0.5 %collective-permute-start.1 = (bf16[128,128]{1,0:T(8,128)(2,1)S(1)}, bf16[128,128]{1,0:T(8,128)(2,1)S(1)}, u32[]{:S(2)}, u32[]{:S(2)}) collective-permute-start(bf16[128,128]{1,0:T(8,128)(2,1)S(1)} %get-tuple-element.18), channel_id=1, source_target_pairs={{0,8},{8,0},{16,24},{24,16},{1,9},{9,1},{17,25},{25,17},{2,10},{10... | collective-permute-start | bytes 98312 | tf_op jit(solution)/shard_map/ppermute | solution.py:496
  17.5 2.1 %collective-permute-done.odd_ref = bf16[128,128]{1,0:T(8,128)(2,1)S(1)} collective-permute-done((bf16[128,128]{1,0:T(8,128)(2,1)S(1)}, bf16[128,128]{1,0:T(8,128)(2,1)S(1)}, u32[]{:S(2)}, u32[]{:S(2)}) %collective-permute-start) | collective-permute-done | bytes 32800 | tf_op jit(solution)/shard_map/ppermute | solution.py:497
  19.6 1.3 %collective-permute-done.1.even_ref = bf16[128,128]{1,0:T(8,128)(2,1)S(1)} collective-permute-done((bf16[128,128]{1,0:T(8,128)(2,1)S(1)}, bf16[128,128]{1,0:T(8,128)(2,1)S(1)}, u32[]{:S(2)}, u32[]{:S(2)}) %collective-permute-start.1) | collective-permute-done | bytes 32800 | tf_op jit(solution)/shard_map/ppermute | solution.py:496
  20.9 4.6 %solve.1 = (f32[2,64,128]{2,1,0:T(8,128)}, f32[64,128]{1,0:T(8,128)}, bf16[64,128]{1,0:T(8,128)(2,1)S(1)}, bf16[32,4,64,128]{3,2,1,0:T(8,128)(2,1)S(1)}) custom-call(f32[4,64,256]{2,1,0:T(8,128)S(1)} %get-tuple-element.15.ext_ref, f32[48,128]{1,0:T(8,128)S(1)} %get-tuple-element.16.pix_ref, bf16[128,128]{1,0:T(8,128)(2,1)S(1)} %collective-permute-done.odd_ref, ...), custom_call_target="tpu_custom_call" | custom-call | tf_op jit(solution)/shard_map/solve/pallas_call | solution.py:499
  25.5 1.0 %collective-permute-start.4 = (bf16[64,128]{1,0:T(8,128)(2,1)S(1)}, bf16[64,128]{1,0:T(8,128)(2,1)S(1)}, u32[]{:S(2)}, u32[]{:S(2)}) collective-permute-start(bf16[64,128]{1,0:T(8,128)(2,1)S(1)} %get-tuple-element.22.refs_0_), channel_id=1, source_target_pairs={{0,24},{8,16},{16,8},{24,0},{1,25},{9,17},{17,9},{25,1},{2,26},{10... | collective-permute-start | bytes 49160 | tf_op jit(solution)/shard_map/ppermute | solution.py:523
  26.5 1.1 %collective-permute-start.3 = (bf16[64,128]{1,0:T(8,128)(2,1)S(1)}, bf16[64,128]{1,0:T(8,128)(2,1)S(1)}, u32[]{:S(2)}, u32[]{:S(2)}) collective-permute-start(bf16[64,128]{1,0:T(8,128)(2,1)S(1)} %get-tuple-element.22.refs_0_), channel_id=1, source_target_pairs={{0,16},{8,24},{16,0},{24,8},{1,17},{9,25},{17,1},{25,9},{2,18},{10... | collective-permute-start | bytes 49160 | tf_op jit(solution)/shard_map/ppermute | solution.py:523
  27.6 1.5 %collective-permute-start.2 = (bf16[64,128]{1,0:T(8,128)(2,1)S(1)}, bf16[64,128]{1,0:T(8,128)(2,1)S(1)}, u32[]{:S(2)}, u32[]{:S(2)}) collective-permute-start(bf16[64,128]{1,0:T(8,128)(2,1)S(1)} %get-tuple-element.22.refs_0_), channel_id=1, source_target_pairs={{0,8},{8,0},{16,24},{24,16},{1,9},{9,1},{17,25},{25,17},{2,10},{10... | collective-permute-start | bytes 49160 | tf_op jit(solution)/shard_map/ppermute | solution.py:523
  29.1 1.2 %collective-permute-done.4.refs_2_ = bf16[64,128]{1,0:T(8,128)(2,1)S(1)} collective-permute-done((bf16[64,128]{1,0:T(8,128)(2,1)S(1)}, bf16[64,128]{1,0:T(8,128)(2,1)S(1)}, u32[]{:S(2)}, u32[]{:S(2)}) %collective-permute-start.4) | collective-permute-done | bytes 16416 | tf_op jit(solution)/shard_map/ppermute | solution.py:523
  30.2 0.2 collective-permute-done.3.refs_1_
  30.4 0.3 project.1.sums_ref
  30.7 0.6 %collective-permute-done.2.block_ref = bf16[64,128]{1,0:T(8,128)(2,1)S(1)} collective-permute-done((bf16[64,128]{1,0:T(8,128)(2,1)S(1)}, bf16[64,128]{1,0:T(8,128)(2,1)S(1)}, u32[]{:S(2)}, u32[]{:S(2)}) %collective-permute-start.2) | collective-permute-done | bytes 16416 | tf_op jit(solution)/shard_map/ppermute | solution.py:523
  31.3 0.3 project_last.1
  31.7 9.4 %all_to_all.11.lines_ref = f32[32,1,128]{2,1,0:T(1,128)S(1)} all-to-all(f32[32,1,128]{2,1,0:T(1,128)S(1)} %project_last.1), channel_id=1, replica_groups=mesh['grp'=4,'tile'=8] {'grp','tile'}, dimensions={0} | all-to-all | bytes 32768 | tf_op jit(solution)/shard_map/all_to_all | solution.py:544
  41.0 0.5 %add_lines.1 = f32[1,128]{1,0:T(1,128)} custom-call(f32[32,1,128]{2,1,0:T(1,128)S(1)} %all_to_all.11.lines_ref), custom_call_target="tpu_custom_call" | custom-call | tf_op jit(solution)/shard_map/add_lines/pallas_call | solution.py:545
Async XLA Ops:
  14.5 5.1 %collective-permute-start = (bf16[128,128]{1,0:T(8,128)(2,1)S(1)}, bf16[128,128]{1,0:T(8,128)(2,1)S(1)}, u32[]{:S(2)}, u32[]{:S(2)}) collective-permute-start(bf16[128,128]{1,0:T(8,128)(2,1)S(1)} %get-tuple-element.17), channel_id=1, source_target_pairs={{0,24},{8,16},{16,8},{24,0},{1,25},{9,17},{17,9},{25,1},{2,26},{10... | collective-permute-start | bytes 98312 | tf_op jit(solution)/shard_map/ppermute | solution.py:497
  17.0 3.9 %collective-permute-start.1 = (bf16[128,128]{1,0:T(8,128)(2,1)S(1)}, bf16[128,128]{1,0:T(8,128)(2,1)S(1)}, u32[]{:S(2)}, u32[]{:S(2)}) collective-permute-start(bf16[128,128]{1,0:T(8,128)(2,1)S(1)} %get-tuple-element.18), channel_id=1, source_target_pairs={{0,8},{8,0},{16,24},{24,16},{1,9},{9,1},{17,25},{25,17},{2,10},{10... | collective-permute-start | bytes 98312 | tf_op jit(solution)/shard_map/ppermute | solution.py:496
  25.5 4.7 %collective-permute-start.4 = (bf16[64,128]{1,0:T(8,128)(2,1)S(1)}, bf16[64,128]{1,0:T(8,128)(2,1)S(1)}, u32[]{:S(2)}, u32[]{:S(2)}) collective-permute-start(bf16[64,128]{1,0:T(8,128)(2,1)S(1)} %get-tuple-element.22.refs_0_), channel_id=1, source_target_pairs={{0,24},{8,16},{16,8},{24,0},{1,25},{9,17},{17,9},{25,1},{2,26},{10... | collective-permute-start | bytes 49160 | tf_op jit(solution)/shard_map/ppermute | solution.py:523
  26.5 3.9 %collective-permute-start.3 = (bf16[64,128]{1,0:T(8,128)(2,1)S(1)}, bf16[64,128]{1,0:T(8,128)(2,1)S(1)}, u32[]{:S(2)}, u32[]{:S(2)}) collective-permute-start(bf16[64,128]{1,0:T(8,128)(2,1)S(1)} %get-tuple-element.22.refs_0_), channel_id=1, source_target_pairs={{0,16},{8,24},{16,0},{24,8},{1,17},{9,25},{17,1},{25,9},{2,18},{10... | collective-permute-start | bytes 49160 | tf_op jit(solution)/shard_map/ppermute | solution.py:523
  27.6 3.7 %collective-permute-start.2 = (bf16[64,128]{1,0:T(8,128)(2,1)S(1)}, bf16[64,128]{1,0:T(8,128)(2,1)S(1)}, u32[]{:S(2)}, u32[]{:S(2)}) collective-permute-start(bf16[64,128]{1,0:T(8,128)(2,1)S(1)} %get-tuple-element.22.refs_0_), channel_id=1, source_target_pairs={{0,8},{8,0},{16,24},{24,16},{1,9},{9,1},{17,25},{25,17},{2,10},{10... | collective-permute-start | bytes 49160 | tf_op jit(solution)/shard_map/ppermute | solution.py:523

commit v7 on v6

--- a/solution.py
+++ b/solution.py
@@ -165,8 +165,8 @@
 
 def solve_kernel(
     n_grp, n_tile, ext_ref, pix_ref, odd_ref, even_ref, bv_hbm, panels_hbm,
-    inc_ref, hess_ref, low_ref, panels_ref,
-    plane_ref, coef_ref, src_ref, w_ref, nat_ref, bv_ref, sems,
+    inc_hbm, hess_ref, low_ref, panels_ref,
+    plane_ref, coef_ref, src_ref, w_ref, nat_ref, bv_ref, inc_ref, sems, inc_sem,
 ):
     size = panels_ref.shape[2]
     copies = fetch(
@@ -323,6 +323,7 @@
         def _():
             for c in range(2):
                 inc_ref[c] = nat_ref[c, 0, HALO : HALO + rows, :]
+            pltpu.make_async_copy(inc_ref, inc_hbm, inc_sem).start()
             misfit()
 
         return carry
@@ -404,6 +405,7 @@
     lax.fori_loop(0, 2, solve, 0)
     for copy in copies:
         copy.wait()
+    pltpu.make_async_copy(inc_ref, inc_hbm, inc_sem).wait()
     hess = -(bv_ref[0] * nat_ref[0, 0, HALO : HALO + rows, :] + bv_ref[1] * nat_ref[1, 0, HALO : HALO + rows, :])
     hess_ref[...] = hess
     low_ref[...] = hess.astype(BF16)
@@ -419,11 +421,14 @@
     return jnp.sum(product.reshape(-1, 8, columns), axis=0)
 
 
-def project_kernel(panels_ref, *refs):
-    blocks, sums_ref = refs[:-1], refs[-1]
+def project_kernel(panels_ref, hess_ref, *refs):
+    blocks, (sums_ref, hess_hbm, sem) = refs[:-3], refs[-3:]
+    copy = pltpu.make_async_copy(hess_ref, hess_hbm, sem)
+    copy.start()
     order = distances(panels_ref.shape[1])
     for k in range(panels_ref.shape[0]):
         sums_ref[k] = sum(project_block(panels_ref, block, k, i) for i, block in zip(order, blocks))
+    copy.wait()
 
 
 def project_last_kernel(panels_ref, block_ref, sums_ref, out_ref):
@@ -496,7 +501,7 @@
     even = lax.ppermute(even, "grp", [(i, i ^ 1) for i in range(n_grp)])
     odd = lax.ppermute(odd, "grp", [(i, (i - 1 + 2 * (i % 2)) % n_grp) for i in range(n_grp)])
 
-    increment, hessian_probe, probe_low, panels_near = pl.pallas_call(
+    increment, hess, probe_low, panels_near = pl.pallas_call(
         functools.partial(solve_kernel, n_grp, n_tile),
         out_shape=(
             jax.ShapeDtypeStruct((2, rows, columns), F32),
@@ -505,7 +510,7 @@
             jax.ShapeDtypeStruct((panels.shape[0], n_grp, rows, columns), BF16),
         ),
         in_specs=vmem(4) + [pl.BlockSpec(memory_space=pltpu.HBM)] * 2,
-        out_specs=tuple(vmem(4)),
+        out_specs=tuple([pl.BlockSpec(memory_space=pltpu.HBM)] + vmem(3)),
         scratch_shapes=[
             pltpu.VMEM((FIELDS, 2, span, 128), F32),
             pltpu.VMEM((10, span, 256), F32),
@@ -513,7 +518,9 @@
             pltpu.VMEM((3, 2, span, 256), F32),
             pltpu.VMEM((2, 2, span, 128), F32),
             pltpu.VMEM(base_velocity.shape, F32),
+            pltpu.VMEM(base_velocity.shape, F32),
             pltpu.SemaphoreType.DMA((1 + n_grp,)),
+            pltpu.SemaphoreType.DMA,
         ],
         compiler_params=params,
         name="solve",
@@ -522,17 +529,21 @@
     column = [probe_low] + [
         lax.ppermute(probe_low, "grp", [(i, i ^ k) for i in range(n_grp)]) for k in distances(n_grp)[1:]
     ]
-    sums = pl.pallas_call(
+    sums, hessian_probe = pl.pallas_call(
         project_kernel,
-        out_shape=jax.ShapeDtypeStruct((panels.shape[0], 8, 128), F32),
-        in_specs=vmem(n_grp),
-        out_specs=pl.BlockSpec(memory_space=pltpu.VMEM),
+        out_shape=(
+            jax.ShapeDtypeStruct((panels.shape[0], 8, 128), F32),
+            jax.ShapeDtypeStruct((rows, columns), F32),
+        ),
+        in_specs=vmem(1 + n_grp),
+        out_specs=(pl.BlockSpec(memory_space=pltpu.VMEM), pl.BlockSpec(memory_space=pltpu.HBM)),
+        scratch_shapes=[pltpu.SemaphoreType.DMA],
         compiler_params=params,
         cost_estimate=pl.CostEstimate(
             flops=2 * panels.size * (n_grp - 1) // n_grp, bytes_accessed=2 * panels.size, transcendentals=0
         ),
         name="project",
-    )(panels_near, *column[:-1])
+    )(panels_near, hess, *column[:-1])
     partial = pl.pallas_call(
         project_last_kernel,
         out_shape=jax.ShapeDtypeStruct((n_grp * n_tile, 1, 128), F32),

time: 41.8 us -> 41.3 us (0.988)
    pallas_call x1, Pallas kernels: 4.58 us -> 3.96 us  [on_device(): pl.pallas_call(functools.partial(solve_kernel, n_grp, n_tile), out_shape=...]
  transfers between devices with their start and end apart: 5 -> 5, of which waited for: 5 -> 5; matrix products, arithmetic and copies ran while one was open for 0% -> 0% of each run, Pallas kernels for 1% -> 2%
where the time goes in v7:
time: 41.3 us; the launch traced here: 41.1 us
  blocking collectives  22 us (53%)
  Pallas kernels  6.77 us (16%)
  starting transfers between devices  6.6 us (16%)
  waiting for transfers between devices  4.99 us (12%)
  between operations  0.67 us (2%)
    all_to_all x1, blocking collectives, on_device(): got = lax.all_to_all(slots, 'tile', split_axis=0, concat_axis=0, tiled=True)  12.5 us
    all_to_all x1, blocking collectives, on_device(): lax.all_to_all(partial, ('grp', 'tile'), split_axis=0, concat_axis=0, til...  9.48 us
    pallas_call x1, Pallas kernels, on_device(): pl.pallas_call(functools.partial(solve_kernel, n_grp, n_tile), out_shape=...  3.96 us
    ppermute x3, starting transfers between devices, on_device(): lax.ppermute(probe_low, 'grp', [(i, i ^ k) for i in range(n_grp)])  3.55 us
    ppermute x1, starting transfers between devices, on_device(): lax.ppermute(odd, 'grp', [(i, (i - 1 + 2 * (i % 2)) % n_grp) for i in ran...  2.51 us
    ppermute x1, waiting for transfers between devices, on_device(): lax.ppermute(odd, 'grp', [(i, (i - 1 + 2 * (i % 2)) % n_grp) for i in ran...  2.06 us
    ppermute x3, waiting for transfers between devices, on_device(): lax.ppermute(probe_low, 'grp', [(i, i ^ k) for i in range(n_grp)])  1.61 us
    ppermute x1, waiting for transfers between devices, on_device(): even = lax.ppermute(even, 'grp', [(i, i ^ 1) for i in range(n_grp)])  1.32 us
  transfers between devices with their start and end apart: 5, of which 5 were waited for; matrix products, arithmetic and copies ran while one was open for 0% of the time, Pallas kernels for 2%

profile of v7, /device:TPU:0, one launch (start us, length us, event | category | flops | bytes accessed | tf_op | source)
XLA Modules:
  0.0 41.1 jit_solution(16794557676907791094)
XLA Ops:
  0.6 1.1 %pack_tiles.1 = (bf16[8,48,128]{2,1,0:T(8,128)(2,1)S(1)}, f32[4,64,128]{2,1,0:T(8,128)S(1)}) custom-call(f32[2,64,128]{2,1,0:T(8,128)} %bv_hbm.1, f32[64,128]{1,0:T(8,128)} %refs_1_.1, f32[64,128]{1,0:T(8,128)} %refs_2_.1, f32[64,128]{1,0:T(8,128)} %refs_3_.1, f32[1,1,2,512]{3,2,1,0:T(2,128)} %refs_4_.1, f32[1,1,1,512]{3,2,1,0:T(1,128)} %refs_5_.1, ...), custom_call_target="tpu_custom_call" | custom-call | tf_op jit(solution)/shard_map/pack_tiles/pallas_call | solution.py:473
  1.8 12.5 %all_to_all.10.got_ref = bf16[8,48,128]{2,1,0:T(8,128)(2,1)S(1)} all-to-all(bf16[8,48,128]{2,1,0:T(8,128)(2,1)S(1)} %get-tuple-element.16), channel_id=1, replica_groups=mesh['grp'=4,'tile'=8] {'tile'}, dimensions={0} | all-to-all | bytes 196608 | tf_op jit(solution)/shard_map/all_to_all | solution.py:485
  14.3 0.2 pack_rows.1
  14.5 2.5 %collective-permute-start = (bf16[128,128]{1,0:T(8,128)(2,1)S(1)}, bf16[128,128]{1,0:T(8,128)(2,1)S(1)}, u32[]{:S(2)}, u32[]{:S(2)}) collective-permute-start(bf16[128,128]{1,0:T(8,128)(2,1)S(1)} %get-tuple-element.19), channel_id=1, source_target_pairs={{0,24},{8,16},{16,8},{24,0},{1,25},{9,17},{17,9},{25,1},{2,26},{10... | collective-permute-start | bytes 98312 | tf_op jit(solution)/shard_map/ppermute | solution.py:502
  17.0 0.5 %collective-permute-start.1 = (bf16[128,128]{1,0:T(8,128)(2,1)S(1)}, bf16[128,128]{1,0:T(8,128)(2,1)S(1)}, u32[]{:S(2)}, u32[]{:S(2)}) collective-permute-start(bf16[128,128]{1,0:T(8,128)(2,1)S(1)} %get-tuple-element.20), channel_id=1, source_target_pairs={{0,8},{8,0},{16,24},{24,16},{1,9},{9,1},{17,25},{25,17},{2,10},{10... | collective-permute-start | bytes 98312 | tf_op jit(solution)/shard_map/ppermute | solution.py:501
  17.5 2.1 %collective-permute-done.odd_ref = bf16[128,128]{1,0:T(8,128)(2,1)S(1)} collective-permute-done((bf16[128,128]{1,0:T(8,128)(2,1)S(1)}, bf16[128,128]{1,0:T(8,128)(2,1)S(1)}, u32[]{:S(2)}, u32[]{:S(2)}) %collective-permute-start) | collective-permute-done | bytes 32800 | tf_op jit(solution)/shard_map/ppermute | solution.py:502
  19.6 1.3 %collective-permute-done.1.even_ref = bf16[128,128]{1,0:T(8,128)(2,1)S(1)} collective-permute-done((bf16[128,128]{1,0:T(8,128)(2,1)S(1)}, bf16[128,128]{1,0:T(8,128)(2,1)S(1)}, u32[]{:S(2)}, u32[]{:S(2)}) %collective-permute-start.1) | collective-permute-done | bytes 32800 | tf_op jit(solution)/shard_map/ppermute | solution.py:501
  20.9 4.0 %solve.1 = (f32[2,64,128]{2,1,0:T(8,128)}, f32[64,128]{1,0:T(8,128)S(1)}, bf16[64,128]{1,0:T(8,128)(2,1)S(1)}, bf16[32,4,64,128]{3,2,1,0:T(8,128)(2,1)S(1)}) custom-call(f32[4,64,256]{2,1,0:T(8,128)S(1)} %get-tuple-element.17.ext_ref, f32[48,128]{1,0:T(8,128)S(1)} %get-tuple-element.18.pix_ref, bf16[128,128]{1,0:T(8,128)(2,1)S(1)} %collective-permute-done.odd_ref, ...), custom_call_target="tpu_custom_call" | custom-call | tf_op jit(solution)/shard_map/solve/pallas_call | solution.py:504
  24.9 1.0 %collective-permute-start.3 = (bf16[64,128]{1,0:T(8,128)(2,1)S(1)}, bf16[64,128]{1,0:T(8,128)(2,1)S(1)}, u32[]{:S(2)}, u32[]{:S(2)}) collective-permute-start(bf16[64,128]{1,0:T(8,128)(2,1)S(1)} %get-tuple-element.24.refs_0_), channel_id=1, source_target_pairs={{0,24},{8,16},{16,8},{24,0},{1,25},{9,17},{17,9},{25,1},{2,26},{10... | collective-permute-start | bytes 49160 | tf_op jit(solution)/shard_map/ppermute | solution.py:530
  25.9 1.1 %collective-permute-start.2 = (bf16[64,128]{1,0:T(8,128)(2,1)S(1)}, bf16[64,128]{1,0:T(8,128)(2,1)S(1)}, u32[]{:S(2)}, u32[]{:S(2)}) collective-permute-start(bf16[64,128]{1,0:T(8,128)(2,1)S(1)} %get-tuple-element.24.refs_0_), channel_id=1, source_target_pairs={{0,16},{8,24},{16,0},{24,8},{1,17},{9,25},{17,1},{25,9},{2,18},{10... | collective-permute-start | bytes 49160 | tf_op jit(solution)/shard_map/ppermute | solution.py:530
  27.0 1.5 %collective-permute-start.4 = (bf16[64,128]{1,0:T(8,128)(2,1)S(1)}, bf16[64,128]{1,0:T(8,128)(2,1)S(1)}, u32[]{:S(2)}, u32[]{:S(2)}) collective-permute-start(bf16[64,128]{1,0:T(8,128)(2,1)S(1)} %get-tuple-element.24.refs_0_), channel_id=1, source_target_pairs={{0,8},{8,0},{16,24},{24,16},{1,9},{9,1},{17,25},{25,17},{2,10},{10... | collective-permute-start | bytes 49160 | tf_op jit(solution)/shard_map/ppermute | solution.py:530
  28.5 1.2 %collective-permute-done.3.refs_2_ = bf16[64,128]{1,0:T(8,128)(2,1)S(1)} collective-permute-done((bf16[64,128]{1,0:T(8,128)(2,1)S(1)}, bf16[64,128]{1,0:T(8,128)(2,1)S(1)}, u32[]{:S(2)}, u32[]{:S(2)}) %collective-permute-start.3) | collective-permute-done | bytes 16416 | tf_op jit(solution)/shard_map/ppermute | solution.py:530
  29.6 0.2 collective-permute-done.2.refs_1_
  29.8 0.6 %project.1 = (f32[32,8,128]{2,1,0:T(8,128)S(1)}, f32[64,128]{1,0:T(8,128)}) custom-call(bf16[32,4,64,128]{3,2,1,0:T(8,128)(2,1)S(1)} %get-tuple-element.22.panels_ref, f32[64,128]{1,0:T(8,128)S(1)} %get-tuple-element.23.hess_ref, bf16[64,128]{1,0:T(8,128)(2,1)S(1)} %get-tuple-element.24.refs_0_, bf16[64,128]{1,0:T(8,128)(2,1)S(1)} %collective-permute-done.2.refs_1_, ...), custom_call_target="tpu_custom_call" | custom-call | flops 1572864 | bytes 2097152 | tf_op jit(solution)/shard_map/project/pallas_call | solution.py:532
  30.4 0.3 collective-permute-done.4.block_ref
  30.7 0.3 project_last.1
  31.0 9.5 %all_to_all.11.lines_ref = f32[32,1,128]{2,1,0:T(1,128)S(1)} all-to-all(f32[32,1,128]{2,1,0:T(1,128)S(1)} %project_last.1), channel_id=1, replica_groups=mesh['grp'=4,'tile'=8] {'grp','tile'}, dimensions={0} | all-to-all | bytes 32768 | tf_op jit(solution)/shard_map/all_to_all | solution.py:555
  40.5 0.5 %add_lines.1 = f32[1,128]{1,0:T(1,128)} custom-call(f32[32,1,128]{2,1,0:T(1,128)S(1)} %all_to_all.11.lines_ref), custom_call_target="tpu_custom_call" | custom-call | tf_op jit(solution)/shard_map/add_lines/pallas_call | solution.py:556
Async XLA Ops:
  14.5 5.1 %collective-permute-start = (bf16[128,128]{1,0:T(8,128)(2,1)S(1)}, bf16[128,128]{1,0:T(8,128)(2,1)S(1)}, u32[]{:S(2)}, u32[]{:S(2)}) collective-permute-start(bf16[128,128]{1,0:T(8,128)(2,1)S(1)} %get-tuple-element.19), channel_id=1, source_target_pairs={{0,24},{8,16},{16,8},{24,0},{1,25},{9,17},{17,9},{25,1},{2,26},{10... | collective-permute-start | bytes 98312 | tf_op jit(solution)/shard_map/ppermute | solution.py:502
  17.0 3.9 %collective-permute-start.1 = (bf16[128,128]{1,0:T(8,128)(2,1)S(1)}, bf16[128,128]{1,0:T(8,128)(2,1)S(1)}, u32[]{:S(2)}, u32[]{:S(2)}) collective-permute-start(bf16[128,128]{1,0:T(8,128)(2,1)S(1)} %get-tuple-element.20), channel_id=1, source_target_pairs={{0,8},{8,0},{16,24},{24,16},{1,9},{9,1},{17,25},{25,17},{2,10},{10... | collective-permute-start | bytes 98312 | tf_op jit(solution)/shard_map/ppermute | solution.py:501
  24.9 4.7 %collective-permute-start.3 = (bf16[64,128]{1,0:T(8,128)(2,1)S(1)}, bf16[64,128]{1,0:T(8,128)(2,1)S(1)}, u32[]{:S(2)}, u32[]{:S(2)}) collective-permute-start(bf16[64,128]{1,0:T(8,128)(2,1)S(1)} %get-tuple-element.24.refs_0_), channel_id=1, source_target_pairs={{0,24},{8,16},{16,8},{24,0},{1,25},{9,17},{17,9},{25,1},{2,26},{10... | collective-permute-start | bytes 49160 | tf_op jit(solution)/shard_map/ppermute | solution.py:530
  25.9 3.9 %collective-permute-start.2 = (bf16[64,128]{1,0:T(8,128)(2,1)S(1)}, bf16[64,128]{1,0:T(8,128)(2,1)S(1)}, u32[]{:S(2)}, u32[]{:S(2)}) collective-permute-start(bf16[64,128]{1,0:T(8,128)(2,1)S(1)} %get-tuple-element.24.refs_0_), channel_id=1, source_target_pairs={{0,16},{8,24},{16,0},{24,8},{1,17},{9,25},{17,1},{25,9},{2,18},{10... | collective-permute-start | bytes 49160 | tf_op jit(solution)/shard_map/ppermute | solution.py:530
  27.0 3.7 %collective-permute-start.4 = (bf16[64,128]{1,0:T(8,128)(2,1)S(1)}, bf16[64,128]{1,0:T(8,128)(2,1)S(1)}, u32[]{:S(2)}, u32[]{:S(2)}) collective-permute-start(bf16[64,128]{1,0:T(8,128)(2,1)S(1)} %get-tuple-element.24.refs_0_), channel_id=1, source_target_pairs={{0,8},{8,0},{16,24},{24,16},{1,9},{9,1},{17,25},{25,17},{2,10},{10... | collective-permute-start | bytes 49160 | tf_op jit(solution)/shard_map/ppermute | solution.py:530

commit v8 on v7

--- a/solution.py
+++ b/solution.py
@@ -411,10 +411,6 @@
     low_ref[...] = hess.astype(BF16)
 
 
-def distances(n_grp):
-    return [0] + list(range(2, n_grp)) + [1]
-
-
 def project_block(panels_ref, probe_ref, k, distance):
     count, n_grp, rows, columns = panels_ref.shape
     product = panels_ref[k, lax.axis_index("grp") ^ distance].astype(F32) * probe_ref[...].astype(F32)
@@ -425,9 +421,8 @@
     blocks, (sums_ref, hess_hbm, sem) = refs[:-3], refs[-3:]
     copy = pltpu.make_async_copy(hess_ref, hess_hbm, sem)
     copy.start()
-    order = distances(panels_ref.shape[1])
     for k in range(panels_ref.shape[0]):
-        sums_ref[k] = sum(project_block(panels_ref, block, k, i) for i, block in zip(order, blocks))
+        sums_ref[k] = sum(project_block(panels_ref, block, k, i) for i, block in enumerate(blocks))
     copy.wait()
 
 
@@ -435,7 +430,7 @@
     count, n_grp = panels_ref.shape[:2]
     sums = []
     for k in range(count):
-        total = sums_ref[k] + project_block(panels_ref, block_ref, k, distances(n_grp)[-1])
+        total = sums_ref[k] + project_block(panels_ref, block_ref, k, n_grp - 1)
         sums.append(jnp.sum(total, axis=0, keepdims=True))
     sums.append(jnp.zeros((128 - count, 128), F32))
     table = jnp.concatenate(sums, axis=0)
@@ -526,9 +521,10 @@
         name="solve",
     )(ext, pix, odd, even, inputs[0], pltpu.with_memory_space_constraint(panels, pltpu.HBM))
 
-    column = [probe_low] + [
-        lax.ppermute(probe_low, "grp", [(i, i ^ k) for i in range(n_grp)]) for k in distances(n_grp)[1:]
-    ]
+    column = [probe_low]
+    while len(column) < n_grp:
+        swap = [(i, i ^ len(column)) for i in range(n_grp)]
+        column += [lax.ppermute(block, "grp", swap) for block in column]
     sums, hessian_probe = pl.pallas_call(
         project_kernel,
         out_shape=(

time: 41.3 us -> 42.4 us (1.027)
  waiting for transfers between devices: 4.99 us -> 8.25 us
  starting transfers between devices: 6.6 us -> 5.08 us
  blocking collectives: 22 us -> 21.4 us
    ppermute x3, waiting for transfers between devices: 1.61 us -> 4.87 us  [on_device(): column += [lax.ppermute(block, 'grp', swap) for block in column]]
    ppermute x3, starting transfers between devices: 3.55 us -> 2.04 us  [on_device(): column += [lax.ppermute(block, 'grp', swap) for block in column]]
    all_to_all x1, blocking collectives: 9.48 us -> 8.83 us  [on_device(): lax.all_to_all(partial, ('grp', 'tile'), split_axis=0, concat_axis=0, til...]
  transfers between devices with their start and end apart: 5 -> 5, of which waited for: 5 -> 4; matrix products, arithmetic and copies ran while one was open for 0% -> 0% of each run, Pallas kernels for 2% -> 1%
where the time goes in v8:
time: 42.4 us; the launch traced here: 42.2 us
  blocking collectives  21.4 us (50%)
  waiting for transfers between devices  8.25 us (19%)
  Pallas kernels  6.77 us (16%)
  starting transfers between devices  5.08 us (12%)
  between operations  0.67 us (2%)
    all_to_all x1, blocking collectives, on_device(): got = lax.all_to_all(slots, 'tile', split_axis=0, concat_axis=0, tiled=True)  12.5 us
    all_to_all x1, blocking collectives, on_device(): lax.all_to_all(partial, ('grp', 'tile'), split_axis=0, concat_axis=0, til...  8.83 us
    ppermute x3, waiting for transfers between devices, on_device(): column += [lax.ppermute(block, 'grp', swap) for block in column]  4.87 us
    pallas_call x1, Pallas kernels, on_device(): pl.pallas_call(functools.partial(solve_kernel, n_grp, n_tile), out_shape=...  3.96 us
    ppermute x1, starting transfers between devices, on_device(): lax.ppermute(odd, 'grp', [(i, (i - 1 + 2 * (i % 2)) % n_grp) for i in ran...  2.51 us
    ppermute x1, waiting for transfers between devices, on_device(): lax.ppermute(odd, 'grp', [(i, (i - 1 + 2 * (i % 2)) % n_grp) for i in ran...  2.06 us
    ppermute x3, starting transfers between devices, on_device(): column += [lax.ppermute(block, 'grp', swap) for block in column]  2.04 us
    ppermute x1, waiting for transfers between devices, on_device(): even = lax.ppermute(even, 'grp', [(i, i ^ 1) for i in range(n_grp)])  1.32 us
  transfers between devices with their start and end apart: 5, of which 4 were waited for; matrix products, arithmetic and copies ran while one was open for 0% of the time, Pallas kernels for 1%

profile of v8, /device:TPU:0, one launch (start us, length us, event | category | flops | bytes accessed | tf_op | source)
XLA Modules:
  0.0 42.2 jit_solution(13762741132825690861)
XLA Ops:
  0.6 1.1 %pack_tiles.1 = (bf16[8,48,128]{2,1,0:T(8,128)(2,1)S(1)}, f32[4,64,128]{2,1,0:T(8,128)S(1)}) custom-call(f32[2,64,128]{2,1,0:T(8,128)} %bv_hbm.1, f32[64,128]{1,0:T(8,128)} %refs_1_.1, f32[64,128]{1,0:T(8,128)} %refs_2_.1, f32[64,128]{1,0:T(8,128)} %refs_3_.1, f32[1,1,2,512]{3,2,1,0:T(2,128)} %refs_4_.1, f32[1,1,1,512]{3,2,1,0:T(1,128)} %refs_5_.1, ...), custom_call_target="tpu_custom_call" | custom-call | tf_op jit(solution)/shard_map/pack_tiles/pallas_call | solution.py:468
  1.8 12.5 %all_to_all.10.got_ref = bf16[8,48,128]{2,1,0:T(8,128)(2,1)S(1)} all-to-all(bf16[8,48,128]{2,1,0:T(8,128)(2,1)S(1)} %get-tuple-element.16), channel_id=1, replica_groups=mesh['grp'=4,'tile'=8] {'tile'}, dimensions={0} | all-to-all | bytes 196608 | tf_op jit(solution)/shard_map/all_to_all | solution.py:480
  14.3 0.2 pack_rows.1
  14.5 2.5 %collective-permute-start = (bf16[128,128]{1,0:T(8,128)(2,1)S(1)}, bf16[128,128]{1,0:T(8,128)(2,1)S(1)}, u32[]{:S(2)}, u32[]{:S(2)}) collective-permute-start(bf16[128,128]{1,0:T(8,128)(2,1)S(1)} %get-tuple-element.19), channel_id=1, source_target_pairs={{0,24},{8,16},{16,8},{24,0},{1,25},{9,17},{17,9},{25,1},{2,26},{10... | collective-permute-start | bytes 98312 | tf_op jit(solution)/shard_map/ppermute | solution.py:497
  17.0 0.5 %collective-permute-start.1 = (bf16[128,128]{1,0:T(8,128)(2,1)S(1)}, bf16[128,128]{1,0:T(8,128)(2,1)S(1)}, u32[]{:S(2)}, u32[]{:S(2)}) collective-permute-start(bf16[128,128]{1,0:T(8,128)(2,1)S(1)} %get-tuple-element.20), channel_id=1, source_target_pairs={{0,8},{8,0},{16,24},{24,16},{1,9},{9,1},{17,25},{25,17},{2,10},{10... | collective-permute-start | bytes 98312 | tf_op jit(solution)/shard_map/ppermute | solution.py:496
  17.5 2.1 %collective-permute-done.odd_ref = bf16[128,128]{1,0:T(8,128)(2,1)S(1)} collective-permute-done((bf16[128,128]{1,0:T(8,128)(2,1)S(1)}, bf16[128,128]{1,0:T(8,128)(2,1)S(1)}, u32[]{:S(2)}, u32[]{:S(2)}) %collective-permute-start) | collective-permute-done | bytes 32800 | tf_op jit(solution)/shard_map/ppermute | solution.py:497
  19.6 1.3 %collective-permute-done.1.even_ref = bf16[128,128]{1,0:T(8,128)(2,1)S(1)} collective-permute-done((bf16[128,128]{1,0:T(8,128)(2,1)S(1)}, bf16[128,128]{1,0:T(8,128)(2,1)S(1)}, u32[]{:S(2)}, u32[]{:S(2)}) %collective-permute-start.1) | collective-permute-done | bytes 32800 | tf_op jit(solution)/shard_map/ppermute | solution.py:496
  20.9 4.0 %solve.1 = (f32[2,64,128]{2,1,0:T(8,128)}, f32[64,128]{1,0:T(8,128)S(1)}, bf16[64,128]{1,0:T(8,128)(2,1)S(1)}, bf16[32,4,64,128]{3,2,1,0:T(8,128)(2,1)S(1)}) custom-call(f32[4,64,256]{2,1,0:T(8,128)S(1)} %get-tuple-element.17.ext_ref, f32[48,128]{1,0:T(8,128)S(1)} %get-tuple-element.18.pix_ref, bf16[128,128]{1,0:T(8,128)(2,1)S(1)} %collective-permute-done.odd_ref, ...), custom_call_target="tpu_custom_call" | custom-call | tf_op jit(solution)/shard_map/solve/pallas_call | solution.py:499
  24.9 0.6 %collective-permute-start.2 = (bf16[64,128]{1,0:T(8,128)(2,1)S(1)}, bf16[64,128]{1,0:T(8,128)(2,1)S(1)}, u32[]{:S(2)}, u32[]{:S(2)}) collective-permute-start(bf16[64,128]{1,0:T(8,128)(2,1)S(1)} %get-tuple-element.24.refs_0_), channel_id=1, source_target_pairs={{0,8},{8,0},{16,24},{24,16},{1,9},{9,1},{17,25},{25,17},{2,10},{10... | collective-permute-start | bytes 49160 | tf_op jit(solution)/shard_map/ppermute | solution.py:527
  25.5 0.9 %collective-permute-start.3 = (bf16[64,128]{1,0:T(8,128)(2,1)S(1)}, bf16[64,128]{1,0:T(8,128)(2,1)S(1)}, u32[]{:S(2)}, u32[]{:S(2)}) collective-permute-start(bf16[64,128]{1,0:T(8,128)(2,1)S(1)} %get-tuple-element.24.refs_0_), channel_id=1, source_target_pairs={{0,16},{8,24},{16,0},{24,8},{1,17},{9,25},{17,1},{25,9},{2,18},{10... | collective-permute-start | bytes 49160 | tf_op jit(solution)/shard_map/ppermute | solution.py:527
  26.4 2.3 %collective-permute-done.2.refs_1_ = bf16[64,128]{1,0:T(8,128)(2,1)S(1)} collective-permute-done((bf16[64,128]{1,0:T(8,128)(2,1)S(1)}, bf16[64,128]{1,0:T(8,128)(2,1)S(1)}, u32[]{:S(2)}, u32[]{:S(2)}) %collective-permute-start.2) | collective-permute-done | bytes 16416 | tf_op jit(solution)/shard_map/ppermute | solution.py:527
  28.7 0.5 %collective-permute-start.4 = (bf16[64,128]{1,0:T(8,128)(2,1)S(1)}, bf16[64,128]{1,0:T(8,128)(2,1)S(1)}, u32[]{:S(2)}, u32[]{:S(2)}) collective-permute-start(bf16[64,128]{1,0:T(8,128)(2,1)S(1)} %collective-permute-done.2.refs_1_), channel_id=1, source_target_pairs={{0,16},{8,24},{16,0},{24,8},{1,17},{9,25},{17,1},{25,9},{2,18},{10... | collective-permute-start | bytes 49160 | tf_op jit(solution)/shard_map/ppermute | solution.py:527
  29.2 0.0 collective-permute-done.3.refs_2_
  29.2 0.6 %project.1 = (f32[32,8,128]{2,1,0:T(8,128)S(1)}, f32[64,128]{1,0:T(8,128)}) custom-call(bf16[32,4,64,128]{3,2,1,0:T(8,128)(2,1)S(1)} %get-tuple-element.22.panels_ref, f32[64,128]{1,0:T(8,128)S(1)} %get-tuple-element.23.hess_ref, bf16[64,128]{1,0:T(8,128)(2,1)S(1)} %get-tuple-element.24.refs_0_, bf16[64,128]{1,0:T(8,128)(2,1)S(1)} %collective-permute-done.2.refs_1_, ...), custom_call_target="tpu_custom_call" | custom-call | flops 1572864 | bytes 2097152 | tf_op jit(solution)/shard_map/project/pallas_call | solution.py:528
  29.9 2.6 %collective-permute-done.4.block_ref = bf16[64,128]{1,0:T(8,128)(2,1)S(1)} collective-permute-done((bf16[64,128]{1,0:T(8,128)(2,1)S(1)}, bf16[64,128]{1,0:T(8,128)(2,1)S(1)}, u32[]{:S(2)}, u32[]{:S(2)}) %collective-permute-start.4) | collective-permute-done | bytes 16416 | tf_op jit(solution)/shard_map/ppermute | solution.py:527
  32.4 0.3 project_last.1
  32.8 8.8 %all_to_all.11.lines_ref = f32[32,1,128]{2,1,0:T(1,128)S(1)} all-to-all(f32[32,1,128]{2,1,0:T(1,128)S(1)} %project_last.1), channel_id=1, replica_groups=mesh['grp'=4,'tile'=8] {'grp','tile'}, dimensions={0} | all-to-all | bytes 32768 | tf_op jit(solution)/shard_map/all_to_all | solution.py:551
  41.6 0.5 %add_lines.1 = f32[1,128]{1,0:T(1,128)} custom-call(f32[32,1,128]{2,1,0:T(1,128)S(1)} %all_to_all.11.lines_ref), custom_call_target="tpu_custom_call" | custom-call | tf_op jit(solution)/shard_map/add_lines/pallas_call | solution.py:552
Async XLA Ops:
  14.5 5.1 %collective-permute-start = (bf16[128,128]{1,0:T(8,128)(2,1)S(1)}, bf16[128,128]{1,0:T(8,128)(2,1)S(1)}, u32[]{:S(2)}, u32[]{:S(2)}) collective-permute-start(bf16[128,128]{1,0:T(8,128)(2,1)S(1)} %get-tuple-element.19), channel_id=1, source_target_pairs={{0,24},{8,16},{16,8},{24,0},{1,25},{9,17},{17,9},{25,1},{2,26},{10... | collective-permute-start | bytes 98312 | tf_op jit(solution)/shard_map/ppermute | solution.py:497
  17.0 3.9 %collective-permute-start.1 = (bf16[128,128]{1,0:T(8,128)(2,1)S(1)}, bf16[128,128]{1,0:T(8,128)(2,1)S(1)}, u32[]{:S(2)}, u32[]{:S(2)}) collective-permute-start(bf16[128,128]{1,0:T(8,128)(2,1)S(1)} %get-tuple-element.20), channel_id=1, source_target_pairs={{0,8},{8,0},{16,24},{24,16},{1,9},{9,1},{17,25},{25,17},{2,10},{10... | collective-permute-start | bytes 98312 | tf_op jit(solution)/shard_map/ppermute | solution.py:496
  24.9 3.8 %collective-permute-start.2 = (bf16[64,128]{1,0:T(8,128)(2,1)S(1)}, bf16[64,128]{1,0:T(8,128)(2,1)S(1)}, u32[]{:S(2)}, u32[]{:S(2)}) collective-permute-start(bf16[64,128]{1,0:T(8,128)(2,1)S(1)} %get-tuple-element.24.refs_0_), channel_id=1, source_target_pairs={{0,8},{8,0},{16,24},{24,16},{1,9},{9,1},{17,25},{25,17},{2,10},{10... | collective-permute-start | bytes 49160 | tf_op jit(solution)/shard_map/ppermute | solution.py:527
  25.5 3.7 %collective-permute-start.3 = (bf16[64,128]{1,0:T(8,128)(2,1)S(1)}, bf16[64,128]{1,0:T(8,128)(2,1)S(1)}, u32[]{:S(2)}, u32[]{:S(2)}) collective-permute-start(bf16[64,128]{1,0:T(8,128)(2,1)S(1)} %get-tuple-element.24.refs_0_), channel_id=1, source_target_pairs={{0,16},{8,24},{16,0},{24,8},{1,17},{9,25},{17,1},{25,9},{2,18},{10... | collective-permute-start | bytes 49160 | tf_op jit(solution)/shard_map/ppermute | solution.py:527
  28.7 3.7 %collective-permute-start.4 = (bf16[64,128]{1,0:T(8,128)(2,1)S(1)}, bf16[64,128]{1,0:T(8,128)(2,1)S(1)}, u32[]{:S(2)}, u32[]{:S(2)}) collective-permute-start(bf16[64,128]{1,0:T(8,128)(2,1)S(1)} %collective-permute-done.2.refs_1_), channel_id=1, source_target_pairs={{0,16},{8,24},{16,0},{24,8},{1,17},{9,25},{17,1},{25,9},{2,18},{10... | collective-permute-start | bytes 49160 | tf_op jit(solution)/shard_map/ppermute | solution.py:527

commit v9 on v7

--- a/solution.py
+++ b/solution.py
@@ -332,7 +332,10 @@
         n_near, n_all = n_tile // 2, 3 * n_tile // 2
         low = lanes((n_tile, 128)) < CAP
         spans = ((0, HALO, rows), (-1, HALO - EDGE, EDGE), (1, HALO + rows, EDGE))
-        rim_lane = lanes((2 * rows, 128))
+
+        def exact(h, delta):
+            return h == 0 and delta == 0
+
         jobs = []
         for delta, first, size in spans:
             if delta == 0:
@@ -350,24 +353,20 @@
                     part = nat_ref[comp, h, first : first + size, :]
                     parts.append(part if h == 0 else pltpu.roll(part, EDGE, 1))
                 field = jnp.concatenate(parts, axis=0)
-                high = field.astype(BF16).astype(F32)
-                rest = field - high
-                if h == 0:
-                    stacked = jnp.concatenate([high.astype(BF16), rest.astype(BF16)], axis=1)
-                else:
-                    lane_here = rim_lane[0 : 2 * size]
-                    stacked = jnp.where(lane_here < 2 * EDGE, high, pltpu.roll(rest, 2 * EDGE, 1))
-                    stacked = jnp.where(lane_here < 4 * EDGE, stacked, 0.0).astype(BF16)
-                jobs.append((h, first, size, begin, count, lane_of, los_x, los_y, r, stacked))
+                stacked = field.astype(BF16)
+                if exact(h, delta):
+                    rest = (field - stacked.astype(F32)).astype(BF16)
+                    stacked = jnp.concatenate([stacked, rest], axis=1)
+                jobs.append((exact(h, delta), h, first, size, begin, count, lane_of, los_x, los_y, r, stacked))
 
         nat_ref[...] = jnp.zeros_like(nat_ref)
-        for h, first, size, begin, count, lane_of, los_x, los_y, r, stacked in jobs:
+        for two_parts, h, first, size, begin, count, lane_of, los_x, los_y, r, stacked in jobs:
             chunk = 4 if h == 0 else 8
             depth = 128 if h == 0 else 2 * EDGE
             wide = chunk * 128
             row_id = lax.broadcasted_iota(jnp.int32, (size, wide), 0).astype(F32)
             lane_id = lax.broadcasted_iota(jnp.int32, (depth, wide), 0).astype(F32)
-            total = jnp.zeros((4 * size, 128), F32)
+            total = jnp.zeros(((4 if two_parts else 2) * size, 128), F32)
             for j in range(0, count, chunk):
 
                 def line(table, offset):
@@ -376,20 +375,21 @@
                 line_x, line_y = line(los_x, begin), line(los_y, begin)
                 hot = jnp.where(lane_id == line(lane_of, 0), 1.0, 0.0).astype(BF16)
                 here = row_id == line(r, begin)
-                twice = [hot, hot]
                 if h == 1:
-                    twice.append(jnp.zeros((128 - 2 * depth, wide), BF16))
                     hot = jnp.concatenate([hot, jnp.zeros((128 - depth, wide), BF16)], axis=0)
-                got = jnp.dot(stacked, jnp.concatenate(twice, axis=0), preferred_element_type=F32)
+                twice = jnp.concatenate([hot, hot], axis=0) if two_parts else hot
+                got = jnp.dot(stacked, twice, preferred_element_type=F32)
                 got_x = jnp.sum(jnp.where(here, got[0:size], 0.0), axis=0, keepdims=True)
                 got_y = jnp.sum(jnp.where(here, got[size:], 0.0), axis=0, keepdims=True)
                 amount = line_x * got_x + line_y * got_y
                 terms = [amount * line_x, amount * line_y]
-                highs = [p.astype(BF16).astype(F32) for p in terms]
-                terms = highs + [p - q for p, q in zip(terms, highs)]
+                if two_parts:
+                    highs = [p.astype(BF16).astype(F32) for p in terms]
+                    terms = highs + [p - q for p, q in zip(terms, highs)]
                 spread = jnp.concatenate([jnp.where(here, p, 0.0) for p in terms], axis=0).astype(BF16)
                 total = total + lax.dot_general(spread, hot, (((1,), (1,)), ((), ())), preferred_element_type=F32)
-            total = total[0 : 2 * size] + total[2 * size :]
+            if two_parts:
+                total = total[0 : 2 * size] + total[2 * size :]
             if h == 1:
                 total = pltpu.roll(total, 128 - EDGE, 1)
             for c in range(2):
@@ -439,9 +439,10 @@
         sums.append(jnp.sum(total, axis=0, keepdims=True))
     sums.append(jnp.zeros((128 - count, 128), F32))
     table = jnp.concatenate(sums, axis=0)
+    high = table.astype(BF16)
+    parts = jnp.concatenate([high, (table - high.astype(F32)).astype(BF16)], axis=1)
     line = lax.dot_general(
-        jnp.ones((8, 128), F32), table, (((1,), (1,)), ((), ())),
-        precision=lax.Precision.HIGHEST, preferred_element_type=F32,
+        jnp.ones((16, 256), BF16), parts, (((1,), (1,)), ((), ())), preferred_element_type=F32
     )
     line = pltpu.roll(line, lax.axis_index("grp") * count, 1)[0:1]
     out_ref[...] = jnp.broadcast_to(line[None], out_ref.shape)

time: 41.3 us -> 41.3 us (level)
  no operation moved by 1% of the time
where the time goes in v9:
time: 41.3 us; the launch traced here: 41.1 us
  blocking collectives  22 us (53%)
  Pallas kernels  6.76 us (16%)
  starting transfers between devices  6.6 us (16%)
  waiting for transfers between devices  4.99 us (12%)
  between operations  0.67 us (2%)
    all_to_all x1, blocking collectives, on_device(): got = lax.all_to_all(slots, 'tile', split_axis=0, concat_axis=0, tiled=True)  12.5 us
    all_to_all x1, blocking collectives, on_device(): lax.all_to_all(partial, ('grp', 'tile'), split_axis=0, concat_axis=0, til...  9.49 us
    pallas_call x1, Pallas kernels, on_device(): pl.pallas_call(functools.partial(solve_kernel, n_grp, n_tile), out_shape=...  3.95 us
    ppermute x3, starting transfers between devices, on_device(): lax.ppermute(probe_low, 'grp', [(i, i ^ k) for i in range(n_grp)])  3.55 us
    ppermute x1, starting transfers between devices, on_device(): lax.ppermute(odd, 'grp', [(i, (i - 1 + 2 * (i % 2)) % n_grp) for i in ran...  2.51 us
    ppermute x1, waiting for transfers between devices, on_device(): lax.ppermute(odd, 'grp', [(i, (i - 1 + 2 * (i % 2)) % n_grp) for i in ran...  2.06 us
    ppermute x3, waiting for transfers between devices, on_device(): lax.ppermute(probe_low, 'grp', [(i, i ^ k) for i in range(n_grp)])  1.62 us
    ppermute x1, waiting for transfers between devices, on_device(): even = lax.ppermute(even, 'grp', [(i, i ^ 1) for i in range(n_grp)])  1.32 us
  transfers between devices with their start and end apart: 5, of which 5 were waited for; matrix products, arithmetic and copies ran while one was open for 0% of the time, Pallas kernels for 2%

profile of v9, /device:TPU:0, one launch (start us, length us, event | category | flops | bytes accessed | tf_op | source)
XLA Modules:
  0.0 41.1 jit_solution(789821406456697596)
XLA Ops:
  0.6 1.1 %pack_tiles.1 = (bf16[8,48,128]{2,1,0:T(8,128)(2,1)S(1)}, f32[4,64,128]{2,1,0:T(8,128)S(1)}) custom-call(f32[2,64,128]{2,1,0:T(8,128)} %bv_hbm.1, f32[64,128]{1,0:T(8,128)} %refs_1_.1, f32[64,128]{1,0:T(8,128)} %refs_2_.1, f32[64,128]{1,0:T(8,128)} %refs_3_.1, f32[1,1,2,512]{3,2,1,0:T(2,128)} %refs_4_.1, f32[1,1,1,512]{3,2,1,0:T(1,128)} %refs_5_.1, ...), custom_call_target="tpu_custom_call" | custom-call | tf_op jit(solution)/shard_map/pack_tiles/pallas_call | solution.py:474
  1.8 12.5 %all_to_all.10.got_ref = bf16[8,48,128]{2,1,0:T(8,128)(2,1)S(1)} all-to-all(bf16[8,48,128]{2,1,0:T(8,128)(2,1)S(1)} %get-tuple-element.16), channel_id=1, replica_groups=mesh['grp'=4,'tile'=8] {'tile'}, dimensions={0} | all-to-all | bytes 196608 | tf_op jit(solution)/shard_map/all_to_all | solution.py:486
  14.3 0.2 pack_rows.1
  14.5 2.5 %collective-permute-start = (bf16[128,128]{1,0:T(8,128)(2,1)S(1)}, bf16[128,128]{1,0:T(8,128)(2,1)S(1)}, u32[]{:S(2)}, u32[]{:S(2)}) collective-permute-start(bf16[128,128]{1,0:T(8,128)(2,1)S(1)} %get-tuple-element.19), channel_id=1, source_target_pairs={{0,24},{8,16},{16,8},{24,0},{1,25},{9,17},{17,9},{25,1},{2,26},{10... | collective-permute-start | bytes 98312 | tf_op jit(solution)/shard_map/ppermute | solution.py:503
  17.0 0.5 %collective-permute-start.1 = (bf16[128,128]{1,0:T(8,128)(2,1)S(1)}, bf16[128,128]{1,0:T(8,128)(2,1)S(1)}, u32[]{:S(2)}, u32[]{:S(2)}) collective-permute-start(bf16[128,128]{1,0:T(8,128)(2,1)S(1)} %get-tuple-element.20), channel_id=1, source_target_pairs={{0,8},{8,0},{16,24},{24,16},{1,9},{9,1},{17,25},{25,17},{2,10},{10... | collective-permute-start | bytes 98312 | tf_op jit(solution)/shard_map/ppermute | solution.py:502
  17.5 2.1 %collective-permute-done.odd_ref = bf16[128,128]{1,0:T(8,128)(2,1)S(1)} collective-permute-done((bf16[128,128]{1,0:T(8,128)(2,1)S(1)}, bf16[128,128]{1,0:T(8,128)(2,1)S(1)}, u32[]{:S(2)}, u32[]{:S(2)}) %collective-permute-start) | collective-permute-done | bytes 32800 | tf_op jit(solution)/shard_map/ppermute | solution.py:503
  19.6 1.3 %collective-permute-done.1.even_ref = bf16[128,128]{1,0:T(8,128)(2,1)S(1)} collective-permute-done((bf16[128,128]{1,0:T(8,128)(2,1)S(1)}, bf16[128,128]{1,0:T(8,128)(2,1)S(1)}, u32[]{:S(2)}, u32[]{:S(2)}) %collective-permute-start.1) | collective-permute-done | bytes 32800 | tf_op jit(solution)/shard_map/ppermute | solution.py:502
  20.9 4.0 %solve.1 = (f32[2,64,128]{2,1,0:T(8,128)}, f32[64,128]{1,0:T(8,128)S(1)}, bf16[64,128]{1,0:T(8,128)(2,1)S(1)}, bf16[32,4,64,128]{3,2,1,0:T(8,128)(2,1)S(1)}) custom-call(f32[4,64,256]{2,1,0:T(8,128)S(1)} %get-tuple-element.17.ext_ref, f32[48,128]{1,0:T(8,128)S(1)} %get-tuple-element.18.pix_ref, bf16[128,128]{1,0:T(8,128)(2,1)S(1)} %collective-permute-done.odd_ref, ...), custom_call_target="tpu_custom_call" | custom-call | tf_op jit(solution)/shard_map/solve/pallas_call | solution.py:505
  24.9 1.0 %collective-permute-start.3 = (bf16[64,128]{1,0:T(8,128)(2,1)S(1)}, bf16[64,128]{1,0:T(8,128)(2,1)S(1)}, u32[]{:S(2)}, u32[]{:S(2)}) collective-permute-start(bf16[64,128]{1,0:T(8,128)(2,1)S(1)} %get-tuple-element.24.refs_0_), channel_id=1, source_target_pairs={{0,24},{8,16},{16,8},{24,0},{1,25},{9,17},{17,9},{25,1},{2,26},{10... | collective-permute-start | bytes 49160 | tf_op jit(solution)/shard_map/ppermute | solution.py:531
  25.9 1.1 %collective-permute-start.2 = (bf16[64,128]{1,0:T(8,128)(2,1)S(1)}, bf16[64,128]{1,0:T(8,128)(2,1)S(1)}, u32[]{:S(2)}, u32[]{:S(2)}) collective-permute-start(bf16[64,128]{1,0:T(8,128)(2,1)S(1)} %get-tuple-element.24.refs_0_), channel_id=1, source_target_pairs={{0,16},{8,24},{16,0},{24,8},{1,17},{9,25},{17,1},{25,9},{2,18},{10... | collective-permute-start | bytes 49160 | tf_op jit(solution)/shard_map/ppermute | solution.py:531
  26.9 1.5 %collective-permute-start.4 = (bf16[64,128]{1,0:T(8,128)(2,1)S(1)}, bf16[64,128]{1,0:T(8,128)(2,1)S(1)}, u32[]{:S(2)}, u32[]{:S(2)}) collective-permute-start(bf16[64,128]{1,0:T(8,128)(2,1)S(1)} %get-tuple-element.24.refs_0_), channel_id=1, source_target_pairs={{0,8},{8,0},{16,24},{24,16},{1,9},{9,1},{17,25},{25,17},{2,10},{10... | collective-permute-start | bytes 49160 | tf_op jit(solution)/shard_map/ppermute | solution.py:531
  28.4 1.2 %collective-permute-done.3.refs_2_ = bf16[64,128]{1,0:T(8,128)(2,1)S(1)} collective-permute-done((bf16[64,128]{1,0:T(8,128)(2,1)S(1)}, bf16[64,128]{1,0:T(8,128)(2,1)S(1)}, u32[]{:S(2)}, u32[]{:S(2)}) %collective-permute-start.3) | collective-permute-done | bytes 16416 | tf_op jit(solution)/shard_map/ppermute | solution.py:531
  29.6 0.2 collective-permute-done.2.refs_1_
  29.8 0.6 %project.1 = (f32[32,8,128]{2,1,0:T(8,128)S(1)}, f32[64,128]{1,0:T(8,128)}) custom-call(bf16[32,4,64,128]{3,2,1,0:T(8,128)(2,1)S(1)} %get-tuple-element.22.panels_ref, f32[64,128]{1,0:T(8,128)S(1)} %get-tuple-element.23.hess_ref, bf16[64,128]{1,0:T(8,128)(2,1)S(1)} %get-tuple-element.24.refs_0_, bf16[64,128]{1,0:T(8,128)(2,1)S(1)} %collective-permute-done.2.refs_1_, ...), custom_call_target="tpu_custom_call" | custom-call | flops 1572864 | bytes 2097152 | tf_op jit(solution)/shard_map/project/pallas_call | solution.py:533
  30.4 0.3 collective-permute-done.4.block_ref
  30.7 0.3 project_last.1
  31.0 9.5 %all_to_all.11.lines_ref = f32[32,1,128]{2,1,0:T(1,128)S(1)} all-to-all(f32[32,1,128]{2,1,0:T(1,128)S(1)} %project_last.1), channel_id=1, replica_groups=mesh['grp'=4,'tile'=8] {'grp','tile'}, dimensions={0} | all-to-all | bytes 32768 | tf_op jit(solution)/shard_map/all_to_all | solution.py:556
  40.5 0.5 %add_lines.1 = f32[1,128]{1,0:T(1,128)} custom-call(f32[32,1,128]{2,1,0:T(1,128)S(1)} %all_to_all.11.lines_ref), custom_call_target="tpu_custom_call" | custom-call | tf_op jit(solution)/shard_map/add_lines/pallas_call | solution.py:557
Async XLA Ops:
  14.5 5.1 %collective-permute-start = (bf16[128,128]{1,0:T(8,128)(2,1)S(1)}, bf16[128,128]{1,0:T(8,128)(2,1)S(1)}, u32[]{:S(2)}, u32[]{:S(2)}) collective-permute-start(bf16[128,128]{1,0:T(8,128)(2,1)S(1)} %get-tuple-element.19), channel_id=1, source_target_pairs={{0,24},{8,16},{16,8},{24,0},{1,25},{9,17},{17,9},{25,1},{2,26},{10... | collective-permute-start | bytes 98312 | tf_op jit(solution)/shard_map/ppermute | solution.py:503
  17.0 3.9 %collective-permute-start.1 = (bf16[128,128]{1,0:T(8,128)(2,1)S(1)}, bf16[128,128]{1,0:T(8,128)(2,1)S(1)}, u32[]{:S(2)}, u32[]{:S(2)}) collective-permute-start(bf16[128,128]{1,0:T(8,128)(2,1)S(1)} %get-tuple-element.20), channel_id=1, source_target_pairs={{0,8},{8,0},{16,24},{24,16},{1,9},{9,1},{17,25},{25,17},{2,10},{10... | collective-permute-start | bytes 98312 | tf_op jit(solution)/shard_map/ppermute | solution.py:502
  24.9 4.7 %collective-permute-start.3 = (bf16[64,128]{1,0:T(8,128)(2,1)S(1)}, bf16[64,128]{1,0:T(8,128)(2,1)S(1)}, u32[]{:S(2)}, u32[]{:S(2)}) collective-permute-start(bf16[64,128]{1,0:T(8,128)(2,1)S(1)} %get-tuple-element.24.refs_0_), channel_id=1, source_target_pairs={{0,24},{8,16},{16,8},{24,0},{1,25},{9,17},{17,9},{25,1},{2,26},{10... | collective-permute-start | bytes 49160 | tf_op jit(solution)/shard_map/ppermute | solution.py:531
  25.9 3.9 %collective-permute-start.2 = (bf16[64,128]{1,0:T(8,128)(2,1)S(1)}, bf16[64,128]{1,0:T(8,128)(2,1)S(1)}, u32[]{:S(2)}, u32[]{:S(2)}) collective-permute-start(bf16[64,128]{1,0:T(8,128)(2,1)S(1)} %get-tuple-element.24.refs_0_), channel_id=1, source_target_pairs={{0,16},{8,24},{16,0},{24,8},{1,17},{9,25},{17,1},{25,9},{2,18},{10... | collective-permute-start | bytes 49160 | tf_op jit(solution)/shard_map/ppermute | solution.py:531
  26.9 3.7 %collective-permute-start.4 = (bf16[64,128]{1,0:T(8,128)(2,1)S(1)}, bf16[64,128]{1,0:T(8,128)(2,1)S(1)}, u32[]{:S(2)}, u32[]{:S(2)}) collective-permute-start(bf16[64,128]{1,0:T(8,128)(2,1)S(1)} %get-tuple-element.24.refs_0_), channel_id=1, source_target_pairs={{0,8},{8,0},{16,24},{24,16},{1,9},{9,1},{17,25},{25,17},{2,10},{10... | collective-permute-start | bytes 49160 | tf_op jit(solution)/shard_map/ppermute | solution.py:531

commit v10 on v9

--- a/solution.py
+++ b/solution.py
@@ -102,8 +102,7 @@
         out_ref[t - 1, 0:half, :] = fold(0).astype(BF16)
 
 
-def pack_rows_kernel(n_tile, fields_ref, got_ref, ext_ref, pix_ref, even_ref, odd_ref):
-    g = lax.axis_index("grp")
+def pack_rows_kernel(n_tile, fields_ref, got_ref, ext_ref, pix_ref, up_ref, down_ref):
     t = lax.axis_index("tile")
     rows = fields_ref.shape[1]
     half = rows // 2
@@ -148,23 +147,16 @@
     pix_ref[...] = pixels
     pixels = pixels.astype(BF16)
 
-    even = lax.rem(g, 2) == 0
-
-    def choose(one, two):
-        even_ref_value, odd_ref_value = jnp.where(even, one, two), jnp.where(even, two, one)
-        return even_ref_value.astype(BF16), odd_ref_value.astype(BF16)
-
-    for f, field in enumerate(fields):
-        at = pl.ds(f * HALO, HALO)
-        even_ref[at, :], odd_ref[at, :] = choose(field[rows - HALO :], field[0:HALO])
-    at = pl.ds(FIELDS * HALO, HALO)
-    even_ref[at, :], odd_ref[at, :] = choose(edge_down, edge_up)
-    for ref in (even_ref, odd_ref):
-        ref[(FIELDS + 1) * HALO :, :] = pixels
+    for ref, first, edge in ((up_ref, 0, edge_up), (down_ref, rows - HALO, edge_down)):
+        for f, field in enumerate(fields):
+            ref[f * HALO : (f + 1) * HALO, :] = field[first : first + HALO].astype(BF16)
+        base = FIELDS * HALO
+        ref[base : base + HALO, :] = edge.astype(BF16)
+        ref[base + HALO :, :] = pixels
 
 
 def solve_kernel(
-    n_grp, n_tile, ext_ref, pix_ref, odd_ref, even_ref, bv_hbm, panels_hbm,
+    n_grp, n_tile, ext_ref, pix_ref, above_ref, below_ref, bv_hbm, panels_hbm,
     inc_hbm, hess_ref, low_ref, panels_ref,
     plane_ref, coef_ref, src_ref, w_ref, nat_ref, bv_ref, inc_ref, sems, inc_sem,
 ):
@@ -181,17 +173,11 @@
     groups = span // STRIPS
     lane = lanes()
 
-    even = lax.rem(g, 2) == 0
-
     def above(first, size):
-        at = pl.ds(first, size)
-        got = jnp.where(even, odd_ref[at, :].astype(F32), even_ref[at, :].astype(F32))
-        return jnp.where(g > 0, got, 0.0)
+        return jnp.where(g > 0, above_ref[first : first + size, :].astype(F32), 0.0)
 
     def below(first, size):
-        at = pl.ds(first, size)
-        got = jnp.where(even, even_ref[at, :].astype(F32), odd_ref[at, :].astype(F32))
-        return jnp.where(g < n_grp - 1, got, 0.0)
+        return jnp.where(g < n_grp - 1, below_ref[first : first + size, :].astype(F32), 0.0)
 
     first_lane = lane == 0
     last_lane = lane == 127
@@ -486,7 +472,7 @@
     got = lax.all_to_all(slots, "tile", split_axis=0, concat_axis=0, tiled=True)
 
     packet = (FIELDS + 1) * HALO + 6 * n_tile
-    ext, pix, even, odd = pl.pallas_call(
+    ext, pix, up, down = pl.pallas_call(
         functools.partial(pack_rows_kernel, n_tile),
         out_shape=(
             jax.ShapeDtypeStruct((FIELDS, rows, 256), F32),
@@ -499,8 +485,8 @@
         compiler_params=params,
         name="pack_rows",
     )(fields, got)
-    even = lax.ppermute(even, "grp", [(i, i ^ 1) for i in range(n_grp)])
-    odd = lax.ppermute(odd, "grp", [(i, (i - 1 + 2 * (i % 2)) % n_grp) for i in range(n_grp)])
+    above = lax.ppermute(down, "grp", [(i, (i + 1) % n_grp) for i in range(n_grp)])
+    below = lax.ppermute(up, "grp", [((i + 1) % n_grp, i) for i in range(n_grp)])
 
     increment, hess, probe_low, panels_near = pl.pallas_call(
         functools.partial(solve_kernel, n_grp, n_tile),
@@ -525,7 +511,7 @@
         ],
         compiler_params=params,
         name="solve",
-    )(ext, pix, odd, even, inputs[0], pltpu.with_memory_space_constraint(panels, pltpu.HBM))
+    )(ext, pix, above, below, inputs[0], pltpu.with_memory_space_constraint(panels, pltpu.HBM))
 
     column = [probe_low] + [
         lax.ppermute(probe_low, "grp", [(i, i ^ k) for i in range(n_grp)]) for k in distances(n_grp)[1:]

time: 41.3 us -> 41.5 us (level)
  blocking collectives: 22 us -> 21.4 us
  waiting for transfers between devices: 4.99 us -> 5.58 us
    ppermute x3, waiting for transfers between devices: 1.62 us -> 3.1 us  [on_device(): lax.ppermute(probe_low, 'grp', [(i, i ^ k) for i in range(n_grp)])]
    ppermute x2, waiting for transfers between devices: 3.38 us -> 2.48 us  [the longest x1 2.18 us: on_device(): lax.ppermute(down, 'grp', [(i, (i + 1) % n_grp) for i in range(n_grp)])]
    all_to_all x1, blocking collectives: 9.49 us -> 8.84 us  [on_device(): lax.all_to_all(partial, ('grp', 'tile'), split_axis=0, concat_axis=0, til...]
where the time goes in v10:
time: 41.5 us; the launch traced here: 41.3 us
  blocking collectives  21.4 us (52%)
  starting transfers between devices  6.9 us (17%)
  Pallas kernels  6.76 us (16%)
  waiting for transfers between devices  5.58 us (13%)
  between operations  0.67 us (2%)
    all_to_all x1, blocking collectives, on_device(): got = lax.all_to_all(slots, 'tile', split_axis=0, concat_axis=0, tiled=True)  12.5 us
    all_to_all x1, blocking collectives, on_device(): lax.all_to_all(partial, ('grp', 'tile'), split_axis=0, concat_axis=0, til...  8.84 us
    pallas_call x1, Pallas kernels, on_device(): pl.pallas_call(functools.partial(solve_kernel, n_grp, n_tile), out_shape=...  3.95 us
    ppermute x3, starting transfers between devices, on_device(): lax.ppermute(probe_low, 'grp', [(i, i ^ k) for i in range(n_grp)])  3.92 us
    ppermute x3, waiting for transfers between devices, on_device(): lax.ppermute(probe_low, 'grp', [(i, i ^ k) for i in range(n_grp)])  3.1 us
    ppermute x1, waiting for transfers between devices, on_device(): lax.ppermute(down, 'grp', [(i, (i + 1) % n_grp) for i in range(n_grp)])  2.18 us
    ppermute x1, starting transfers between devices, on_device(): lax.ppermute(down, 'grp', [(i, (i + 1) % n_grp) for i in range(n_grp)])  1.54 us
    ppermute x1, starting transfers between devices, on_device(): lax.ppermute(up, 'grp', [((i + 1) % n_grp, i) for i in range(n_grp)])  1.43 us
  transfers between devices with their start and end apart: 5, of which 5 were waited for; matrix products, arithmetic and copies ran while one was open for 0% of the time, Pallas kernels for 2%

profile of v10, /device:TPU:0, one launch (start us, length us, event | category | flops | bytes accessed | tf_op | source)
XLA Modules:
  0.0 41.3 jit_solution(12189566625452894450)
XLA Ops:
  0.6 1.1 %pack_tiles.1 = (bf16[8,48,128]{2,1,0:T(8,128)(2,1)S(1)}, f32[4,64,128]{2,1,0:T(8,128)S(1)}) custom-call(f32[2,64,128]{2,1,0:T(8,128)} %bv_hbm.1, f32[64,128]{1,0:T(8,128)} %refs_1_.1, f32[64,128]{1,0:T(8,128)} %refs_2_.1, f32[64,128]{1,0:T(8,128)} %refs_3_.1, f32[1,1,2,512]{3,2,1,0:T(2,128)} %refs_4_.1, f32[1,1,1,512]{3,2,1,0:T(1,128)} %refs_5_.1, ...), custom_call_target="tpu_custom_call" | custom-call | tf_op jit(solution)/shard_map/pack_tiles/pallas_call | solution.py:460
  1.8 12.5 %all_to_all.10.got_ref = bf16[8,48,128]{2,1,0:T(8,128)(2,1)S(1)} all-to-all(bf16[8,48,128]{2,1,0:T(8,128)(2,1)S(1)} %get-tuple-element.16), channel_id=1, replica_groups=mesh['grp'=4,'tile'=8] {'tile'}, dimensions={0} | all-to-all | bytes 196608 | tf_op jit(solution)/shard_map/all_to_all | solution.py:472
  14.3 0.2 pack_rows.1
  14.5 1.5 %collective-permute-start = (bf16[128,128]{1,0:T(8,128)(2,1)S(1)}, bf16[128,128]{1,0:T(8,128)(2,1)S(1)}, u32[]{:S(2)}, u32[]{:S(2)}) collective-permute-start(bf16[128,128]{1,0:T(8,128)(2,1)S(1)} %get-tuple-element.19), channel_id=1, source_target_pairs={{0,8},{8,16},{16,24},{24,0},{1,9},{9,17},{17,25},{25,1},{2,10},{10... | collective-permute-start | bytes 98312 | tf_op jit(solution)/shard_map/ppermute | solution.py:488
  16.0 1.4 %collective-permute-start.1 = (bf16[128,128]{1,0:T(8,128)(2,1)S(1)}, bf16[128,128]{1,0:T(8,128)(2,1)S(1)}, u32[]{:S(2)}, u32[]{:S(2)}) collective-permute-start(bf16[128,128]{1,0:T(8,128)(2,1)S(1)} %get-tuple-element.20), channel_id=1, source_target_pairs={{8,0},{16,8},{24,16},{0,24},{9,1},{17,9},{25,17},{1,25},{10,2},{18... | collective-permute-start | bytes 98312 | tf_op jit(solution)/shard_map/ppermute | solution.py:489
  17.5 2.2 %collective-permute-done.above_ref = bf16[128,128]{1,0:T(8,128)(2,1)S(1)} collective-permute-done((bf16[128,128]{1,0:T(8,128)(2,1)S(1)}, bf16[128,128]{1,0:T(8,128)(2,1)S(1)}, u32[]{:S(2)}, u32[]{:S(2)}) %collective-permute-start) | collective-permute-done | bytes 32800 | tf_op jit(solution)/shard_map/ppermute | solution.py:488
  19.7 0.3 collective-permute-done.1.below_ref
  20.0 4.0 %solve.1 = (f32[2,64,128]{2,1,0:T(8,128)}, f32[64,128]{1,0:T(8,128)S(1)}, bf16[64,128]{1,0:T(8,128)(2,1)S(1)}, bf16[32,4,64,128]{3,2,1,0:T(8,128)(2,1)S(1)}) custom-call(f32[4,64,256]{2,1,0:T(8,128)S(1)} %get-tuple-element.17.ext_ref, f32[48,128]{1,0:T(8,128)S(1)} %get-tuple-element.18.pix_ref, bf16[128,128]{1,0:T(8,128)(2,1)S(1)} %collective-permute-done.above_ref, ...), custom_call_target="tpu_custom_call" | custom-call | tf_op jit(solution)/shard_map/solve/pallas_call | solution.py:491
  23.9 2.4 %collective-permute-start.3 = (bf16[64,128]{1,0:T(8,128)(2,1)S(1)}, bf16[64,128]{1,0:T(8,128)(2,1)S(1)}, u32[]{:S(2)}, u32[]{:S(2)}) collective-permute-start(bf16[64,128]{1,0:T(8,128)(2,1)S(1)} %get-tuple-element.24.refs_0_), channel_id=1, source_target_pairs={{0,24},{8,16},{16,8},{24,0},{1,25},{9,17},{17,9},{25,1},{2,26},{10... | collective-permute-start | bytes 49160 | tf_op jit(solution)/shard_map/ppermute | solution.py:517
  26.3 1.5 %collective-permute-start.2 = (bf16[64,128]{1,0:T(8,128)(2,1)S(1)}, bf16[64,128]{1,0:T(8,128)(2,1)S(1)}, u32[]{:S(2)}, u32[]{:S(2)}) collective-permute-start(bf16[64,128]{1,0:T(8,128)(2,1)S(1)} %get-tuple-element.24.refs_0_), channel_id=1, source_target_pairs={{0,16},{8,24},{16,0},{24,8},{1,17},{9,25},{17,1},{25,9},{2,18},{10... | collective-permute-start | bytes 49160 | tf_op jit(solution)/shard_map/ppermute | solution.py:517
  27.8 0.0 collective-permute-start.4
  27.8 0.8 %collective-permute-done.3.refs_2_ = bf16[64,128]{1,0:T(8,128)(2,1)S(1)} collective-permute-done((bf16[64,128]{1,0:T(8,128)(2,1)S(1)}, bf16[64,128]{1,0:T(8,128)(2,1)S(1)}, u32[]{:S(2)}, u32[]{:S(2)}) %collective-permute-start.3) | collective-permute-done | bytes 16416 | tf_op jit(solution)/shard_map/ppermute | solution.py:517
  28.6 1.4 %collective-permute-done.2.refs_1_ = bf16[64,128]{1,0:T(8,128)(2,1)S(1)} collective-permute-done((bf16[64,128]{1,0:T(8,128)(2,1)S(1)}, bf16[64,128]{1,0:T(8,128)(2,1)S(1)}, u32[]{:S(2)}, u32[]{:S(2)}) %collective-permute-start.2) | collective-permute-done | bytes 16416 | tf_op jit(solution)/shard_map/ppermute | solution.py:517
  30.1 0.6 %project.1 = (f32[32,8,128]{2,1,0:T(8,128)S(1)}, f32[64,128]{1,0:T(8,128)}) custom-call(bf16[32,4,64,128]{3,2,1,0:T(8,128)(2,1)S(1)} %get-tuple-element.22.panels_ref, f32[64,128]{1,0:T(8,128)S(1)} %get-tuple-element.23.hess_ref, bf16[64,128]{1,0:T(8,128)(2,1)S(1)} %get-tuple-element.24.refs_0_, bf16[64,128]{1,0:T(8,128)(2,1)S(1)} %collective-permute-done.2.refs_1_, ...), custom_call_target="tpu_custom_call" | custom-call | flops 1572864 | bytes 2097152 | tf_op jit(solution)/shard_map/project/pallas_call | solution.py:519
  30.7 0.9 %collective-permute-done.4.block_ref = bf16[64,128]{1,0:T(8,128)(2,1)S(1)} collective-permute-done((bf16[64,128]{1,0:T(8,128)(2,1)S(1)}, bf16[64,128]{1,0:T(8,128)(2,1)S(1)}, u32[]{:S(2)}, u32[]{:S(2)}) %collective-permute-start.4) | collective-permute-done | bytes 16416 | tf_op jit(solution)/shard_map/ppermute | solution.py:517
  31.6 0.3 project_last.1
  31.9 8.8 %all_to_all.11.lines_ref = f32[32,1,128]{2,1,0:T(1,128)S(1)} all-to-all(f32[32,1,128]{2,1,0:T(1,128)S(1)} %project_last.1), channel_id=1, replica_groups=mesh['grp'=4,'tile'=8] {'grp','tile'}, dimensions={0} | all-to-all | bytes 32768 | tf_op jit(solution)/shard_map/all_to_all | solution.py:542
  40.8 0.5 %add_lines.1 = f32[1,128]{1,0:T(1,128)} custom-call(f32[32,1,128]{2,1,0:T(1,128)S(1)} %all_to_all.11.lines_ref), custom_call_target="tpu_custom_call" | custom-call | tf_op jit(solution)/shard_map/add_lines/pallas_call | solution.py:543
Async XLA Ops:
  14.5 5.2 %collective-permute-start = (bf16[128,128]{1,0:T(8,128)(2,1)S(1)}, bf16[128,128]{1,0:T(8,128)(2,1)S(1)}, u32[]{:S(2)}, u32[]{:S(2)}) collective-permute-start(bf16[128,128]{1,0:T(8,128)(2,1)S(1)} %get-tuple-element.19), channel_id=1, source_target_pairs={{0,8},{8,16},{16,24},{24,0},{1,9},{9,17},{17,25},{25,1},{2,10},{10... | collective-permute-start | bytes 98312 | tf_op jit(solution)/shard_map/ppermute | solution.py:488
  16.0 3.9 %collective-permute-start.1 = (bf16[128,128]{1,0:T(8,128)(2,1)S(1)}, bf16[128,128]{1,0:T(8,128)(2,1)S(1)}, u32[]{:S(2)}, u32[]{:S(2)}) collective-permute-start(bf16[128,128]{1,0:T(8,128)(2,1)S(1)} %get-tuple-element.20), channel_id=1, source_target_pairs={{8,0},{16,8},{24,16},{0,24},{9,1},{17,9},{25,17},{1,25},{10,2},{18... | collective-permute-start | bytes 98312 | tf_op jit(solution)/shard_map/ppermute | solution.py:489
  23.9 4.7 %collective-permute-start.3 = (bf16[64,128]{1,0:T(8,128)(2,1)S(1)}, bf16[64,128]{1,0:T(8,128)(2,1)S(1)}, u32[]{:S(2)}, u32[]{:S(2)}) collective-permute-start(bf16[64,128]{1,0:T(8,128)(2,1)S(1)} %get-tuple-element.24.refs_0_), channel_id=1, source_target_pairs={{0,24},{8,16},{16,8},{24,0},{1,25},{9,17},{17,9},{25,1},{2,26},{10... | collective-permute-start | bytes 49160 | tf_op jit(solution)/shard_map/ppermute | solution.py:517
  26.3 3.7 %collective-permute-start.2 = (bf16[64,128]{1,0:T(8,128)(2,1)S(1)}, bf16[64,128]{1,0:T(8,128)(2,1)S(1)}, u32[]{:S(2)}, u32[]{:S(2)}) collective-permute-start(bf16[64,128]{1,0:T(8,128)(2,1)S(1)} %get-tuple-element.24.refs_0_), channel_id=1, source_target_pairs={{0,16},{8,24},{16,0},{24,8},{1,17},{9,25},{17,1},{25,9},{2,18},{10... | collective-permute-start | bytes 49160 | tf_op jit(solution)/shard_map/ppermute | solution.py:517
  27.8 3.7 %collective-permute-start.4 = (bf16[64,128]{1,0:T(8,128)(2,1)S(1)}, bf16[64,128]{1,0:T(8,128)(2,1)S(1)}, u32[]{:S(2)}, u32[]{:S(2)}) collective-permute-start(bf16[64,128]{1,0:T(8,128)(2,1)S(1)} %get-tuple-element.24.refs_0_), channel_id=1, source_target_pairs={{0,8},{8,0},{16,24},{24,16},{1,9},{9,1},{17,25},{25,17},{2,10},{10... | collective-permute-start | bytes 49160 | tf_op jit(solution)/shard_map/ppermute | solution.py:517

commit v11 on v9

--- a/solution.py
+++ b/solution.py
@@ -93,13 +93,8 @@
                 packed = jnp.where((lane >= start) & (lane < start + HALO), piece, packed)
         return packed
 
-    @pl.when(t < n_tile - 1)
-    def _():
-        out_ref[t + 1, 0:half, :] = fold(128 - HALO).astype(BF16)
-
-    @pl.when(t > 0)
-    def _():
-        out_ref[t - 1, 0:half, :] = fold(0).astype(BF16)
+    out_ref[jnp.minimum(t + 1, n_tile - 1), 0:half, :] = fold(128 - HALO).astype(BF16)
+    out_ref[jnp.maximum(t - 1, 0), 0:half, :] = fold(0).astype(BF16)
 
 
 def pack_rows_kernel(n_tile, fields_ref, got_ref, ext_ref, pix_ref, even_ref, odd_ref):

time: 41.3 us -> 41.2 us (level)
  no operation moved by 1% of the time
where the time goes in v11:
time: 41.2 us; the launch traced here: 41 us
  blocking collectives  22 us (53%)
  Pallas kernels  6.77 us (16%)
  starting transfers between devices  6.6 us (16%)
  waiting for transfers between devices  4.99 us (12%)
  between operations  0.67 us (2%)
    all_to_all x1, blocking collectives, on_device(): got = lax.all_to_all(slots, 'tile', split_axis=0, concat_axis=0, tiled=True)  12.5 us
    all_to_all x1, blocking collectives, on_device(): lax.all_to_all(partial, ('grp', 'tile'), split_axis=0, concat_axis=0, til...  9.49 us
    pallas_call x1, Pallas kernels, on_device(): pl.pallas_call(functools.partial(solve_kernel, n_grp, n_tile), out_shape=...  3.95 us
    ppermute x3, starting transfers between devices, on_device(): lax.ppermute(probe_low, 'grp', [(i, i ^ k) for i in range(n_grp)])  3.55 us
    ppermute x1, starting transfers between devices, on_device(): lax.ppermute(odd, 'grp', [(i, (i - 1 + 2 * (i % 2)) % n_grp) for i in ran...  2.51 us
    ppermute x1, waiting for transfers between devices, on_device(): lax.ppermute(odd, 'grp', [(i, (i - 1 + 2 * (i % 2)) % n_grp) for i in ran...  2.06 us
    ppermute x3, waiting for transfers between devices, on_device(): lax.ppermute(probe_low, 'grp', [(i, i ^ k) for i in range(n_grp)])  1.62 us
    ppermute x1, waiting for transfers between devices, on_device(): even = lax.ppermute(even, 'grp', [(i, i ^ 1) for i in range(n_grp)])  1.32 us
  transfers between devices with their start and end apart: 5, of which 5 were waited for; matrix products, arithmetic and copies ran while one was open for 0% of the time, Pallas kernels for 2%

profile of v11, /device:TPU:0, one launch (start us, length us, event | category | flops | bytes accessed | tf_op | source)
XLA Modules:
  0.0 41.0 jit_solution(2376182225259324336)
XLA Ops:
  0.6 1.1 %pack_tiles.1 = (bf16[8,48,128]{2,1,0:T(8,128)(2,1)S(1)}, f32[4,64,128]{2,1,0:T(8,128)S(1)}) custom-call(f32[2,64,128]{2,1,0:T(8,128)} %bv_hbm.1, f32[64,128]{1,0:T(8,128)} %refs_1_.1, f32[64,128]{1,0:T(8,128)} %refs_2_.1, f32[64,128]{1,0:T(8,128)} %refs_3_.1, f32[1,1,2,512]{3,2,1,0:T(2,128)} %refs_4_.1, f32[1,1,1,512]{3,2,1,0:T(1,128)} %refs_5_.1, ...), custom_call_target="tpu_custom_call" | custom-call | tf_op jit(solution)/shard_map/pack_tiles/pallas_call | solution.py:469
  1.8 12.5 %all_to_all.10.got_ref = bf16[8,48,128]{2,1,0:T(8,128)(2,1)S(1)} all-to-all(bf16[8,48,128]{2,1,0:T(8,128)(2,1)S(1)} %get-tuple-element.16), channel_id=1, replica_groups=mesh['grp'=4,'tile'=8] {'tile'}, dimensions={0} | all-to-all | bytes 196608 | tf_op jit(solution)/shard_map/all_to_all | solution.py:481
  14.2 0.2 pack_rows.1
  14.4 2.5 %collective-permute-start = (bf16[128,128]{1,0:T(8,128)(2,1)S(1)}, bf16[128,128]{1,0:T(8,128)(2,1)S(1)}, u32[]{:S(2)}, u32[]{:S(2)}) collective-permute-start(bf16[128,128]{1,0:T(8,128)(2,1)S(1)} %get-tuple-element.19), channel_id=1, source_target_pairs={{0,24},{8,16},{16,8},{24,0},{1,25},{9,17},{17,9},{25,1},{2,26},{10... | collective-permute-start | bytes 98312 | tf_op jit(solution)/shard_map/ppermute | solution.py:498
  16.9 0.5 %collective-permute-start.1 = (bf16[128,128]{1,0:T(8,128)(2,1)S(1)}, bf16[128,128]{1,0:T(8,128)(2,1)S(1)}, u32[]{:S(2)}, u32[]{:S(2)}) collective-permute-start(bf16[128,128]{1,0:T(8,128)(2,1)S(1)} %get-tuple-element.20), channel_id=1, source_target_pairs={{0,8},{8,0},{16,24},{24,16},{1,9},{9,1},{17,25},{25,17},{2,10},{10... | collective-permute-start | bytes 98312 | tf_op jit(solution)/shard_map/ppermute | solution.py:497
  17.5 2.1 %collective-permute-done.odd_ref = bf16[128,128]{1,0:T(8,128)(2,1)S(1)} collective-permute-done((bf16[128,128]{1,0:T(8,128)(2,1)S(1)}, bf16[128,128]{1,0:T(8,128)(2,1)S(1)}, u32[]{:S(2)}, u32[]{:S(2)}) %collective-permute-start) | collective-permute-done | bytes 32800 | tf_op jit(solution)/shard_map/ppermute | solution.py:498
  19.5 1.3 %collective-permute-done.1.even_ref = bf16[128,128]{1,0:T(8,128)(2,1)S(1)} collective-permute-done((bf16[128,128]{1,0:T(8,128)(2,1)S(1)}, bf16[128,128]{1,0:T(8,128)(2,1)S(1)}, u32[]{:S(2)}, u32[]{:S(2)}) %collective-permute-start.1) | collective-permute-done | bytes 32800 | tf_op jit(solution)/shard_map/ppermute | solution.py:497
  20.8 4.0 %solve.1 = (f32[2,64,128]{2,1,0:T(8,128)}, f32[64,128]{1,0:T(8,128)S(1)}, bf16[64,128]{1,0:T(8,128)(2,1)S(1)}, bf16[32,4,64,128]{3,2,1,0:T(8,128)(2,1)S(1)}) custom-call(f32[4,64,256]{2,1,0:T(8,128)S(1)} %get-tuple-element.17.ext_ref, f32[48,128]{1,0:T(8,128)S(1)} %get-tuple-element.18.pix_ref, bf16[128,128]{1,0:T(8,128)(2,1)S(1)} %collective-permute-done.odd_ref, ...), custom_call_target="tpu_custom_call" | custom-call | tf_op jit(solution)/shard_map/solve/pallas_call | solution.py:500
  24.8 1.0 %collective-permute-start.3 = (bf16[64,128]{1,0:T(8,128)(2,1)S(1)}, bf16[64,128]{1,0:T(8,128)(2,1)S(1)}, u32[]{:S(2)}, u32[]{:S(2)}) collective-permute-start(bf16[64,128]{1,0:T(8,128)(2,1)S(1)} %get-tuple-element.24.refs_0_), channel_id=1, source_target_pairs={{0,24},{8,16},{16,8},{24,0},{1,25},{9,17},{17,9},{25,1},{2,26},{10... | collective-permute-start | bytes 49160 | tf_op jit(solution)/shard_map/ppermute | solution.py:526
  25.8 1.1 %collective-permute-start.2 = (bf16[64,128]{1,0:T(8,128)(2,1)S(1)}, bf16[64,128]{1,0:T(8,128)(2,1)S(1)}, u32[]{:S(2)}, u32[]{:S(2)}) collective-permute-start(bf16[64,128]{1,0:T(8,128)(2,1)S(1)} %get-tuple-element.24.refs_0_), channel_id=1, source_target_pairs={{0,16},{8,24},{16,0},{24,8},{1,17},{9,25},{17,1},{25,9},{2,18},{10... | collective-permute-start | bytes 49160 | tf_op jit(solution)/shard_map/ppermute | solution.py:526
  26.9 1.5 %collective-permute-start.4 = (bf16[64,128]{1,0:T(8,128)(2,1)S(1)}, bf16[64,128]{1,0:T(8,128)(2,1)S(1)}, u32[]{:S(2)}, u32[]{:S(2)}) collective-permute-start(bf16[64,128]{1,0:T(8,128)(2,1)S(1)} %get-tuple-element.24.refs_0_), channel_id=1, source_target_pairs={{0,8},{8,0},{16,24},{24,16},{1,9},{9,1},{17,25},{25,17},{2,10},{10... | collective-permute-start | bytes 49160 | tf_op jit(solution)/shard_map/ppermute | solution.py:526
  28.4 1.2 %collective-permute-done.3.refs_2_ = bf16[64,128]{1,0:T(8,128)(2,1)S(1)} collective-permute-done((bf16[64,128]{1,0:T(8,128)(2,1)S(1)}, bf16[64,128]{1,0:T(8,128)(2,1)S(1)}, u32[]{:S(2)}, u32[]{:S(2)}) %collective-permute-start.3) | collective-permute-done | bytes 16416 | tf_op jit(solution)/shard_map/ppermute | solution.py:526
  29.5 0.2 collective-permute-done.2.refs_1_
  29.7 0.6 %project.1 = (f32[32,8,128]{2,1,0:T(8,128)S(1)}, f32[64,128]{1,0:T(8,128)}) custom-call(bf16[32,4,64,128]{3,2,1,0:T(8,128)(2,1)S(1)} %get-tuple-element.22.panels_ref, f32[64,128]{1,0:T(8,128)S(1)} %get-tuple-element.23.hess_ref, bf16[64,128]{1,0:T(8,128)(2,1)S(1)} %get-tuple-element.24.refs_0_, bf16[64,128]{1,0:T(8,128)(2,1)S(1)} %collective-permute-done.2.refs_1_, ...), custom_call_target="tpu_custom_call" | custom-call | flops 1572864 | bytes 2097152 | tf_op jit(solution)/shard_map/project/pallas_call | solution.py:528
  30.3 0.3 collective-permute-done.4.block_ref
  30.6 0.3 project_last.1
  30.9 9.5 %all_to_all.11.lines_ref = f32[32,1,128]{2,1,0:T(1,128)S(1)} all-to-all(f32[32,1,128]{2,1,0:T(1,128)S(1)} %project_last.1), channel_id=1, replica_groups=mesh['grp'=4,'tile'=8] {'grp','tile'}, dimensions={0} | all-to-all | bytes 32768 | tf_op jit(solution)/shard_map/all_to_all | solution.py:551
  40.4 0.5 %add_lines.1 = f32[1,128]{1,0:T(1,128)} custom-call(f32[32,1,128]{2,1,0:T(1,128)S(1)} %all_to_all.11.lines_ref), custom_call_target="tpu_custom_call" | custom-call | tf_op jit(solution)/shard_map/add_lines/pallas_call | solution.py:552
Async XLA Ops:
  14.4 5.1 %collective-permute-start = (bf16[128,128]{1,0:T(8,128)(2,1)S(1)}, bf16[128,128]{1,0:T(8,128)(2,1)S(1)}, u32[]{:S(2)}, u32[]{:S(2)}) collective-permute-start(bf16[128,128]{1,0:T(8,128)(2,1)S(1)} %get-tuple-element.19), channel_id=1, source_target_pairs={{0,24},{8,16},{16,8},{24,0},{1,25},{9,17},{17,9},{25,1},{2,26},{10... | collective-permute-start | bytes 98312 | tf_op jit(solution)/shard_map/ppermute | solution.py:498
  16.9 3.9 %collective-permute-start.1 = (bf16[128,128]{1,0:T(8,128)(2,1)S(1)}, bf16[128,128]{1,0:T(8,128)(2,1)S(1)}, u32[]{:S(2)}, u32[]{:S(2)}) collective-permute-start(bf16[128,128]{1,0:T(8,128)(2,1)S(1)} %get-tuple-element.20), channel_id=1, source_target_pairs={{0,8},{8,0},{16,24},{24,16},{1,9},{9,1},{17,25},{25,17},{2,10},{10... | collective-permute-start | bytes 98312 | tf_op jit(solution)/shard_map/ppermute | solution.py:497
  24.8 4.7 %collective-permute-start.3 = (bf16[64,128]{1,0:T(8,128)(2,1)S(1)}, bf16[64,128]{1,0:T(8,128)(2,1)S(1)}, u32[]{:S(2)}, u32[]{:S(2)}) collective-permute-start(bf16[64,128]{1,0:T(8,128)(2,1)S(1)} %get-tuple-element.24.refs_0_), channel_id=1, source_target_pairs={{0,24},{8,16},{16,8},{24,0},{1,25},{9,17},{17,9},{25,1},{2,26},{10... | collective-permute-start | bytes 49160 | tf_op jit(solution)/shard_map/ppermute | solution.py:526
  25.8 3.9 %collective-permute-start.2 = (bf16[64,128]{1,0:T(8,128)(2,1)S(1)}, bf16[64,128]{1,0:T(8,128)(2,1)S(1)}, u32[]{:S(2)}, u32[]{:S(2)}) collective-permute-start(bf16[64,128]{1,0:T(8,128)(2,1)S(1)} %get-tuple-element.24.refs_0_), channel_id=1, source_target_pairs={{0,16},{8,24},{16,0},{24,8},{1,17},{9,25},{17,1},{25,9},{2,18},{10... | collective-permute-start | bytes 49160 | tf_op jit(solution)/shard_map/ppermute | solution.py:526
  26.9 3.7 %collective-permute-start.4 = (bf16[64,128]{1,0:T(8,128)(2,1)S(1)}, bf16[64,128]{1,0:T(8,128)(2,1)S(1)}, u32[]{:S(2)}, u32[]{:S(2)}) collective-permute-start(bf16[64,128]{1,0:T(8,128)(2,1)S(1)} %get-tuple-element.24.refs_0_), channel_id=1, source_target_pairs={{0,8},{8,0},{16,24},{24,16},{1,9},{9,1},{17,25},{25,17},{2,10},{10... | collective-permute-start | bytes 49160 | tf_op jit(solution)/shard_map/ppermute | solution.py:526

commit v12 on v10

--- a/solution.py
+++ b/solution.py
@@ -93,13 +93,8 @@
                 packed = jnp.where((lane >= start) & (lane < start + HALO), piece, packed)
         return packed
 
-    @pl.when(t < n_tile - 1)
-    def _():
-        out_ref[t + 1, 0:half, :] = fold(128 - HALO).astype(BF16)
-
-    @pl.when(t > 0)
-    def _():
-        out_ref[t - 1, 0:half, :] = fold(0).astype(BF16)
+    out_ref[jnp.minimum(t + 1, n_tile - 1), 0:half, :] = fold(128 - HALO).astype(BF16)
+    out_ref[jnp.maximum(t - 1, 0), 0:half, :] = fold(0).astype(BF16)
 
 
 def pack_rows_kernel(n_tile, fields_ref, got_ref, ext_ref, pix_ref, up_ref, down_ref):
@@ -398,7 +393,7 @@
 
 
 def distances(n_grp):
-    return [0] + list(range(2, n_grp)) + [1]
+    return [0, 1] + list(range(3, n_grp)) + [2]
 
 
 def project_block(panels_ref, probe_ref, k, distance):

time: 41.5 us -> 42 us (1.012)
  blocking collectives: 21.4 us -> 22.7 us
  waiting for transfers between devices: 5.58 us -> 4.71 us
    all_to_all x1, blocking collectives: 8.84 us -> 10.2 us  [on_device(): lax.all_to_all(partial, ('grp', 'tile'), split_axis=0, concat_axis=0, til...]
    ppermute x3, waiting for transfers between devices: 3.1 us -> 2.23 us  [on_device(): lax.ppermute(probe_low, 'grp', [(i, i ^ k) for i in range(n_grp)])]
  transfers between devices with their start and end apart: 5 -> 5, of which waited for: 5 -> 4; matrix products, arithmetic and copies ran while one was open for 0% -> 0% of each run, Pallas kernels for 2% -> 1%
where the time goes in v12:
time: 42 us; the launch traced here: 41.8 us
  blocking collectives  22.7 us (54%)
  starting transfers between devices  6.9 us (16%)
  Pallas kernels  6.77 us (16%)
  waiting for transfers between devices  4.71 us (11%)
  between operations  0.67 us (2%)
    all_to_all x1, blocking collectives, on_device(): got = lax.all_to_all(slots, 'tile', split_axis=0, concat_axis=0, tiled=True)  12.5 us
    all_to_all x1, blocking collectives, on_device(): lax.all_to_all(partial, ('grp', 'tile'), split_axis=0, concat_axis=0, til...  10.2 us
    pallas_call x1, Pallas kernels, on_device(): pl.pallas_call(functools.partial(solve_kernel, n_grp, n_tile), out_shape=...  3.95 us
    ppermute x3, starting transfers between devices, on_device(): lax.ppermute(probe_low, 'grp', [(i, i ^ k) for i in range(n_grp)])  3.92 us
    ppermute x3, waiting for transfers between devices, on_device(): lax.ppermute(probe_low, 'grp', [(i, i ^ k) for i in range(n_grp)])  2.23 us
    ppermute x1, waiting for transfers between devices, on_device(): lax.ppermute(down, 'grp', [(i, (i + 1) % n_grp) for i in range(n_grp)])  2.18 us
    ppermute x1, starting transfers between devices, on_device(): lax.ppermute(down, 'grp', [(i, (i + 1) % n_grp) for i in range(n_grp)])  1.54 us
    ppermute x1, starting transfers between devices, on_device(): lax.ppermute(up, 'grp', [((i + 1) % n_grp, i) for i in range(n_grp)])  1.43 us
  transfers between devices with their start and end apart: 5, of which 4 were waited for; matrix products, arithmetic and copies ran while one was open for 0% of the time, Pallas kernels for 1%

profile of v12, /device:TPU:0, one launch (start us, length us, event | category | flops | bytes accessed | tf_op | source)
XLA Modules:
  0.0 41.8 jit_solution(6860804862896037500)
XLA Ops:
  0.6 1.1 %pack_tiles.1 = (bf16[8,48,128]{2,1,0:T(8,128)(2,1)S(1)}, f32[4,64,128]{2,1,0:T(8,128)S(1)}) custom-call(f32[2,64,128]{2,1,0:T(8,128)} %bv_hbm.1, f32[64,128]{1,0:T(8,128)} %refs_1_.1, f32[64,128]{1,0:T(8,128)} %refs_2_.1, f32[64,128]{1,0:T(8,128)} %refs_3_.1, f32[1,1,2,512]{3,2,1,0:T(2,128)} %refs_4_.1, f32[1,1,1,512]{3,2,1,0:T(1,128)} %refs_5_.1, ...), custom_call_target="tpu_custom_call" | custom-call | tf_op jit(solution)/shard_map/pack_tiles/pallas_call | solution.py:455
  1.8 12.5 %all_to_all.10.got_ref = bf16[8,48,128]{2,1,0:T(8,128)(2,1)S(1)} all-to-all(bf16[8,48,128]{2,1,0:T(8,128)(2,1)S(1)} %get-tuple-element.16), channel_id=1, replica_groups=mesh['grp'=4,'tile'=8] {'tile'}, dimensions={0} | all-to-all | bytes 196608 | tf_op jit(solution)/shard_map/all_to_all | solution.py:467
  14.2 0.2 pack_rows.1
  14.4 1.5 %collective-permute-start = (bf16[128,128]{1,0:T(8,128)(2,1)S(1)}, bf16[128,128]{1,0:T(8,128)(2,1)S(1)}, u32[]{:S(2)}, u32[]{:S(2)}) collective-permute-start(bf16[128,128]{1,0:T(8,128)(2,1)S(1)} %get-tuple-element.19), channel_id=1, source_target_pairs={{0,8},{8,16},{16,24},{24,0},{1,9},{9,17},{17,25},{25,1},{2,10},{10... | collective-permute-start | bytes 98312 | tf_op jit(solution)/shard_map/ppermute | solution.py:483
  16.0 1.4 %collective-permute-start.1 = (bf16[128,128]{1,0:T(8,128)(2,1)S(1)}, bf16[128,128]{1,0:T(8,128)(2,1)S(1)}, u32[]{:S(2)}, u32[]{:S(2)}) collective-permute-start(bf16[128,128]{1,0:T(8,128)(2,1)S(1)} %get-tuple-element.20), channel_id=1, source_target_pairs={{8,0},{16,8},{24,16},{0,24},{9,1},{17,9},{25,17},{1,25},{10,2},{18... | collective-permute-start | bytes 98312 | tf_op jit(solution)/shard_map/ppermute | solution.py:484
  17.4 2.2 %collective-permute-done.above_ref = bf16[128,128]{1,0:T(8,128)(2,1)S(1)} collective-permute-done((bf16[128,128]{1,0:T(8,128)(2,1)S(1)}, bf16[128,128]{1,0:T(8,128)(2,1)S(1)}, u32[]{:S(2)}, u32[]{:S(2)}) %collective-permute-start) | collective-permute-done | bytes 32800 | tf_op jit(solution)/shard_map/ppermute | solution.py:483
  19.6 0.3 collective-permute-done.1.below_ref
  19.9 4.0 %solve.1 = (f32[2,64,128]{2,1,0:T(8,128)}, f32[64,128]{1,0:T(8,128)S(1)}, bf16[64,128]{1,0:T(8,128)(2,1)S(1)}, bf16[32,4,64,128]{3,2,1,0:T(8,128)(2,1)S(1)}) custom-call(f32[4,64,256]{2,1,0:T(8,128)S(1)} %get-tuple-element.17.ext_ref, f32[48,128]{1,0:T(8,128)S(1)} %get-tuple-element.18.pix_ref, bf16[128,128]{1,0:T(8,128)(2,1)S(1)} %collective-permute-done.above_ref, ...), custom_call_target="tpu_custom_call" | custom-call | tf_op jit(solution)/shard_map/solve/pallas_call | solution.py:486
  23.8 2.4 %collective-permute-start.3 = (bf16[64,128]{1,0:T(8,128)(2,1)S(1)}, bf16[64,128]{1,0:T(8,128)(2,1)S(1)}, u32[]{:S(2)}, u32[]{:S(2)}) collective-permute-start(bf16[64,128]{1,0:T(8,128)(2,1)S(1)} %get-tuple-element.24.refs_0_), channel_id=1, source_target_pairs={{0,24},{8,16},{16,8},{24,0},{1,25},{9,17},{17,9},{25,1},{2,26},{10... | collective-permute-start | bytes 49160 | tf_op jit(solution)/shard_map/ppermute | solution.py:512
  26.2 0.6 %collective-permute-start.2 = (bf16[64,128]{1,0:T(8,128)(2,1)S(1)}, bf16[64,128]{1,0:T(8,128)(2,1)S(1)}, u32[]{:S(2)}, u32[]{:S(2)}) collective-permute-start(bf16[64,128]{1,0:T(8,128)(2,1)S(1)} %get-tuple-element.24.refs_0_), channel_id=1, source_target_pairs={{0,8},{8,0},{16,24},{24,16},{1,9},{9,1},{17,25},{25,17},{2,10},{10... | collective-permute-start | bytes 49160 | tf_op jit(solution)/shard_map/ppermute | solution.py:512
  26.9 0.9 %collective-permute-start.4 = (bf16[64,128]{1,0:T(8,128)(2,1)S(1)}, bf16[64,128]{1,0:T(8,128)(2,1)S(1)}, u32[]{:S(2)}, u32[]{:S(2)}) collective-permute-start(bf16[64,128]{1,0:T(8,128)(2,1)S(1)} %get-tuple-element.24.refs_0_), channel_id=1, source_target_pairs={{0,16},{8,24},{16,0},{24,8},{1,17},{9,25},{17,1},{25,9},{2,18},{10... | collective-permute-start | bytes 49160 | tf_op jit(solution)/shard_map/ppermute | solution.py:512
  27.8 0.8 %collective-permute-done.3.refs_2_ = bf16[64,128]{1,0:T(8,128)(2,1)S(1)} collective-permute-done((bf16[64,128]{1,0:T(8,128)(2,1)S(1)}, bf16[64,128]{1,0:T(8,128)(2,1)S(1)}, u32[]{:S(2)}, u32[]{:S(2)}) %collective-permute-start.3) | collective-permute-done | bytes 16416 | tf_op jit(solution)/shard_map/ppermute | solution.py:512
  28.5 1.4 %collective-permute-done.2.refs_1_ = bf16[64,128]{1,0:T(8,128)(2,1)S(1)} collective-permute-done((bf16[64,128]{1,0:T(8,128)(2,1)S(1)}, bf16[64,128]{1,0:T(8,128)(2,1)S(1)}, u32[]{:S(2)}, u32[]{:S(2)}) %collective-permute-start.2) | collective-permute-done | bytes 16416 | tf_op jit(solution)/shard_map/ppermute | solution.py:512
  30.0 0.6 %project.1 = (f32[32,8,128]{2,1,0:T(8,128)S(1)}, f32[64,128]{1,0:T(8,128)}) custom-call(bf16[32,4,64,128]{3,2,1,0:T(8,128)(2,1)S(1)} %get-tuple-element.22.panels_ref, f32[64,128]{1,0:T(8,128)S(1)} %get-tuple-element.23.hess_ref, bf16[64,128]{1,0:T(8,128)(2,1)S(1)} %get-tuple-element.24.refs_0_, bf16[64,128]{1,0:T(8,128)(2,1)S(1)} %collective-permute-done.2.refs_1_, ...), custom_call_target="tpu_custom_call" | custom-call | flops 1572864 | bytes 2097152 | tf_op jit(solution)/shard_map/project/pallas_call | solution.py:514
  30.6 0.0 collective-permute-done.4.block_ref
  30.6 0.3 project_last.1
  31.0 10.2 %all_to_all.11.lines_ref = f32[32,1,128]{2,1,0:T(1,128)S(1)} all-to-all(f32[32,1,128]{2,1,0:T(1,128)S(1)} %project_last.1), channel_id=1, replica_groups=mesh['grp'=4,'tile'=8] {'grp','tile'}, dimensions={0} | all-to-all | bytes 32768 | tf_op jit(solution)/shard_map/all_to_all | solution.py:537
  41.2 0.5 %add_lines.1 = f32[1,128]{1,0:T(1,128)} custom-call(f32[32,1,128]{2,1,0:T(1,128)S(1)} %all_to_all.11.lines_ref), custom_call_target="tpu_custom_call" | custom-call | tf_op jit(solution)/shard_map/add_lines/pallas_call | solution.py:538
Async XLA Ops:
  14.4 5.2 %collective-permute-start = (bf16[128,128]{1,0:T(8,128)(2,1)S(1)}, bf16[128,128]{1,0:T(8,128)(2,1)S(1)}, u32[]{:S(2)}, u32[]{:S(2)}) collective-permute-start(bf16[128,128]{1,0:T(8,128)(2,1)S(1)} %get-tuple-element.19), channel_id=1, source_target_pairs={{0,8},{8,16},{16,24},{24,0},{1,9},{9,17},{17,25},{25,1},{2,10},{10... | collective-permute-start | bytes 98312 | tf_op jit(solution)/shard_map/ppermute | solution.py:483
  16.0 3.9 %collective-permute-start.1 = (bf16[128,128]{1,0:T(8,128)(2,1)S(1)}, bf16[128,128]{1,0:T(8,128)(2,1)S(1)}, u32[]{:S(2)}, u32[]{:S(2)}) collective-permute-start(bf16[128,128]{1,0:T(8,128)(2,1)S(1)} %get-tuple-element.20), channel_id=1, source_target_pairs={{8,0},{16,8},{24,16},{0,24},{9,1},{17,9},{25,17},{1,25},{10,2},{18... | collective-permute-start | bytes 98312 | tf_op jit(solution)/shard_map/ppermute | solution.py:484
  23.8 4.7 %collective-permute-start.3 = (bf16[64,128]{1,0:T(8,128)(2,1)S(1)}, bf16[64,128]{1,0:T(8,128)(2,1)S(1)}, u32[]{:S(2)}, u32[]{:S(2)}) collective-permute-start(bf16[64,128]{1,0:T(8,128)(2,1)S(1)} %get-tuple-element.24.refs_0_), channel_id=1, source_target_pairs={{0,24},{8,16},{16,8},{24,0},{1,25},{9,17},{17,9},{25,1},{2,26},{10... | collective-permute-start | bytes 49160 | tf_op jit(solution)/shard_map/ppermute | solution.py:512
  26.2 3.7 %collective-permute-start.2 = (bf16[64,128]{1,0:T(8,128)(2,1)S(1)}, bf16[64,128]{1,0:T(8,128)(2,1)S(1)}, u32[]{:S(2)}, u32[]{:S(2)}) collective-permute-start(bf16[64,128]{1,0:T(8,128)(2,1)S(1)} %get-tuple-element.24.refs_0_), channel_id=1, source_target_pairs={{0,8},{8,0},{16,24},{24,16},{1,9},{9,1},{17,25},{25,17},{2,10},{10... | collective-permute-start | bytes 49160 | tf_op jit(solution)/shard_map/ppermute | solution.py:512
  26.9 3.7 %collective-permute-start.4 = (bf16[64,128]{1,0:T(8,128)(2,1)S(1)}, bf16[64,128]{1,0:T(8,128)(2,1)S(1)}, u32[]{:S(2)}, u32[]{:S(2)}) collective-permute-start(bf16[64,128]{1,0:T(8,128)(2,1)S(1)} %get-tuple-element.24.refs_0_), channel_id=1, source_target_pairs={{0,16},{8,24},{16,0},{24,8},{1,17},{9,25},{17,1},{25,9},{2,18},{10... | collective-permute-start | bytes 49160 | tf_op jit(solution)/shard_map/ppermute | solution.py:512

commit v13 on v11

--- a/solution.py
+++ b/solution.py
@@ -251,16 +251,16 @@
                 (east, west, north, south, 0.25 * node_pp, 0.25 * node_mm, 0.25 * node_pm, 0.25 * node_mp, inv_x, inv_y)
             ):
                 coef_ref[i, at, cols] = plane
-            src_ref[0, at, cols] = inv_x * strided(0, h, v)
-            src_ref[1, at, cols] = inv_y * strided(1, h, v)
+            for c, inv in ((0, inv_x), (1, inv_y)):
+                scaled = inv * strided(c, h, v)
+                src_ref[c, at, cols] = scaled
+                w_ref[0, c, at, cols] = scaled
         prev, cur = cur, nxt
 
     def natural(h, v):
         return (h, pl.ds(v, STRIPS, stride=groups), slice(None))
 
     def relax():
-        w_ref[0] = src_ref[...]
-
         def sweep(now, later, start):
             rows_seen = {}
 
@@ -395,7 +395,9 @@
             for h in range(2):
                 cols = pl.ds(h * 128, 128)
                 for c in range(2):
-                    src_ref[c, at, cols] = coef_ref[8 + c, at, cols] * nat_ref[(c,) + natural(h, v)]
+                    scaled = coef_ref[8 + c, at, cols] * nat_ref[(c,) + natural(h, v)]
+                    src_ref[c, at, cols] = scaled
+                    w_ref[0, c, at, cols] = scaled
 
     lax.fori_loop(0, 2, solve, 0)
     for copy in copies:

time: 41.2 us -> 41.2 us (level)
  no operation moved by 1% of the time
where the time goes in v13:
time: 41.2 us; the launch traced here: 41 us
  blocking collectives  22 us (53%)
  Pallas kernels  6.75 us (16%)
  starting transfers between devices  6.6 us (16%)
  waiting for transfers between devices  4.99 us (12%)
  between operations  0.67 us (2%)
    all_to_all x1, blocking collectives, on_device(): got = lax.all_to_all(slots, 'tile', split_axis=0, concat_axis=0, tiled=True)  12.5 us
    all_to_all x1, blocking collectives, on_device(): lax.all_to_all(partial, ('grp', 'tile'), split_axis=0, concat_axis=0, til...  9.5 us
    pallas_call x1, Pallas kernels, on_device(): pl.pallas_call(functools.partial(solve_kernel, n_grp, n_tile), out_shape=...  3.93 us
    ppermute x3, starting transfers between devices, on_device(): lax.ppermute(probe_low, 'grp', [(i, i ^ k) for i in range(n_grp)])  3.55 us
    ppermute x1, starting transfers between devices, on_device(): lax.ppermute(odd, 'grp', [(i, (i - 1 + 2 * (i % 2)) % n_grp) for i in ran...  2.51 us
    ppermute x1, waiting for transfers between devices, on_device(): lax.ppermute(odd, 'grp', [(i, (i - 1 + 2 * (i % 2)) % n_grp) for i in ran...  2.06 us
    ppermute x3, waiting for transfers between devices, on_device(): lax.ppermute(probe_low, 'grp', [(i, i ^ k) for i in range(n_grp)])  1.61 us
    ppermute x1, waiting for transfers between devices, on_device(): even = lax.ppermute(even, 'grp', [(i, i ^ 1) for i in range(n_grp)])  1.32 us
  transfers between devices with their start and end apart: 5, of which 5 were waited for; matrix products, arithmetic and copies ran while one was open for 0% of the time, Pallas kernels for 2%

profile of v13, /device:TPU:0, one launch (start us, length us, event | category | flops | bytes accessed | tf_op | source)
XLA Modules:
  0.0 41.0 jit_solution(8468076892285856098)
XLA Ops:
  0.6 1.1 %pack_tiles.1 = (bf16[8,48,128]{2,1,0:T(8,128)(2,1)S(1)}, f32[4,64,128]{2,1,0:T(8,128)S(1)}) custom-call(f32[2,64,128]{2,1,0:T(8,128)} %bv_hbm.1, f32[64,128]{1,0:T(8,128)} %refs_1_.1, f32[64,128]{1,0:T(8,128)} %refs_2_.1, f32[64,128]{1,0:T(8,128)} %refs_3_.1, f32[1,1,2,512]{3,2,1,0:T(2,128)} %refs_4_.1, f32[1,1,1,512]{3,2,1,0:T(1,128)} %refs_5_.1, ...), custom_call_target="tpu_custom_call" | custom-call | tf_op jit(solution)/shard_map/pack_tiles/pallas_call | solution.py:471
  1.8 12.5 %all_to_all.10.got_ref = bf16[8,48,128]{2,1,0:T(8,128)(2,1)S(1)} all-to-all(bf16[8,48,128]{2,1,0:T(8,128)(2,1)S(1)} %get-tuple-element.16), channel_id=1, replica_groups=mesh['grp'=4,'tile'=8] {'tile'}, dimensions={0} | all-to-all | bytes 196608 | tf_op jit(solution)/shard_map/all_to_all | solution.py:483
  14.2 0.2 pack_rows.1
  14.4 2.5 %collective-permute-start = (bf16[128,128]{1,0:T(8,128)(2,1)S(1)}, bf16[128,128]{1,0:T(8,128)(2,1)S(1)}, u32[]{:S(2)}, u32[]{:S(2)}) collective-permute-start(bf16[128,128]{1,0:T(8,128)(2,1)S(1)} %get-tuple-element.19), channel_id=1, source_target_pairs={{0,24},{8,16},{16,8},{24,0},{1,25},{9,17},{17,9},{25,1},{2,26},{10... | collective-permute-start | bytes 98312 | tf_op jit(solution)/shard_map/ppermute | solution.py:500
  16.9 0.5 %collective-permute-start.1 = (bf16[128,128]{1,0:T(8,128)(2,1)S(1)}, bf16[128,128]{1,0:T(8,128)(2,1)S(1)}, u32[]{:S(2)}, u32[]{:S(2)}) collective-permute-start(bf16[128,128]{1,0:T(8,128)(2,1)S(1)} %get-tuple-element.20), channel_id=1, source_target_pairs={{0,8},{8,0},{16,24},{24,16},{1,9},{9,1},{17,25},{25,17},{2,10},{10... | collective-permute-start | bytes 98312 | tf_op jit(solution)/shard_map/ppermute | solution.py:499
  17.5 2.1 %collective-permute-done.odd_ref = bf16[128,128]{1,0:T(8,128)(2,1)S(1)} collective-permute-done((bf16[128,128]{1,0:T(8,128)(2,1)S(1)}, bf16[128,128]{1,0:T(8,128)(2,1)S(1)}, u32[]{:S(2)}, u32[]{:S(2)}) %collective-permute-start) | collective-permute-done | bytes 32800 | tf_op jit(solution)/shard_map/ppermute | solution.py:500
  19.5 1.3 %collective-permute-done.1.even_ref = bf16[128,128]{1,0:T(8,128)(2,1)S(1)} collective-permute-done((bf16[128,128]{1,0:T(8,128)(2,1)S(1)}, bf16[128,128]{1,0:T(8,128)(2,1)S(1)}, u32[]{:S(2)}, u32[]{:S(2)}) %collective-permute-start.1) | collective-permute-done | bytes 32800 | tf_op jit(solution)/shard_map/ppermute | solution.py:499
  20.8 3.9 %solve.1 = (f32[2,64,128]{2,1,0:T(8,128)}, f32[64,128]{1,0:T(8,128)S(1)}, bf16[64,128]{1,0:T(8,128)(2,1)S(1)}, bf16[32,4,64,128]{3,2,1,0:T(8,128)(2,1)S(1)}) custom-call(f32[4,64,256]{2,1,0:T(8,128)S(1)} %get-tuple-element.17.ext_ref, f32[48,128]{1,0:T(8,128)S(1)} %get-tuple-element.18.pix_ref, bf16[128,128]{1,0:T(8,128)(2,1)S(1)} %collective-permute-done.odd_ref, ...), custom_call_target="tpu_custom_call" | custom-call | tf_op jit(solution)/shard_map/solve/pallas_call | solution.py:502
  24.8 1.0 %collective-permute-start.3 = (bf16[64,128]{1,0:T(8,128)(2,1)S(1)}, bf16[64,128]{1,0:T(8,128)(2,1)S(1)}, u32[]{:S(2)}, u32[]{:S(2)}) collective-permute-start(bf16[64,128]{1,0:T(8,128)(2,1)S(1)} %get-tuple-element.24.refs_0_), channel_id=1, source_target_pairs={{0,24},{8,16},{16,8},{24,0},{1,25},{9,17},{17,9},{25,1},{2,26},{10... | collective-permute-start | bytes 49160 | tf_op jit(solution)/shard_map/ppermute | solution.py:528
  25.8 1.1 %collective-permute-start.2 = (bf16[64,128]{1,0:T(8,128)(2,1)S(1)}, bf16[64,128]{1,0:T(8,128)(2,1)S(1)}, u32[]{:S(2)}, u32[]{:S(2)}) collective-permute-start(bf16[64,128]{1,0:T(8,128)(2,1)S(1)} %get-tuple-element.24.refs_0_), channel_id=1, source_target_pairs={{0,16},{8,24},{16,0},{24,8},{1,17},{9,25},{17,1},{25,9},{2,18},{10... | collective-permute-start | bytes 49160 | tf_op jit(solution)/shard_map/ppermute | solution.py:528
  26.8 1.5 %collective-permute-start.4 = (bf16[64,128]{1,0:T(8,128)(2,1)S(1)}, bf16[64,128]{1,0:T(8,128)(2,1)S(1)}, u32[]{:S(2)}, u32[]{:S(2)}) collective-permute-start(bf16[64,128]{1,0:T(8,128)(2,1)S(1)} %get-tuple-element.24.refs_0_), channel_id=1, source_target_pairs={{0,8},{8,0},{16,24},{24,16},{1,9},{9,1},{17,25},{25,17},{2,10},{10... | collective-permute-start | bytes 49160 | tf_op jit(solution)/shard_map/ppermute | solution.py:528
  28.3 1.2 %collective-permute-done.3.refs_2_ = bf16[64,128]{1,0:T(8,128)(2,1)S(1)} collective-permute-done((bf16[64,128]{1,0:T(8,128)(2,1)S(1)}, bf16[64,128]{1,0:T(8,128)(2,1)S(1)}, u32[]{:S(2)}, u32[]{:S(2)}) %collective-permute-start.3) | collective-permute-done | bytes 16416 | tf_op jit(solution)/shard_map/ppermute | solution.py:528
  29.5 0.2 collective-permute-done.2.refs_1_
  29.7 0.6 %project.1 = (f32[32,8,128]{2,1,0:T(8,128)S(1)}, f32[64,128]{1,0:T(8,128)}) custom-call(bf16[32,4,64,128]{3,2,1,0:T(8,128)(2,1)S(1)} %get-tuple-element.22.panels_ref, f32[64,128]{1,0:T(8,128)S(1)} %get-tuple-element.23.hess_ref, bf16[64,128]{1,0:T(8,128)(2,1)S(1)} %get-tuple-element.24.refs_0_, bf16[64,128]{1,0:T(8,128)(2,1)S(1)} %collective-permute-done.2.refs_1_, ...), custom_call_target="tpu_custom_call" | custom-call | flops 1572864 | bytes 2097152 | tf_op jit(solution)/shard_map/project/pallas_call | solution.py:530
  30.3 0.3 collective-permute-done.4.block_ref
  30.6 0.3 project_last.1
  30.9 9.5 %all_to_all.11.lines_ref = f32[32,1,128]{2,1,0:T(1,128)S(1)} all-to-all(f32[32,1,128]{2,1,0:T(1,128)S(1)} %project_last.1), channel_id=1, replica_groups=mesh['grp'=4,'tile'=8] {'grp','tile'}, dimensions={0} | all-to-all | bytes 32768 | tf_op jit(solution)/shard_map/all_to_all | solution.py:553
  40.4 0.5 %add_lines.1 = f32[1,128]{1,0:T(1,128)} custom-call(f32[32,1,128]{2,1,0:T(1,128)S(1)} %all_to_all.11.lines_ref), custom_call_target="tpu_custom_call" | custom-call | tf_op jit(solution)/shard_map/add_lines/pallas_call | solution.py:554
Async XLA Ops:
  14.4 5.1 %collective-permute-start = (bf16[128,128]{1,0:T(8,128)(2,1)S(1)}, bf16[128,128]{1,0:T(8,128)(2,1)S(1)}, u32[]{:S(2)}, u32[]{:S(2)}) collective-permute-start(bf16[128,128]{1,0:T(8,128)(2,1)S(1)} %get-tuple-element.19), channel_id=1, source_target_pairs={{0,24},{8,16},{16,8},{24,0},{1,25},{9,17},{17,9},{25,1},{2,26},{10... | collective-permute-start | bytes 98312 | tf_op jit(solution)/shard_map/ppermute | solution.py:500
  16.9 3.9 %collective-permute-start.1 = (bf16[128,128]{1,0:T(8,128)(2,1)S(1)}, bf16[128,128]{1,0:T(8,128)(2,1)S(1)}, u32[]{:S(2)}, u32[]{:S(2)}) collective-permute-start(bf16[128,128]{1,0:T(8,128)(2,1)S(1)} %get-tuple-element.20), channel_id=1, source_target_pairs={{0,8},{8,0},{16,24},{24,16},{1,9},{9,1},{17,25},{25,17},{2,10},{10... | collective-permute-start | bytes 98312 | tf_op jit(solution)/shard_map/ppermute | solution.py:499
  24.8 4.7 %collective-permute-start.3 = (bf16[64,128]{1,0:T(8,128)(2,1)S(1)}, bf16[64,128]{1,0:T(8,128)(2,1)S(1)}, u32[]{:S(2)}, u32[]{:S(2)}) collective-permute-start(bf16[64,128]{1,0:T(8,128)(2,1)S(1)} %get-tuple-element.24.refs_0_), channel_id=1, source_target_pairs={{0,24},{8,16},{16,8},{24,0},{1,25},{9,17},{17,9},{25,1},{2,26},{10... | collective-permute-start | bytes 49160 | tf_op jit(solution)/shard_map/ppermute | solution.py:528
  25.8 3.9 %collective-permute-start.2 = (bf16[64,128]{1,0:T(8,128)(2,1)S(1)}, bf16[64,128]{1,0:T(8,128)(2,1)S(1)}, u32[]{:S(2)}, u32[]{:S(2)}) collective-permute-start(bf16[64,128]{1,0:T(8,128)(2,1)S(1)} %get-tuple-element.24.refs_0_), channel_id=1, source_target_pairs={{0,16},{8,24},{16,0},{24,8},{1,17},{9,25},{17,1},{25,9},{2,18},{10... | collective-permute-start | bytes 49160 | tf_op jit(solution)/shard_map/ppermute | solution.py:528
  26.8 3.7 %collective-permute-start.4 = (bf16[64,128]{1,0:T(8,128)(2,1)S(1)}, bf16[64,128]{1,0:T(8,128)(2,1)S(1)}, u32[]{:S(2)}, u32[]{:S(2)}) collective-permute-start(bf16[64,128]{1,0:T(8,128)(2,1)S(1)} %get-tuple-element.24.refs_0_), channel_id=1, source_target_pairs={{0,8},{8,0},{16,24},{24,16},{1,9},{9,1},{17,25},{25,17},{2,10},{10... | collective-permute-start | bytes 49160 | tf_op jit(solution)/shard_map/ppermute | solution.py:528

commit v14 on v11

--- a/solution.py
+++ b/solution.py
@@ -356,7 +356,7 @@
 
         nat_ref[...] = jnp.zeros_like(nat_ref)
         for two_parts, h, first, size, begin, count, lane_of, los_x, los_y, r, stacked in jobs:
-            chunk = 4 if h == 0 else 8
+            chunk = 4
             depth = 128 if h == 0 else 2 * EDGE
             wide = chunk * 128
             row_id = lax.broadcasted_iota(jnp.int32, (size, wide), 0).astype(F32)

time: 41.2 us -> 41.2 us (level)
  no operation moved by 1% of the time
where the time goes in v14:
time: 41.2 us; the launch traced here: 41 us
  blocking collectives  22 us (53%)
  Pallas kernels  6.79 us (16%)
  starting transfers between devices  6.6 us (16%)
  waiting for transfers between devices  4.99 us (12%)
  between operations  0.67 us (2%)
    all_to_all x1, blocking collectives, on_device(): got = lax.all_to_all(slots, 'tile', split_axis=0, concat_axis=0, tiled=True)  12.5 us
    all_to_all x1, blocking collectives, on_device(): lax.all_to_all(partial, ('grp', 'tile'), split_axis=0, concat_axis=0, til...  9.49 us
    pallas_call x1, Pallas kernels, on_device(): pl.pallas_call(functools.partial(solve_kernel, n_grp, n_tile), out_shape=...  3.97 us
    ppermute x3, starting transfers between devices, on_device(): lax.ppermute(probe_low, 'grp', [(i, i ^ k) for i in range(n_grp)])  3.55 us
    ppermute x1, starting transfers between devices, on_device(): lax.ppermute(odd, 'grp', [(i, (i - 1 + 2 * (i % 2)) % n_grp) for i in ran...  2.51 us
    ppermute x1, waiting for transfers between devices, on_device(): lax.ppermute(odd, 'grp', [(i, (i - 1 + 2 * (i % 2)) % n_grp) for i in ran...  2.06 us
    ppermute x3, waiting for transfers between devices, on_device(): lax.ppermute(probe_low, 'grp', [(i, i ^ k) for i in range(n_grp)])  1.61 us
    ppermute x1, waiting for transfers between devices, on_device(): even = lax.ppermute(even, 'grp', [(i, i ^ 1) for i in range(n_grp)])  1.32 us
  transfers between devices with their start and end apart: 5, of which 5 were waited for; matrix products, arithmetic and copies ran while one was open for 0% of the time, Pallas kernels for 2%

profile of v14, /device:TPU:0, one launch (start us, length us, event | category | flops | bytes accessed | tf_op | source)
XLA Modules:
  0.0 41.0 jit_solution(11974499349467553292)
XLA Ops:
  0.6 1.1 %pack_tiles.1 = (bf16[8,48,128]{2,1,0:T(8,128)(2,1)S(1)}, f32[4,64,128]{2,1,0:T(8,128)S(1)}) custom-call(f32[2,64,128]{2,1,0:T(8,128)} %bv_hbm.1, f32[64,128]{1,0:T(8,128)} %refs_1_.1, f32[64,128]{1,0:T(8,128)} %refs_2_.1, f32[64,128]{1,0:T(8,128)} %refs_3_.1, f32[1,1,2,512]{3,2,1,0:T(2,128)} %refs_4_.1, f32[1,1,1,512]{3,2,1,0:T(1,128)} %refs_5_.1, ...), custom_call_target="tpu_custom_call" | custom-call | tf_op jit(solution)/shard_map/pack_tiles/pallas_call | solution.py:469
  1.8 12.5 %all_to_all.10.got_ref = bf16[8,48,128]{2,1,0:T(8,128)(2,1)S(1)} all-to-all(bf16[8,48,128]{2,1,0:T(8,128)(2,1)S(1)} %get-tuple-element.16), channel_id=1, replica_groups=mesh['grp'=4,'tile'=8] {'tile'}, dimensions={0} | all-to-all | bytes 196608 | tf_op jit(solution)/shard_map/all_to_all | solution.py:481
  14.2 0.2 pack_rows.1
  14.4 2.5 %collective-permute-start = (bf16[128,128]{1,0:T(8,128)(2,1)S(1)}, bf16[128,128]{1,0:T(8,128)(2,1)S(1)}, u32[]{:S(2)}, u32[]{:S(2)}) collective-permute-start(bf16[128,128]{1,0:T(8,128)(2,1)S(1)} %get-tuple-element.19), channel_id=1, source_target_pairs={{0,24},{8,16},{16,8},{24,0},{1,25},{9,17},{17,9},{25,1},{2,26},{10... | collective-permute-start | bytes 98312 | tf_op jit(solution)/shard_map/ppermute | solution.py:498
  16.9 0.5 %collective-permute-start.1 = (bf16[128,128]{1,0:T(8,128)(2,1)S(1)}, bf16[128,128]{1,0:T(8,128)(2,1)S(1)}, u32[]{:S(2)}, u32[]{:S(2)}) collective-permute-start(bf16[128,128]{1,0:T(8,128)(2,1)S(1)} %get-tuple-element.20), channel_id=1, source_target_pairs={{0,8},{8,0},{16,24},{24,16},{1,9},{9,1},{17,25},{25,17},{2,10},{10... | collective-permute-start | bytes 98312 | tf_op jit(solution)/shard_map/ppermute | solution.py:497
  17.5 2.1 %collective-permute-done.odd_ref = bf16[128,128]{1,0:T(8,128)(2,1)S(1)} collective-permute-done((bf16[128,128]{1,0:T(8,128)(2,1)S(1)}, bf16[128,128]{1,0:T(8,128)(2,1)S(1)}, u32[]{:S(2)}, u32[]{:S(2)}) %collective-permute-start) | collective-permute-done | bytes 32800 | tf_op jit(solution)/shard_map/ppermute | solution.py:498
  19.5 1.3 %collective-permute-done.1.even_ref = bf16[128,128]{1,0:T(8,128)(2,1)S(1)} collective-permute-done((bf16[128,128]{1,0:T(8,128)(2,1)S(1)}, bf16[128,128]{1,0:T(8,128)(2,1)S(1)}, u32[]{:S(2)}, u32[]{:S(2)}) %collective-permute-start.1) | collective-permute-done | bytes 32800 | tf_op jit(solution)/shard_map/ppermute | solution.py:497
  20.8 4.0 %solve.1 = (f32[2,64,128]{2,1,0:T(8,128)}, f32[64,128]{1,0:T(8,128)S(1)}, bf16[64,128]{1,0:T(8,128)(2,1)S(1)}, bf16[32,4,64,128]{3,2,1,0:T(8,128)(2,1)S(1)}) custom-call(f32[4,64,256]{2,1,0:T(8,128)S(1)} %get-tuple-element.17.ext_ref, f32[48,128]{1,0:T(8,128)S(1)} %get-tuple-element.18.pix_ref, bf16[128,128]{1,0:T(8,128)(2,1)S(1)} %collective-permute-done.odd_ref, ...), custom_call_target="tpu_custom_call" | custom-call | tf_op jit(solution)/shard_map/solve/pallas_call | solution.py:500
  24.8 1.0 %collective-permute-start.3 = (bf16[64,128]{1,0:T(8,128)(2,1)S(1)}, bf16[64,128]{1,0:T(8,128)(2,1)S(1)}, u32[]{:S(2)}, u32[]{:S(2)}) collective-permute-start(bf16[64,128]{1,0:T(8,128)(2,1)S(1)} %get-tuple-element.24.refs_0_), channel_id=1, source_target_pairs={{0,24},{8,16},{16,8},{24,0},{1,25},{9,17},{17,9},{25,1},{2,26},{10... | collective-permute-start | bytes 49160 | tf_op jit(solution)/shard_map/ppermute | solution.py:526
  25.8 1.1 %collective-permute-start.2 = (bf16[64,128]{1,0:T(8,128)(2,1)S(1)}, bf16[64,128]{1,0:T(8,128)(2,1)S(1)}, u32[]{:S(2)}, u32[]{:S(2)}) collective-permute-start(bf16[64,128]{1,0:T(8,128)(2,1)S(1)} %get-tuple-element.24.refs_0_), channel_id=1, source_target_pairs={{0,16},{8,24},{16,0},{24,8},{1,17},{9,25},{17,1},{25,9},{2,18},{10... | collective-permute-start | bytes 49160 | tf_op jit(solution)/shard_map/ppermute | solution.py:526
  26.9 1.5 %collective-permute-start.4 = (bf16[64,128]{1,0:T(8,128)(2,1)S(1)}, bf16[64,128]{1,0:T(8,128)(2,1)S(1)}, u32[]{:S(2)}, u32[]{:S(2)}) collective-permute-start(bf16[64,128]{1,0:T(8,128)(2,1)S(1)} %get-tuple-element.24.refs_0_), channel_id=1, source_target_pairs={{0,8},{8,0},{16,24},{24,16},{1,9},{9,1},{17,25},{25,17},{2,10},{10... | collective-permute-start | bytes 49160 | tf_op jit(solution)/shard_map/ppermute | solution.py:526
  28.4 1.2 %collective-permute-done.3.refs_2_ = bf16[64,128]{1,0:T(8,128)(2,1)S(1)} collective-permute-done((bf16[64,128]{1,0:T(8,128)(2,1)S(1)}, bf16[64,128]{1,0:T(8,128)(2,1)S(1)}, u32[]{:S(2)}, u32[]{:S(2)}) %collective-permute-start.3) | collective-permute-done | bytes 16416 | tf_op jit(solution)/shard_map/ppermute | solution.py:526
  29.6 0.2 collective-permute-done.2.refs_1_
  29.7 0.6 %project.1 = (f32[32,8,128]{2,1,0:T(8,128)S(1)}, f32[64,128]{1,0:T(8,128)}) custom-call(bf16[32,4,64,128]{3,2,1,0:T(8,128)(2,1)S(1)} %get-tuple-element.22.panels_ref, f32[64,128]{1,0:T(8,128)S(1)} %get-tuple-element.23.hess_ref, bf16[64,128]{1,0:T(8,128)(2,1)S(1)} %get-tuple-element.24.refs_0_, bf16[64,128]{1,0:T(8,128)(2,1)S(1)} %collective-permute-done.2.refs_1_, ...), custom_call_target="tpu_custom_call" | custom-call | flops 1572864 | bytes 2097152 | tf_op jit(solution)/shard_map/project/pallas_call | solution.py:528
  30.3 0.3 collective-permute-done.4.block_ref
  30.6 0.3 project_last.1
  31.0 9.5 %all_to_all.11.lines_ref = f32[32,1,128]{2,1,0:T(1,128)S(1)} all-to-all(f32[32,1,128]{2,1,0:T(1,128)S(1)} %project_last.1), channel_id=1, replica_groups=mesh['grp'=4,'tile'=8] {'grp','tile'}, dimensions={0} | all-to-all | bytes 32768 | tf_op jit(solution)/shard_map/all_to_all | solution.py:551
  40.5 0.5 %add_lines.1 = f32[1,128]{1,0:T(1,128)} custom-call(f32[32,1,128]{2,1,0:T(1,128)S(1)} %all_to_all.11.lines_ref), custom_call_target="tpu_custom_call" | custom-call | tf_op jit(solution)/shard_map/add_lines/pallas_call | solution.py:552
Async XLA Ops:
  14.4 5.1 %collective-permute-start = (bf16[128,128]{1,0:T(8,128)(2,1)S(1)}, bf16[128,128]{1,0:T(8,128)(2,1)S(1)}, u32[]{:S(2)}, u32[]{:S(2)}) collective-permute-start(bf16[128,128]{1,0:T(8,128)(2,1)S(1)} %get-tuple-element.19), channel_id=1, source_target_pairs={{0,24},{8,16},{16,8},{24,0},{1,25},{9,17},{17,9},{25,1},{2,26},{10... | collective-permute-start | bytes 98312 | tf_op jit(solution)/shard_map/ppermute | solution.py:498
  16.9 3.9 %collective-permute-start.1 = (bf16[128,128]{1,0:T(8,128)(2,1)S(1)}, bf16[128,128]{1,0:T(8,128)(2,1)S(1)}, u32[]{:S(2)}, u32[]{:S(2)}) collective-permute-start(bf16[128,128]{1,0:T(8,128)(2,1)S(1)} %get-tuple-element.20), channel_id=1, source_target_pairs={{0,8},{8,0},{16,24},{24,16},{1,9},{9,1},{17,25},{25,17},{2,10},{10... | collective-permute-start | bytes 98312 | tf_op jit(solution)/shard_map/ppermute | solution.py:497
  24.8 4.7 %collective-permute-start.3 = (bf16[64,128]{1,0:T(8,128)(2,1)S(1)}, bf16[64,128]{1,0:T(8,128)(2,1)S(1)}, u32[]{:S(2)}, u32[]{:S(2)}) collective-permute-start(bf16[64,128]{1,0:T(8,128)(2,1)S(1)} %get-tuple-element.24.refs_0_), channel_id=1, source_target_pairs={{0,24},{8,16},{16,8},{24,0},{1,25},{9,17},{17,9},{25,1},{2,26},{10... | collective-permute-start | bytes 49160 | tf_op jit(solution)/shard_map/ppermute | solution.py:526
  25.8 3.9 %collective-permute-start.2 = (bf16[64,128]{1,0:T(8,128)(2,1)S(1)}, bf16[64,128]{1,0:T(8,128)(2,1)S(1)}, u32[]{:S(2)}, u32[]{:S(2)}) collective-permute-start(bf16[64,128]{1,0:T(8,128)(2,1)S(1)} %get-tuple-element.24.refs_0_), channel_id=1, source_target_pairs={{0,16},{8,24},{16,0},{24,8},{1,17},{9,25},{17,1},{25,9},{2,18},{10... | collective-permute-start | bytes 49160 | tf_op jit(solution)/shard_map/ppermute | solution.py:526
  26.9 3.7 %collective-permute-start.4 = (bf16[64,128]{1,0:T(8,128)(2,1)S(1)}, bf16[64,128]{1,0:T(8,128)(2,1)S(1)}, u32[]{:S(2)}, u32[]{:S(2)}) collective-permute-start(bf16[64,128]{1,0:T(8,128)(2,1)S(1)} %get-tuple-element.24.refs_0_), channel_id=1, source_target_pairs={{0,8},{8,0},{16,24},{24,16},{1,9},{9,1},{17,25},{25,17},{2,10},{10... | collective-permute-start | bytes 49160 | tf_op jit(solution)/shard_map/ppermute | solution.py:526
